TPU v7x, 32 devices: a whole 2x2x4 slice. The times are simulated.
32 devices in a mesh: node: 8 (over z, y), col: 4 (over x, core).
Axes of the slice: x: 2, y: 2, z: 4, core: 2. Of those that a mesh axis runs over, the one named last changes fastest.
Arguments:
- panel: bfloat16 [38912, 256], P('node', 'col'), may hold values from -6 to 6
- basis: bfloat16 [38912, 2048], P('node', 'col'), may hold values from -0.0390625 to 0.0390625
- g_blocks: bfloat16 [304, 3, 128, 128], P('node'), may hold values from -0.3125 to 0.3125
- c_blocks: bfloat16 [304, 3, 128, 128], P('node'), may hold values from -0.3125 to 0.3125
- block_cols: int32 [304, 3], P('node'), may hold values from 0 to 303, as said below
Outputs:
- reduced_g: float32 [2048, 256], P(('col', 'node'))
- reduced_c: float32 [2048, 256], P(('col', 'node'))
Inputs may be any that keep to these rules, and one draw needn't show every extreme that they name: `block_cols`: block row i names block columns within 4 of i: the first is i itself, and one lies exactly 4 away wherever that stays inside the grid.
All inputs are finite; a program needn't handle non-finite values.
Results may differ from a plain program's by a relative error of at most 0.0029.
Values may be sent and summed in bfloat16 or wider, within the bound.
No kernel may reach another device: no remote copies, remote signals or barrier semaphores. Data moves between devices by JAX's collectives and lax.ppermute only.
A program may use at most 64 MiB of HBM per device.

v0:
```python
import jax
import jax.numpy as jnp
from jax import lax
from jax.sharding import PartitionSpec as P

BS = 128
HB = 4


def with_halo(block, sides, width):
    for axis, dim in sides:
        count = lax.axis_size(axis)
        forward = [(i, i + 1) for i in range(count - 1)]
        backward = [(target, source) for source, target in forward]
        low = lax.ppermute(
            lax.slice_in_dim(block, block.shape[dim] - width, None, axis=dim), axis, forward
        )
        high = lax.ppermute(lax.slice_in_dim(block, 0, width, axis=dim), axis, backward)
        block = jnp.concatenate([low, block, high], axis=dim)
    return block


def spread_product(extended, blocks_g, blocks_c, local_ids):
    rows_dev = blocks_g.shape[0]
    block_size = blocks_g.shape[2]
    columns = extended.shape[1]
    block_tiles = extended.reshape(-1, block_size, columns)
    nearby = block_tiles[local_ids]
    prod_g = jnp.einsum("rsab,rsbk->rak", blocks_g, nearby, preferred_element_type=jnp.float32)
    prod_c = jnp.einsum("rsab,rsbk->rak", blocks_c, nearby, preferred_element_type=jnp.float32)
    stacked = jnp.stack([prod_g, prod_c], 2).astype(jnp.bfloat16)
    return stacked.reshape(rows_dev * block_size, 2, columns)


def body(panel, basis, g_blocks, c_blocks, block_cols):
    blocks_dev = block_cols.shape[0]
    offset = lax.axis_index("node") * blocks_dev - HB
    local_ids = block_cols - offset
    extended = with_halo(panel, (("node", 0),), HB * BS)
    stacked = lax.all_gather(
        spread_product(extended, g_blocks, c_blocks, local_ids), "col", axis=2, tiled=True
    )
    combined = stacked.reshape(stacked.shape[0], -1)
    reduced = lax.psum_scatter(
        lax.dot_general(
            basis, combined, (((0,), (0,)), ((), ())), preferred_element_type=jnp.float32
        ),
        "node",
        scatter_dimension=0,
        tiled=True,
    )
    half_cols = combined.shape[1] // 2
    return (reduced[:, :half_cols], reduced[:, half_cols:])


def solution(mesh):
    in_specs = (
        P("node", "col"),
        P("node", "col"),
        P("node", None, None, None),
        P("node", None, None, None),
        P("node", None),
    )
    out_specs = (P(("col", "node"), None), P(("col", "node"), None))
    return jax.shard_map(body, mesh=mesh, in_specs=in_specs, out_specs=out_specs, check_vma=False)
```

profile of v0, /device:TPU:0, one launch (start us, length us, event | category | flops | bytes accessed | tf_op | source)
XLA Modules:
  0.0 149.6 jit_solution(1145882568582058674)
XLA Ops:
  7.2 0.0 all-gather.2.cloned.1.call-start
  7.2 0.9 fusion.4
  8.1 4.9 %collective-permute-start = (bf16[512,64]{0,1:T(8,128)(2,1)S(1)}, bf16[512,64]{0,1:T(8,128)(2,1)S(1)}, u32[]{:S(2)}, u32[]{:S(2)}) collective-permute-start(bf16[512,64]{0,1:T(8,128)(2,1)S(1)} %get-tuple-element.8), channel_id=1, source_target_pairs={{0,4},{4,8},{8,12},{12,16},{16,20},{20,24},{24,28},{1,5},{5,9},{9,... | collective-permute-start | bytes 196616 | tf_op jit(solution)/shard_map/ppermute | solution.py:15
  13.0 1.3 collective-permute-start.1
  14.3 0.7 compare_select_fusion
  15.0 0.1 copy.17
  15.1 0.1 reshape.21
  15.2 3.9 %collective-permute-done.1 = bf16[512,64]{0,1:T(8,128)(2,1)S(1)} collective-permute-done((bf16[512,64]{0,1:T(8,128)(2,1)S(1)}, bf16[512,64]{0,1:T(8,128)(2,1)S(1)}, u32[]{:S(2)}, u32[]{:S(2)}) %collective-permute-start.1) | collective-permute-done | bytes 65568 | tf_op jit(solution)/shard_map/ppermute | solution.py:18
  19.1 1.3 copy_bitcast_fusion
  20.4 0.9 gather_fusion
  21.4 4.0 %fusion.3 = bf16[38,128,64]{1,2,0:T(8,128)(2,1)S(1)} fusion(bf16[38,3,128,64]{2,3,1,0:T(8,128)(2,1)S(1)} %bitcast.38, bf16[38,3,128,128]{3,2,1,0:T(8,128)(2,1)} %param.7), kind=kOutput, calls=%fused_computation.7 | convolution fusion | flops 239386624 | bytes 6225920 | tf_op jit(solution)/shard_map/rsab,rsbk->rak/dot_general | solution.py:29
  25.3 1.8 %fusion.2 = bf16[38,128,64]{1,2,0:T(8,128)(2,1)S(1)} fusion(bf16[38,3,128,64]{2,3,1,0:T(8,128)(2,1)S(1)} %bitcast.39, bf16[38,3,128,128]{3,2,1,0:T(8,128)(2,1)S(1)} %copy-done), kind=kOutput, calls=%fused_computation.6 | convolution fusion | flops 239386624 | bytes 6225920 | tf_op jit(solution)/shard_map/rsab,rsbk->rak/dot_general | solution.py:30
  27.1 0.4 copy.20
  27.5 0.3 stack.10
  27.9 0.4 copy.19
  28.3 0.3 stack.9
  28.6 1.2 pad_maximum_fusion
  29.8 0.0 all-gather.2.cloned.1.call-update
  29.8 0.0 reduce-scatter.4.cloned.1.call-start
  29.9 40.2 %all-gather.2.cloned.1.call-done = bf16[4864,2,256]{0,2,1:T(8,128)(2,1)} async-done(((bf16[4864,2,64]{0,2,1:T(8,128)(2,1)}), bf16[4864,2,256]{0,2,1:T(8,128)(2,1)}) %all-gather.2.cloned.1.call-update) | async-done | bytes 4980752 | tf_op jit(solution)/shard_map/all_gather | solution.py:40
  70.1 6.2 %convolution_bitcast_fusion.2 = f32[512,512]{0,1:T(8,128)S(1)} fusion(bf16[4864,512]{0,1:T(8,128)(2,1)} %bitcast.40, bf16[4864,512]{1,0:T(8,128)(2,1)} %param.6), kind=kOutput, calls=%fused_computation.3 | convolution fusion | flops 2550136832 | bytes 11010048 | tf_op jit(solution)/shard_map/dot_general | solution.py:45
  76.3 1.3 copy.25
  77.6 63.7 %reduce-scatter.4.cloned.1.call-done = f32[64,512]{1,0:T(8,128)} async-done(((f32[512,512]{1,0:T(8,128)}), f32[64,512]{1,0:T(8,128)}) %reduce-scatter.4.cloned.1.call-update) | async-done | bytes 131088
  141.3 1.5 %fusion.5 = (f32[64,256]{1,0:T(8,128)}, f32[64,256]{1,0:T(8,128)}) fusion(f32[64,512]{1,0:T(8,128)} %reduce-scatter.4.cloned.1.call-done), kind=kLoop, calls=%fused_computation.14 | loop fusion | bytes 262144 | tf_op jit(solution)/shard_map/slice | solution.py:53
  (5 shorter events, 0.0 us)
Async XLA Ops:
  7.2 62.9 %all-gather.2.cloned.1.call-start = ((), (), s32[]{:S(2)}) async-start(), calls=%async_computation.1 | async-start | bytes 6225920 | tf_op jit(solution)/shard_map/all_gather | solution.py:40
  8.1 7.1 %collective-permute-start = (bf16[512,64]{0,1:T(8,128)(2,1)S(1)}, bf16[512,64]{0,1:T(8,128)(2,1)S(1)}, u32[]{:S(2)}, u32[]{:S(2)}) collective-permute-start(bf16[512,64]{0,1:T(8,128)(2,1)S(1)} %get-tuple-element.8), channel_id=1, source_target_pairs={{0,4},{4,8},{8,12},{12,16},{16,20},{20,24},{24,28},{1,5},{5,9},{9,... | collective-permute-start | bytes 196616 | tf_op jit(solution)/shard_map/ppermute | solution.py:15
  13.0 6.2 %collective-permute-start.1 = (bf16[512,64]{0,1:T(8,128)(2,1)S(1)}, bf16[512,64]{0,1:T(8,128)(2,1)S(1)}, u32[]{:S(2)}, u32[]{:S(2)}) collective-permute-start(bf16[512,64]{0,1:T(8,128)(2,1)S(1)} %get-tuple-element.9), channel_id=1, source_target_pairs={{4,0},{8,4},{12,8},{16,12},{20,16},{24,20},{28,24},{5,1},{9,5},{13... | collective-permute-start | bytes 196616 | tf_op jit(solution)/shard_map/ppermute | solution.py:18
  21.3 4.0 %copy-start = (bf16[38,3,128,128]{3,2,1,0:T(8,128)(2,1)S(1)}, bf16[38,3,128,128]{3,2,1,0:T(8,128)(2,1)}, u32[]{:S(2)}) copy-start(bf16[38,3,128,128]{3,2,1,0:T(8,128)(2,1)} %param.8) | copy-start | bytes 11206660
  29.8 111.4 %reduce-scatter.4.cloned.1.call-start = ((), (), s32[]{:S(2)}) async-start(), calls=%async_computation.2 | async-start | bytes 1179648
Sparse Core Ops, SparseCore 0:
  30.0 40.0 all-gather.1
  77.7 63.4 reduce-scatter.3
where the time goes:
time: 150 us
  waiting for transfers between devices  108 us (72%)
  between operations  14.2 us (9%)
  matrix products  11.9 us (8%)
  local copies, waits for them, and re-layouts  6.36 us (4%)
  starting transfers between devices  6.25 us (4%)
  other arithmetic  3.15 us (2%)
    unnamed x3, waiting for transfers between devices  63.7 us
    all_gather x1, waiting for transfers between devices, body(): lax.all_gather(spread_product(extended, g_blocks, c_blocks, local_ids), '...  40.2 us
    dot_general x1, matrix products, body(): lax.dot_general(basis, combined, (((0,), (0,)), ((), ())), preferred_elem...  6.18 us
    ppermute x1, starting transfers between devices, with_halo(): lax.ppermute(lax.slice_in_dim(block, block.shape[dim] - width, None, axis...  4.87 us
    dot_general x1, matrix products, spread_product(): jnp.einsum('rsab,rsbk->rak', blocks_g, nearby, preferred_element_type=jnp...  3.97 us
    ppermute x1, waiting for transfers between devices, with_halo(): lax.ppermute(lax.slice_in_dim(block, 0, width, axis=dim), axis, backward)  3.92 us
  transfers between devices with their start and end apart: 4, of which 3 were waited for; matrix products, arithmetic and copies ran while one was open for 1% of the time, Pallas kernels for 0%

commit v1 on v0

v1 whole, which is shorter than its diff:
```python
import functools

import jax
import jax.numpy as jnp
from jax import lax
from jax.experimental import pallas as pl
from jax.experimental.pallas import tpu as pltpu
from jax.sharding import PartitionSpec as P

BS = 128
HB = 4
F32 = jnp.float32
BF16 = jnp.bfloat16


def cuts(total, parts):
    edges = [total * i // parts for i in range(parts + 1)]
    return list(zip(edges[:-1], edges[1:]))


def project_kernel(groups, ids_ref, mine, other, low_m, high_m, low_o, high_o, g_hbm, c_hbm, basis_hbm,
                   send_ref, keep_ref, ext, g_buf, c_buf, b_buf, yt, acc, sems):
    rows = g_hbm.shape[0]
    slots = g_hbm.shape[1]
    width = mine.shape[0]
    inner = mine.shape[1]
    halo = HB * BS
    node = lax.axis_index("node")
    core = lax.axis_index("col") % 2
    spans = cuts(rows, 4)

    copies = []
    for step, (lo, hi) in enumerate(spans):
        span = pl.ds(lo, hi - lo)
        nodes = pl.ds(lo * BS, (hi - lo) * BS)
        batch = [
            pltpu.make_async_copy(g_hbm.at[span], g_buf.at[span], sems.at[step, 0]),
            pltpu.make_async_copy(c_hbm.at[span], c_buf.at[span], sems.at[step, 1]),
            pltpu.make_async_copy(basis_hbm.at[nodes], b_buf.at[nodes], sems.at[step, 2]),
        ]
        for copy in batch:
            copy.start()
        copies.append(batch)

    for place, low, middle, high in ((core, low_m, mine, high_m), (1 - core, low_o, other, high_o)):
        at = pl.ds(pl.multiple_of(place * width, width), width)
        ext[at, 0:halo] = low[...]
        ext[at, halo:halo + inner] = middle[...]
        ext[at, halo + inner:] = high[...]

    offset = node * rows - HB
    for step, (lo, hi) in enumerate(spans):
        for copy in copies[step]:
            copy.wait()
        for row in range(lo, hi):
            near = []
            for slot in range(slots):
                local = jnp.clip(ids_ref[slot, row] - offset, 0, rows + 2 * HB - 1)
                near.append(ext[:, pl.ds(pl.multiple_of(local * BS, BS), BS)])
            near = jnp.concatenate(near, axis=1)
            both = jnp.concatenate(
                [
                    jnp.concatenate([g_buf[row, slot] for slot in range(slots)], axis=1),
                    jnp.concatenate([c_buf[row, slot] for slot in range(slots)], axis=1),
                ],
                axis=0,
            )
            prod = lax.dot_general(near, both, (((1,), (1,)), ((), ())), preferred_element_type=F32)
            prod = prod.astype(BF16)
            yt[0:2 * width, row * BS:(row + 1) * BS] = prod[:, 0:BS]
            yt[2 * width:4 * width, row * BS:(row + 1) * BS] = prod[:, BS:2 * BS]
        part = jnp.dot(yt[:, lo * BS:hi * BS], b_buf[lo * BS:hi * BS, :], preferred_element_type=F32)
        if step == 0:
            acc[...] = part
        else:
            acc[...] += part
    total = acc[...].T
    states, columns = total.shape
    total = total.reshape(groups, 2, states // (2 * groups), columns)
    odd = node % 2 == 1
    keep_ref[...] = jnp.where(odd, total[:, 1], total[:, 0])
    send_ref[...] = jnp.where(odd, total[:, 0], total[:, 1]).astype(BF16)


def project(ids, mine, other, halos_m, halos_o, g_blocks, c_blocks, basis, groups):
    rows, slots = g_blocks.shape[0], g_blocks.shape[1]
    width, inner = mine.shape
    states = basis.shape[1]
    piece = (groups, states // (2 * groups), 4 * width)
    vmem = pl.BlockSpec(memory_space=pltpu.VMEM)
    hbm = pl.BlockSpec(memory_space=pl.ANY)
    flops = 2 * rows * BS * 4 * width * (slots * BS + states)
    return pl.pallas_call(
        functools.partial(project_kernel, groups),
        out_shape=(jax.ShapeDtypeStruct(piece, BF16), jax.ShapeDtypeStruct(piece, F32)),
        in_specs=[pl.BlockSpec(memory_space=pltpu.SMEM)] + [vmem] * 6 + [hbm] * 3,
        out_specs=(vmem, vmem),
        scratch_shapes=[
            pltpu.VMEM((2 * width, inner + 2 * HB * BS), BF16),
            pltpu.VMEM(g_blocks.shape, BF16),
            pltpu.VMEM(c_blocks.shape, BF16),
            pltpu.VMEM(basis.shape, BF16),
            pltpu.VMEM((4 * width, inner), BF16),
            pltpu.VMEM((4 * width, states), F32),
            pltpu.SemaphoreType.DMA((4, 3)),
        ],
        compiler_params=pltpu.CompilerParams(vmem_limit_bytes=40 * 1024 * 1024),
        cost_estimate=pl.CostEstimate(flops=flops, bytes_accessed=14_000_000, transcendentals=0),
    )(ids, mine, other, *halos_m, *halos_o, g_blocks, c_blocks, basis)


def spread_kernel(groups, keep_a, got_a, keep_b, got_b, keep_ref, *send_refs):
    here = lax.axis_index("node") // 2
    half = keep_a.shape[2]
    for step in range(groups):
        at = here ^ step
        for lo, keep, got in ((0, keep_a, got_a), (half, keep_b, got_b)):
            value = keep[at] + got[at].astype(F32)
            if step == 0:
                keep_ref[:, lo:lo + half] = value
            else:
                send_refs[step - 1][:, lo:lo + half] = value.astype(BF16)


def spread(groups, keep_a, got_a, keep_b, got_b):
    piece = (keep_a.shape[1], 2 * keep_a.shape[2])
    vmem = pl.BlockSpec(memory_space=pltpu.VMEM)
    return pl.pallas_call(
        functools.partial(spread_kernel, groups),
        out_shape=[jax.ShapeDtypeStruct(piece, F32)] + [jax.ShapeDtypeStruct(piece, BF16)] * (groups - 1),
        in_specs=[vmem] * 4,
        out_specs=[vmem] * groups,
    )(keep_a, got_a, keep_b, got_b)


def finish_kernel(keep, *refs):
    got, (out_g, out_c) = refs[:-2], refs[-2:]
    total = keep[...]
    for ref in got:
        total = total + ref[...].astype(F32)
    first = lax.axis_index("col") // 2
    quarter = total.shape[1] // 4
    for place, base in ((first, 0), (1 - first, 2 * quarter)):
        at = pl.ds(pl.multiple_of(place * quarter, quarter), quarter)
        out_g[:, at] = total[:, base:base + quarter]
        out_c[:, at] = total[:, base + quarter:base + 2 * quarter]


def finish(keep, got):
    piece = jax.ShapeDtypeStruct((keep.shape[0], keep.shape[1] // 2), F32)
    vmem = pl.BlockSpec(memory_space=pltpu.VMEM)
    return pl.pallas_call(
        finish_kernel,
        out_shape=(piece, piece),
        in_specs=[vmem] * (1 + len(got)),
        out_specs=(vmem, vmem),
    )(keep, *got)


def body(panel, basis, g_blocks, c_blocks, block_cols):
    nodes, cols = lax.axis_size("node"), lax.axis_size("col")
    groups = nodes // 2
    halo = HB * BS
    ids = block_cols.T
    mine = panel.T
    across = [(i, i ^ 2) for i in range(cols)]
    cores = [(i, i ^ 1) for i in range(cols)]
    up = [(i, i + 1) for i in range(nodes - 1)]
    down = [(i + 1, i) for i in range(nodes - 1)]
    pairs = [(i, i ^ 1) for i in range(nodes)]

    far = lax.ppermute(mine, "col", across)
    other = lax.ppermute(mine, "col", cores)
    low = lax.ppermute(mine[:, -halo:], "node", up)
    high = lax.ppermute(mine[:, :halo], "node", down)
    halos = jnp.concatenate([low, high], axis=1)
    far_halos = lax.ppermute(halos, "col", across)
    other_halos = lax.ppermute(halos, "col", cores)

    def sides(both):
        return both[:, :halo], both[:, halo:]

    send_a, keep_a = project(ids, mine, other, (low, high), sides(other_halos), g_blocks, c_blocks, basis, groups)
    got_a = lax.ppermute(send_a, "node", pairs)
    far_other = lax.ppermute(far, "col", cores)
    far_other_halos = lax.ppermute(far_halos, "col", cores)
    send_b, keep_b = project(
        ids, far, far_other, sides(far_halos), sides(far_other_halos), g_blocks, c_blocks, basis, groups
    )
    got_b = lax.ppermute(send_b, "node", pairs)
    keep, *sends = spread(groups, keep_a, got_a, keep_b, got_b)
    got = []
    for step, send in enumerate(sends, 1):
        got.append(lax.ppermute(send, "node", [(i, i ^ (2 * step)) for i in range(nodes)]))
    return finish(keep, got)


def solution(mesh):
    in_specs = (
        P("node", "col"),
        P("node", "col"),
        P("node", None, None, None),
        P("node", None, None, None),
        P("node", None),
    )
    out_specs = (P(("col", "node"), None), P(("col", "node"), None))
    return jax.shard_map(body, mesh=mesh, in_specs=in_specs, out_specs=out_specs, check_vma=False)
```

time: 150 us -> 72.5 us (0.48)
  waiting for transfers between devices: 108 us -> 25.1 us
  Pallas kernels: 0 us -> 18.7 us
  between operations: 14.2 us -> 0.76 us
  matrix products: 11.9 us -> 0 us
  starting transfers between devices: 6.25 us -> 15.7 us
  local copies, waits for them, and re-layouts: 6.36 us -> 11.9 us
  other arithmetic: 3.15 us -> 0 us
    unnamed x3 -> x0, waiting for transfers between devices: 63.7 us -> none
    all_gather x1 -> x0, waiting for transfers between devices: 40.2 us -> none  [body(): lax.all_gather(spread_product(extended, g_blocks, c_blocks, local_ids), '...]
    ppermute x2 -> x13, waiting for transfers between devices: 3.93 us -> 25.1 us  [the longest x1 9.82 us: body(): far_halos = lax.ppermute(halos, 'col', across)]
    pallas_call x0 -> x4, Pallas kernels: none -> 18.7 us  [the longest x2 15.2 us: project(): pl.pallas_call(functools.partial(project_kernel, groups), out_shape=(jax....]
    dot_general x3 -> x0, matrix products: 11.9 us -> none  [the longest x1 6.18 us: body(): lax.dot_general(basis, combined, (((0,), (0,)), ((), ())), preferred_elem...]
    unnamed x3 -> x29, local copies, waits for them, and re-layouts: 1.31 us -> 10.9 us
    ppermute x2 -> x13, starting transfers between devices: 6.17 us -> 15.7 us  [the longest x1 4.87 us: body(): low = lax.ppermute(mine[:, -halo:], 'node', up)]
    slice x2 -> x4, local copies, waits for them, and re-layouts: 2.41 us -> 0.91 us  [the longest x1 0.88 us: body(): high = lax.ppermute(mine[:, :halo], 'node', down)]
  transfers between devices with their start and end apart: 4 -> 13, of which waited for: 3 -> 7; matrix products, arithmetic and copies ran while one was open for 1% -> 0% of each run, Pallas kernels for 0% -> 21%
where the time goes in v1:
time: 72.5 us; the launch traced here: 72.1 us
  waiting for transfers between devices  25.1 us (35%)
  Pallas kernels  18.7 us (26%)
  starting transfers between devices  15.7 us (22%)
  local copies, waits for them, and re-layouts  11.9 us (16%)
  between operations  0.76 us (1%)
    pallas_call x2, Pallas kernels, project(): pl.pallas_call(functools.partial(project_kernel, groups), out_shape=(jax....  15.2 us
    unnamed x29, local copies, waits for them, and re-layouts  10.9 us
    ppermute x1, waiting for transfers between devices, body(): far_halos = lax.ppermute(halos, 'col', across)  9.82 us
    ppermute x3, waiting for transfers between devices, body(): lax.ppermute(send, 'node', [(i, i ^ 2 * step) for i in range(nodes)])  4.9 us
    ppermute x1, starting transfers between devices, body(): low = lax.ppermute(mine[:, -halo:], 'node', up)  4.87 us
    ppermute x1, waiting for transfers between devices, body(): high = lax.ppermute(mine[:, :halo], 'node', down)  4.83 us
    ppermute x1, waiting for transfers between devices, body(): got_b = lax.ppermute(send_b, 'node', pairs)  4.78 us
    ppermute x3, starting transfers between devices, body(): lax.ppermute(send, 'node', [(i, i ^ 2 * step) for i in range(nodes)])  4.39 us
  transfers between devices with their start and end apart: 13, of which 7 were waited for; matrix products, arithmetic and copies ran while one was open for 0% of the time, Pallas kernels for 21%

profile of v1, /device:TPU:0, one launch (start us, length us, event | category | flops | bytes accessed | tf_op | source)
XLA Modules:
  0.0 72.1 jit_solution(7744692907724820532)
XLA Ops:
  0.6 0.9 %fusion = (bf16[64,512]{1,0:T(8,128)(2,1)S(1)}, bf16[64,512]{1,0:T(8,128)(2,1)S(1)}) fusion(bf16[64,4864]{1,0:T(8,128)(2,1)} %bitcast.2), kind=kLoop, calls=%fused_computation.2 | loop fusion | bytes 262144 | tf_op jit(solution)/shard_map/slice | solution.py:175
  1.5 4.9 %collective-permute-start.1 = (bf16[64,512]{1,0:T(8,128)(2,1)S(1)}, bf16[64,512]{1,0:T(8,128)(2,1)S(1)}, u32[]{:S(2)}, u32[]{:S(2)}) collective-permute-start(bf16[64,512]{1,0:T(8,128)(2,1)S(1)} %get-tuple-element.19), channel_id=1, source_target_pairs={{0,4},{4,8},{8,12},{12,16},{16,20},{20,24},{24,28},{1,5},{5,9},{9,... | collective-permute-start | bytes 196616 | tf_op jit(solution)/shard_map/ppermute | solution.py:174
  6.4 1.6 %collective-permute-start.5 = (bf16[64,4864]{1,0:T(8,128)(2,1)}, bf16[64,4864]{1,0:T(8,128)(2,1)S(1)}, u32[]{:S(2)}, u32[]{:S(2)}) collective-permute-start(bf16[64,4864]{1,0:T(8,128)(2,1)} %bitcast.3), channel_id=1, source_target_pairs={{0,2},{1,3},{2,0},{3,1},{4,6},{5,7},{6,4},{7,5},{8,10},{9,11},{10,... | collective-permute-start | bytes 1867784 | tf_op jit(solution)/shard_map/ppermute | solution.py:172
  8.0 1.3 %collective-permute-start.2 = (bf16[64,512]{1,0:T(8,128)(2,1)S(1)}, bf16[64,512]{1,0:T(8,128)(2,1)S(1)}, u32[]{:S(2)}, u32[]{:S(2)}) collective-permute-start(bf16[64,512]{1,0:T(8,128)(2,1)S(1)} %get-tuple-element.18), channel_id=1, source_target_pairs={{4,0},{8,4},{12,8},{16,12},{20,16},{24,20},{28,24},{5,1},{9,5},{13... | collective-permute-start | bytes 196616 | tf_op jit(solution)/shard_map/ppermute | solution.py:175
  9.3 4.8 %collective-permute-done.2.high_m = bf16[64,512]{1,0:T(8,128)(2,1)S(1)} collective-permute-done((bf16[64,512]{1,0:T(8,128)(2,1)S(1)}, bf16[64,512]{1,0:T(8,128)(2,1)S(1)}, u32[]{:S(2)}, u32[]{:S(2)}) %collective-permute-start.2) | collective-permute-done | bytes 65568 | tf_op jit(solution)/shard_map/ppermute | solution.py:175
  15.2 9.8 %collective-permute-done.7 = bf16[64,1024]{1,0:T(8,128)(2,1)S(1)} collective-permute-done((bf16[64,1024]{1,0:T(8,128)(2,1)S(1)}, bf16[64,1024]{1,0:T(8,128)(2,1)S(1)}, u32[]{:S(2)}, u32[]{:S(2)}) %collective-permute-start.7) | collective-permute-done | bytes 131104 | tf_op jit(solution)/shard_map/ppermute | solution.py:177
  25.6 0.7 %collective-permute-done.8 = bf16[64,1024]{1,0:T(8,128)(2,1)S(1)} collective-permute-done((bf16[64,1024]{1,0:T(8,128)(2,1)S(1)}, bf16[64,1024]{1,0:T(8,128)(2,1)S(1)}, u32[]{:S(2)}, u32[]{:S(2)}) %collective-permute-start.8) | collective-permute-done | bytes 131104 | tf_op jit(solution)/shard_map/ppermute | solution.py:186
  26.4 2.4 %copy-done = bf16[4864,512]{1,0:T(8,128)(2,1)S(1)} copy-done((bf16[4864,512]{1,0:T(8,128)(2,1)S(1)}, bf16[4864,512]{1,0:T(8,128)(2,1)}, u32[]{:S(2)}) %copy-start) | copy-done | bytes 4980760
  28.8 2.1 %copy-done.2 = bf16[38,3,128,128]{3,2,1,0:T(8,128)(2,1)S(1)} copy-done((bf16[38,3,128,128]{3,2,1,0:T(8,128)(2,1)S(1)}, bf16[38,3,128,128]{3,2,1,0:T(8,128)(2,1)}, u32[]{:S(2)}) %copy-start.2) | copy-done | bytes 3735576
  30.8 2.1 %copy-done.4 = bf16[38,3,128,128]{3,2,1,0:T(8,128)(2,1)S(1)} copy-done((bf16[38,3,128,128]{3,2,1,0:T(8,128)(2,1)S(1)}, bf16[38,3,128,128]{3,2,1,0:T(8,128)(2,1)}, u32[]{:S(2)}) %copy-start.4) | copy-done | bytes 3735576
  32.9 1.1 %copy-done.5 = bf16[4864,64]{0,1:T(8,128)(2,1)S(1)} copy-done((bf16[4864,64]{0,1:T(8,128)(2,1)S(1)}, bf16[4864,64]{0,1:T(8,128)(2,1)}, u32[]{:S(2)}) %copy-start.5) | copy-done | bytes 622616
  34.6 7.6 %shard_map.68 = (bf16[4,64,256]{2,1,0:T(8,128)(2,1)S(1)}, f32[4,64,256]{2,1,0:T(8,128)S(1)}) custom-call(s32[3,38]{1,0:T(4,128)S(1)} %bitcast.6, bf16[64,4864]{1,0:T(8,128)(2,1)S(1)} %bitcast.5, bf16[64,4864]{1,0:T(8,128)(2,1)S(1)} %collective-permute-done.other, bf16[64,512]{1,0:T(8,128)(2,1)S(1)} %collective-permute-done.1.low_m, ...), custom_call_target="tpu_custom_call" | custom-call | flops 2231369728 | bytes 14000000 | tf_op jit(solution)/shard_map/pallas_call | solution.py:93
  42.9 1.5 %collective-permute-start.4 = (bf16[4,64,256]{2,1,0:T(8,128)(2,1)S(1)}, bf16[4,64,256]{2,1,0:T(8,128)(2,1)S(1)}, u32[]{:S(2)}, u32[]{:S(2)}) collective-permute-start(bf16[4,64,256]{2,1,0:T(8,128)(2,1)S(1)} %get-tuple-element.11), channel_id=1, source_target_pairs={{0,4},{4,0},{8,12},{12,8},{16,20},{20,16},{24,28},{28,24},{1,5},{5... | collective-permute-start | bytes 393224 | tf_op jit(solution)/shard_map/ppermute | solution.py:184
  44.4 7.6 %shard_map.69 = (bf16[4,64,256]{2,1,0:T(8,128)(2,1)S(1)}, f32[4,64,256]{2,1,0:T(8,128)S(1)}) custom-call(s32[3,38]{1,0:T(4,128)S(1)} %bitcast.7, bf16[64,4864]{1,0:T(8,128)(2,1)S(1)} %collective-permute-done.5.mine, bf16[64,4864]{1,0:T(8,128)(2,1)S(1)} %collective-permute-done.6.other, bf16[64,512]{1,0:T(8,128)(2,1)S(1)} %get-tuple-element.23.low_m, ...), custom_call_target="tpu_custom_call" | custom-call | flops 2231369728 | bytes 14000000 | tf_op jit(solution)/shard_map/pallas_call | solution.py:93
  52.0 0.7 copy-done.7
  53.2 4.8 %collective-permute-done.9.got_b = bf16[4,64,256]{2,1,0:T(8,128)(2,1)S(1)} collective-permute-done((bf16[4,64,256]{2,1,0:T(8,128)(2,1)S(1)}, bf16[4,64,256]{2,1,0:T(8,128)(2,1)S(1)}, u32[]{:S(2)}, u32[]{:S(2)}) %collective-permute-start.9) | collective-permute-done | bytes 131104 | tf_op jit(solution)/shard_map/ppermute | solution.py:190
  58.7 1.9 %shard_map.70 = (f32[64,512]{1,0:T(8,128)}, bf16[64,512]{1,0:T(8,128)(2,1)}, bf16[64,512]{1,0:T(8,128)(2,1)}, bf16[64,512]{1,0:T(8,128)(2,1)}) custom-call(f32[4,64,256]{2,1,0:T(8,128)} %copy-done.6, bf16[4,64,256]{2,1,0:T(8,128)(2,1)} %copy-done.9, f32[4,64,256]{2,1,0:T(8,128)} %copy-done.7, bf16[4,64,256]{2,1,0:T(8,128)(2,1)} %copy-done.10), custom_call_target="tpu_custom_call" | custom-call | tf_op jit(solution)/shard_map/pallas_call | solution.py:128
  60.5 1.6 %collective-permute-start.10 = (bf16[64,512]{1,0:T(8,128)(2,1)}, bf16[64,512]{1,0:T(8,128)(2,1)S(1)}, u32[]{:S(2)}, u32[]{:S(2)}) collective-permute-start(bf16[64,512]{1,0:T(8,128)(2,1)} %get-tuple-element.15), channel_id=1, source_target_pairs={{0,8},{4,12},{8,0},{12,4},{16,24},{20,28},{24,16},{28,20},{1,9},{5... | collective-permute-start | bytes 196616 | tf_op jit(solution)/shard_map/ppermute | solution.py:194
  62.1 1.3 %collective-permute-start.11 = (bf16[64,512]{1,0:T(8,128)(2,1)}, bf16[64,512]{1,0:T(8,128)(2,1)S(1)}, u32[]{:S(2)}, u32[]{:S(2)}) collective-permute-start(bf16[64,512]{1,0:T(8,128)(2,1)} %get-tuple-element.16), channel_id=1, source_target_pairs={{0,16},{4,20},{8,24},{12,28},{16,0},{20,4},{24,8},{28,12},{1,17},{... | collective-permute-start | bytes 196616 | tf_op jit(solution)/shard_map/ppermute | solution.py:194
  63.4 1.5 %collective-permute-start.12 = (bf16[64,512]{1,0:T(8,128)(2,1)}, bf16[64,512]{1,0:T(8,128)(2,1)S(1)}, u32[]{:S(2)}, u32[]{:S(2)}) collective-permute-start(bf16[64,512]{1,0:T(8,128)(2,1)} %get-tuple-element.17), channel_id=1, source_target_pairs={{0,24},{4,28},{8,16},{12,20},{16,8},{20,12},{24,0},{28,4},{1,25},{... | collective-permute-start | bytes 196616 | tf_op jit(solution)/shard_map/ppermute | solution.py:194
  64.9 0.7 %collective-permute-done.10.refs_0_ = bf16[64,512]{1,0:T(8,128)(2,1)S(1)} collective-permute-done((bf16[64,512]{1,0:T(8,128)(2,1)}, bf16[64,512]{1,0:T(8,128)(2,1)S(1)}, u32[]{:S(2)}, u32[]{:S(2)}) %collective-permute-start.10) | collective-permute-done | bytes 65568 | tf_op jit(solution)/shard_map/ppermute | solution.py:194
  65.6 3.2 %collective-permute-done.11.refs_1_ = bf16[64,512]{1,0:T(8,128)(2,1)S(1)} collective-permute-done((bf16[64,512]{1,0:T(8,128)(2,1)}, bf16[64,512]{1,0:T(8,128)(2,1)S(1)}, u32[]{:S(2)}, u32[]{:S(2)}) %collective-permute-start.11) | collective-permute-done | bytes 65568 | tf_op jit(solution)/shard_map/ppermute | solution.py:194
  68.9 0.9 %collective-permute-done.12.refs_2_ = bf16[64,512]{1,0:T(8,128)(2,1)S(1)} collective-permute-done((bf16[64,512]{1,0:T(8,128)(2,1)}, bf16[64,512]{1,0:T(8,128)(2,1)S(1)}, u32[]{:S(2)}, u32[]{:S(2)}) %collective-permute-start.12) | collective-permute-done | bytes 65568 | tf_op jit(solution)/shard_map/ppermute | solution.py:194
  70.4 1.6 %shard_map.71 = (f32[64,256]{1,0:T(8,128)}, f32[64,256]{1,0:T(8,128)}) custom-call(f32[64,512]{1,0:T(8,128)} %get-tuple-element.14.keep, bf16[64,512]{1,0:T(8,128)(2,1)} %copy-done.11, bf16[64,512]{1,0:T(8,128)(2,1)} %copy-done.12, bf16[64,512]{1,0:T(8,128)(2,1)} %copy-done.13), custom_call_target="tpu_custom_call" | custom-call | tf_op jit(solution)/shard_map/pallas_call | solution.py:152
  (40 shorter events, 4.8 us)
Async XLA Ops:
  1.5 7.7 %collective-permute-start.1 = (bf16[64,512]{1,0:T(8,128)(2,1)S(1)}, bf16[64,512]{1,0:T(8,128)(2,1)S(1)}, u32[]{:S(2)}, u32[]{:S(2)}) collective-permute-start(bf16[64,512]{1,0:T(8,128)(2,1)S(1)} %get-tuple-element.19), channel_id=1, source_target_pairs={{0,4},{4,8},{8,12},{12,16},{16,20},{20,24},{24,28},{1,5},{5,9},{9,... | collective-permute-start | bytes 196616 | tf_op jit(solution)/shard_map/ppermute | solution.py:174
  6.4 18.6 %collective-permute-start.5 = (bf16[64,4864]{1,0:T(8,128)(2,1)}, bf16[64,4864]{1,0:T(8,128)(2,1)S(1)}, u32[]{:S(2)}, u32[]{:S(2)}) collective-permute-start(bf16[64,4864]{1,0:T(8,128)(2,1)} %bitcast.3), channel_id=1, source_target_pairs={{0,2},{1,3},{2,0},{3,1},{4,6},{5,7},{6,4},{7,5},{8,10},{9,11},{10,... | collective-permute-start | bytes 1867784 | tf_op jit(solution)/shard_map/ppermute | solution.py:172
  8.0 6.1 %collective-permute-start.2 = (bf16[64,512]{1,0:T(8,128)(2,1)S(1)}, bf16[64,512]{1,0:T(8,128)(2,1)S(1)}, u32[]{:S(2)}, u32[]{:S(2)}) collective-permute-start(bf16[64,512]{1,0:T(8,128)(2,1)S(1)} %get-tuple-element.18), channel_id=1, source_target_pairs={{4,0},{8,4},{12,8},{16,12},{20,16},{24,20},{28,24},{5,1},{9,5},{13... | collective-permute-start | bytes 196616 | tf_op jit(solution)/shard_map/ppermute | solution.py:175
  14.1 10.9 %collective-permute-start.7 = (bf16[64,1024]{1,0:T(8,128)(2,1)S(1)}, bf16[64,1024]{1,0:T(8,128)(2,1)S(1)}, u32[]{:S(2)}, u32[]{:S(2)}) collective-permute-start(bf16[64,1024]{1,0:T(8,128)(2,1)S(1)} %constant_dynamic-update-slice_fusion), channel_id=1, source_target_pairs={{0,2},{1,3},{2,0},{3,1},{4,6},{5,7},{6,4},{7,5},{8,10},{9,11},{10,... | collective-permute-start | bytes 393224 | tf_op jit(solution)/shard_map/ppermute | solution.py:177
  14.6 11.7 %collective-permute-start = (bf16[64,4864]{1,0:T(8,128)(2,1)}, bf16[64,4864]{1,0:T(8,128)(2,1)S(1)}, u32[]{:S(2)}, u32[]{:S(2)}) collective-permute-start(bf16[64,4864]{1,0:T(8,128)(2,1)} %bitcast.4), channel_id=1, source_target_pairs={{0,1},{1,0},{2,3},{3,2},{4,5},{5,4},{6,7},{7,6},{8,9},{9,8},{10,11... | collective-permute-start | bytes 1867784 | tf_op jit(solution)/shard_map/ppermute | solution.py:173
  14.6 10.9 %collective-permute-start.3 = (bf16[64,1024]{1,0:T(8,128)(2,1)S(1)}, bf16[64,1024]{1,0:T(8,128)(2,1)S(1)}, u32[]{:S(2)}, u32[]{:S(2)}) collective-permute-start(bf16[64,1024]{1,0:T(8,128)(2,1)S(1)} %constant_dynamic-update-slice_fusion), channel_id=1, source_target_pairs={{0,1},{1,0},{2,3},{3,2},{4,5},{5,4},{6,7},{7,6},{8,9},{9,8},{10,11... | collective-permute-start | bytes 393224 | tf_op jit(solution)/shard_map/ppermute | solution.py:178
  25.0 1.3 %collective-permute-start.8 = (bf16[64,1024]{1,0:T(8,128)(2,1)S(1)}, bf16[64,1024]{1,0:T(8,128)(2,1)S(1)}, u32[]{:S(2)}, u32[]{:S(2)}) collective-permute-start(bf16[64,1024]{1,0:T(8,128)(2,1)S(1)} %collective-permute-done.7), channel_id=1, source_target_pairs={{0,1},{1,0},{2,3},{3,2},{4,5},{5,4},{6,7},{7,6},{8,9},{9,8},{10,11... | collective-permute-start | bytes 393224 | tf_op jit(solution)/shard_map/ppermute | solution.py:186
  25.0 19.4 %collective-permute-start.6 = (bf16[64,4864]{1,0:T(8,128)(2,1)S(1)}, bf16[64,4864]{1,0:T(8,128)(2,1)S(1)}, u32[]{:S(2)}, u32[]{:S(2)}) collective-permute-start(bf16[64,4864]{1,0:T(8,128)(2,1)S(1)} %collective-permute-done.5.mine), channel_id=1, source_target_pairs={{0,1},{1,0},{2,3},{3,2},{4,5},{5,4},{6,7},{7,6},{8,9},{9,8},{10,11... | collective-permute-start | bytes 1867784 | tf_op jit(solution)/shard_map/ppermute | solution.py:185
  26.3 2.4 %copy-start = (bf16[4864,512]{1,0:T(8,128)(2,1)S(1)}, bf16[4864,512]{1,0:T(8,128)(2,1)}, u32[]{:S(2)}) copy-start(bf16[4864,512]{1,0:T(8,128)(2,1)} %basis_hbm.3) | copy-start | bytes 14942212
  28.8 2.1 %copy-start.2 = (bf16[38,3,128,128]{3,2,1,0:T(8,128)(2,1)S(1)}, bf16[38,3,128,128]{3,2,1,0:T(8,128)(2,1)}, u32[]{:S(2)}) copy-start(bf16[38,3,128,128]{3,2,1,0:T(8,128)(2,1)} %g_hbm.3) | copy-start | bytes 11206660
  30.8 2.1 %copy-start.4 = (bf16[38,3,128,128]{3,2,1,0:T(8,128)(2,1)S(1)}, bf16[38,3,128,128]{3,2,1,0:T(8,128)(2,1)}, u32[]{:S(2)}) copy-start(bf16[38,3,128,128]{3,2,1,0:T(8,128)(2,1)} %c_hbm.3) | copy-start | bytes 11206660
  32.9 1.1 %copy-start.5 = (bf16[4864,64]{0,1:T(8,128)(2,1)S(1)}, bf16[4864,64]{0,1:T(8,128)(2,1)}, u32[]{:S(2)}) copy-start(bf16[4864,64]{0,1:T(8,128)(2,1)} %param.5) | copy-start | bytes 1867780
  34.6 9.8 %copy-start.1 = (bf16[4864,512]{1,0:T(8,128)(2,1)S(1)}, bf16[4864,512]{1,0:T(8,128)(2,1)}, u32[]{:S(2)}) copy-start(bf16[4864,512]{1,0:T(8,128)(2,1)} %basis_hbm.3) | copy-start | bytes 14942212
  34.6 9.8 %copy-start.3 = (bf16[38,3,128,128]{3,2,1,0:T(8,128)(2,1)S(1)}, bf16[38,3,128,128]{3,2,1,0:T(8,128)(2,1)}, u32[]{:S(2)}) copy-start(bf16[38,3,128,128]{3,2,1,0:T(8,128)(2,1)} %g_hbm.3) | copy-start | bytes 11206660
  42.2 0.7 copy-start.6
  42.9 10.3 %collective-permute-start.4 = (bf16[4,64,256]{2,1,0:T(8,128)(2,1)S(1)}, bf16[4,64,256]{2,1,0:T(8,128)(2,1)S(1)}, u32[]{:S(2)}, u32[]{:S(2)}) collective-permute-start(bf16[4,64,256]{2,1,0:T(8,128)(2,1)S(1)} %get-tuple-element.11), channel_id=1, source_target_pairs={{0,4},{4,0},{8,12},{12,8},{16,20},{20,16},{24,28},{28,24},{1,5},{5... | collective-permute-start | bytes 393224 | tf_op jit(solution)/shard_map/ppermute | solution.py:184
  52.0 0.7 copy-start.7
  52.7 5.3 %collective-permute-start.9 = (bf16[4,64,256]{2,1,0:T(8,128)(2,1)S(1)}, bf16[4,64,256]{2,1,0:T(8,128)(2,1)S(1)}, u32[]{:S(2)}, u32[]{:S(2)}) collective-permute-start(bf16[4,64,256]{2,1,0:T(8,128)(2,1)S(1)} %get-tuple-element.13), channel_id=1, source_target_pairs={{0,4},{4,0},{8,12},{12,8},{16,20},{20,16},{24,28},{28,24},{1,5},{5... | collective-permute-start | bytes 393224 | tf_op jit(solution)/shard_map/ppermute | solution.py:190
  53.2 4.8 %copy-start.9 = (bf16[4,64,256]{2,1,0:T(8,128)(2,1)}, bf16[4,64,256]{2,1,0:T(8,128)(2,1)S(1)}, u32[]{:S(2)}) copy-start(bf16[4,64,256]{2,1,0:T(8,128)(2,1)S(1)} %collective-permute-done.4.got_a) | copy-start | bytes 393220
  60.5 5.1 %collective-permute-start.10 = (bf16[64,512]{1,0:T(8,128)(2,1)}, bf16[64,512]{1,0:T(8,128)(2,1)S(1)}, u32[]{:S(2)}, u32[]{:S(2)}) collective-permute-start(bf16[64,512]{1,0:T(8,128)(2,1)} %get-tuple-element.15), channel_id=1, source_target_pairs={{0,8},{4,12},{8,0},{12,4},{16,24},{20,28},{24,16},{28,20},{1,9},{5... | collective-permute-start | bytes 196616 | tf_op jit(solution)/shard_map/ppermute | solution.py:194
  62.1 6.8 %collective-permute-start.11 = (bf16[64,512]{1,0:T(8,128)(2,1)}, bf16[64,512]{1,0:T(8,128)(2,1)S(1)}, u32[]{:S(2)}, u32[]{:S(2)}) collective-permute-start(bf16[64,512]{1,0:T(8,128)(2,1)} %get-tuple-element.16), channel_id=1, source_target_pairs={{0,16},{4,20},{8,24},{12,28},{16,0},{20,4},{24,8},{28,12},{1,17},{... | collective-permute-start | bytes 196616 | tf_op jit(solution)/shard_map/ppermute | solution.py:194
  63.4 6.4 %collective-permute-start.12 = (bf16[64,512]{1,0:T(8,128)(2,1)}, bf16[64,512]{1,0:T(8,128)(2,1)S(1)}, u32[]{:S(2)}, u32[]{:S(2)}) collective-permute-start(bf16[64,512]{1,0:T(8,128)(2,1)} %get-tuple-element.17), channel_id=1, source_target_pairs={{0,24},{4,28},{8,16},{12,20},{16,8},{20,12},{24,0},{28,4},{1,25},{... | collective-permute-start | bytes 196616 | tf_op jit(solution)/shard_map/ppermute | solution.py:194
  65.6 4.2 %copy-start.11 = (bf16[64,512]{1,0:T(8,128)(2,1)}, bf16[64,512]{1,0:T(8,128)(2,1)S(1)}, u32[]{:S(2)}) copy-start(bf16[64,512]{1,0:T(8,128)(2,1)S(1)} %collective-permute-done.10.refs_0_) | copy-start | bytes 196612
  68.9 1.0 %copy-start.12 = (bf16[64,512]{1,0:T(8,128)(2,1)}, bf16[64,512]{1,0:T(8,128)(2,1)S(1)}, u32[]{:S(2)}) copy-start(bf16[64,512]{1,0:T(8,128)(2,1)S(1)} %collective-permute-done.11.refs_1_) | copy-start | bytes 196612
  (3 other events, 2.0 us)

commit v2 on v1

--- a/solution.py
+++ b/solution.py
@@ -9,6 +9,7 @@
 
 BS = 128
 HB = 4
+MIB = 1024 * 1024
 F32 = jnp.float32
 BF16 = jnp.bfloat16
 
@@ -18,29 +19,42 @@
     return list(zip(edges[:-1], edges[1:]))
 
 
-def project_kernel(groups, ids_ref, mine, other, low_m, high_m, low_o, high_o, g_hbm, c_hbm, basis_hbm,
-                   send_ref, keep_ref, ext, g_buf, c_buf, b_buf, yt, acc, sems):
-    rows = g_hbm.shape[0]
-    slots = g_hbm.shape[1]
-    width = mine.shape[0]
-    inner = mine.shape[1]
+def load_kernel(*refs):
+    count = len(refs) // 2
+    sources, targets, sems = refs[:count], refs[count:2 * count], refs[-1]
+    copies = []
+    for which, (source, target) in enumerate(zip(sources, targets)):
+        for part, (lo, hi) in enumerate(cuts(source.shape[0], 2)):
+            span = pl.ds(lo, hi - lo)
+            copies.append(pltpu.make_async_copy(source.at[span], target.at[span], sems.at[which, part]))
+    for copy in copies:
+        copy.start()
+    for copy in copies:
+        copy.wait()
+
+
+def load(*arrays):
+    hbm = pl.BlockSpec(memory_space=pltpu.HBM)
+    anywhere = pl.BlockSpec(memory_space=pl.ANY)
+    size = sum(array.size * array.dtype.itemsize for array in arrays)
+    return pl.pallas_call(
+        load_kernel,
+        out_shape=[jax.ShapeDtypeStruct(array.shape, array.dtype) for array in arrays],
+        in_specs=[hbm] * len(arrays),
+        out_specs=[anywhere] * len(arrays),
+        scratch_shapes=[pltpu.SemaphoreType.DMA((len(arrays), 2))],
+        compiler_params=pltpu.CompilerParams(vmem_limit_bytes=44 * MIB),
+        cost_estimate=pl.CostEstimate(flops=0, bytes_accessed=size // 100, transcendentals=0),
+    )(*arrays)
+
+
+def project_kernel(groups, ids_ref, mine, other, low_m, high_m, low_o, high_o, g_ref, c_ref, basis_ref,
+                   send_ref, keep_ref, ext, prods):
+    rows, slots = g_ref.shape[0], g_ref.shape[1]
+    width, inner = mine.shape
     halo = HB * BS
     node = lax.axis_index("node")
     core = lax.axis_index("col") % 2
-    spans = cuts(rows, 4)
-
-    copies = []
-    for step, (lo, hi) in enumerate(spans):
-        span = pl.ds(lo, hi - lo)
-        nodes = pl.ds(lo * BS, (hi - lo) * BS)
-        batch = [
-            pltpu.make_async_copy(g_hbm.at[span], g_buf.at[span], sems.at[step, 0]),
-            pltpu.make_async_copy(c_hbm.at[span], c_buf.at[span], sems.at[step, 1]),
-            pltpu.make_async_copy(basis_hbm.at[nodes], b_buf.at[nodes], sems.at[step, 2]),
-        ]
-        for copy in batch:
-            copy.start()
-        copies.append(batch)
 
     for place, low, middle, high in ((core, low_m, mine, high_m), (1 - core, low_o, other, high_o)):
         at = pl.ds(pl.multiple_of(place * width, width), width)
@@ -49,32 +63,21 @@
         ext[at, halo + inner:] = high[...]
 
     offset = node * rows - HB
-    for step, (lo, hi) in enumerate(spans):
-        for copy in copies[step]:
-            copy.wait()
-        for row in range(lo, hi):
-            near = []
-            for slot in range(slots):
-                local = jnp.clip(ids_ref[slot, row] - offset, 0, rows + 2 * HB - 1)
-                near.append(ext[:, pl.ds(pl.multiple_of(local * BS, BS), BS)])
-            near = jnp.concatenate(near, axis=1)
-            both = jnp.concatenate(
-                [
-                    jnp.concatenate([g_buf[row, slot] for slot in range(slots)], axis=1),
-                    jnp.concatenate([c_buf[row, slot] for slot in range(slots)], axis=1),
-                ],
-                axis=0,
-            )
-            prod = lax.dot_general(near, both, (((1,), (1,)), ((), ())), preferred_element_type=F32)
-            prod = prod.astype(BF16)
-            yt[0:2 * width, row * BS:(row + 1) * BS] = prod[:, 0:BS]
-            yt[2 * width:4 * width, row * BS:(row + 1) * BS] = prod[:, BS:2 * BS]
-        part = jnp.dot(yt[:, lo * BS:hi * BS], b_buf[lo * BS:hi * BS, :], preferred_element_type=F32)
-        if step == 0:
-            acc[...] = part
-        else:
-            acc[...] += part
-    total = acc[...].T
+    for row in range(rows):
+        near = []
+        for slot in range(slots):
+            local = jnp.clip(ids_ref[slot, row] - offset, 0, rows + 2 * HB - 1)
+            near.append(ext[:, pl.ds(pl.multiple_of(local * BS, BS), BS)])
+        near = jnp.concatenate(near, axis=1)
+        both = jnp.concatenate(
+            [jnp.concatenate([ref[row, slot] for slot in range(slots)], axis=1) for ref in (g_ref, c_ref)], axis=0
+        )
+        prod = lax.dot_general(both, near, (((1,), (1,)), ((), ())), preferred_element_type=F32).astype(BF16)
+        prods[row * BS:(row + 1) * BS, 0:2 * width] = prod[0:BS]
+        prods[row * BS:(row + 1) * BS, 2 * width:4 * width] = prod[BS:2 * BS]
+    total = lax.dot_general(
+        basis_ref[...], prods[...], (((0,), (0,)), ((), ())), preferred_element_type=F32
+    )
     states, columns = total.shape
     total = total.reshape(groups, 2, states // (2 * groups), columns)
     odd = node % 2 == 1
@@ -88,24 +91,18 @@
     states = basis.shape[1]
     piece = (groups, states // (2 * groups), 4 * width)
     vmem = pl.BlockSpec(memory_space=pltpu.VMEM)
-    hbm = pl.BlockSpec(memory_space=pl.ANY)
     flops = 2 * rows * BS * 4 * width * (slots * BS + states)
     return pl.pallas_call(
         functools.partial(project_kernel, groups),
         out_shape=(jax.ShapeDtypeStruct(piece, BF16), jax.ShapeDtypeStruct(piece, F32)),
-        in_specs=[pl.BlockSpec(memory_space=pltpu.SMEM)] + [vmem] * 6 + [hbm] * 3,
+        in_specs=[pl.BlockSpec(memory_space=pltpu.SMEM)] + [vmem] * 9,
         out_specs=(vmem, vmem),
         scratch_shapes=[
             pltpu.VMEM((2 * width, inner + 2 * HB * BS), BF16),
-            pltpu.VMEM(g_blocks.shape, BF16),
-            pltpu.VMEM(c_blocks.shape, BF16),
-            pltpu.VMEM(basis.shape, BF16),
-            pltpu.VMEM((4 * width, inner), BF16),
-            pltpu.VMEM((4 * width, states), F32),
-            pltpu.SemaphoreType.DMA((4, 3)),
+            pltpu.VMEM((inner, 4 * width), BF16),
         ],
-        compiler_params=pltpu.CompilerParams(vmem_limit_bytes=40 * 1024 * 1024),
-        cost_estimate=pl.CostEstimate(flops=flops, bytes_accessed=14_000_000, transcendentals=0),
+        compiler_params=pltpu.CompilerParams(vmem_limit_bytes=14 * MIB),
+        cost_estimate=pl.CostEstimate(flops=flops // 100, bytes_accessed=0, transcendentals=0),
     )(ids, mine, other, *halos_m, *halos_o, g_blocks, c_blocks, basis)
 
 
@@ -130,6 +127,7 @@
         out_shape=[jax.ShapeDtypeStruct(piece, F32)] + [jax.ShapeDtypeStruct(piece, BF16)] * (groups - 1),
         in_specs=[vmem] * 4,
         out_specs=[vmem] * groups,
+        compiler_params=pltpu.CompilerParams(vmem_limit_bytes=4 * MIB),
     )(keep_a, got_a, keep_b, got_b)
 
 
@@ -154,6 +152,7 @@
         out_shape=(piece, piece),
         in_specs=[vmem] * (1 + len(got)),
         out_specs=(vmem, vmem),
+        compiler_params=pltpu.CompilerParams(vmem_limit_bytes=4 * MIB),
     )(keep, *got)
 
 
@@ -171,8 +170,11 @@
 
     far = lax.ppermute(mine, "col", across)
     other = lax.ppermute(mine, "col", cores)
-    low = lax.ppermute(mine[:, -halo:], "node", up)
-    high = lax.ppermute(mine[:, :halo], "node", down)
+    last, first, other = lax.optimization_barrier((mine[:, -halo:], mine[:, :halo], other))
+    low = lax.ppermute(last, "node", up)
+    high = lax.ppermute(first, "node", down)
+    g_blocks, c_blocks, basis = load(g_blocks, c_blocks, basis)
+    low, high, g_blocks, c_blocks, basis = lax.optimization_barrier((low, high, g_blocks, c_blocks, basis))
     halos = jnp.concatenate([low, high], axis=1)
     far_halos = lax.ppermute(halos, "col", across)
     other_halos = lax.ppermute(halos, "col", cores)
@@ -181,6 +183,7 @@
         return both[:, :halo], both[:, halo:]
 
     send_a, keep_a = project(ids, mine, other, (low, high), sides(other_halos), g_blocks, c_blocks, basis, groups)
+    far, send_a = lax.optimization_barrier((far, send_a))
     got_a = lax.ppermute(send_a, "node", pairs)
     far_other = lax.ppermute(far, "col", cores)
     far_other_halos = lax.ppermute(far_halos, "col", cores)

time: 72.5 us -> 201 us (2.77)
  Pallas kernels: 18.7 us -> 161 us
  waiting for transfers between devices: 25.1 us -> 16.1 us
  local copies, waits for them, and re-layouts: 11.9 us -> 3.33 us
  starting transfers between devices: 15.7 us -> 19.8 us
    pallas_call x0 -> x1, Pallas kernels: none -> 152 us  [load(): pl.pallas_call(load_kernel, out_shape=[jax.ShapeDtypeStruct(array.shape,...]
    unnamed x29 -> x7, local copies, waits for them, and re-layouts: 10.9 us -> 2.42 us
    ppermute x1, waiting for transfers between devices: 9.82 us -> 2.57 us  [body(): far_halos = lax.ppermute(halos, 'col', across)]
    pallas_call x2, Pallas kernels: 15.2 us -> 8.25 us  [project(): pl.pallas_call(functools.partial(project_kernel, groups), out_shape=(jax....]
    ppermute x2, waiting for transfers between devices: 4.84 us -> 0.01 us  [the longest x1 0.01 us: body(): high = lax.ppermute(first, 'node', down)]
    ppermute x1, starting transfers between devices: 0.48 us -> 2.71 us  [body(): got_b = lax.ppermute(send_b, 'node', pairs)]
  transfers between devices with their start and end apart: 13 -> 13, of which waited for: 7 -> 7; matrix products, arithmetic and copies ran while one was open for 0% -> 0% of each run, Pallas kernels for 21% -> 80%
where the time goes in v2:
time: 201 us
  Pallas kernels  161 us (80%)
  starting transfers between devices  19.8 us (10%)
  waiting for transfers between devices  16.1 us (8%)
  local copies, waits for them, and re-layouts  3.33 us (2%)
    pallas_call x1, Pallas kernels, load(): pl.pallas_call(load_kernel, out_shape=[jax.ShapeDtypeStruct(array.shape,...  152 us
    pallas_call x2, Pallas kernels, project(): pl.pallas_call(functools.partial(project_kernel, groups), out_shape=(jax....  8.25 us
    ppermute x3, waiting for transfers between devices, body(): lax.ppermute(send, 'node', [(i, i ^ 2 * step) for i in range(nodes)])  6.06 us
    ppermute x3, starting transfers between devices, body(): lax.ppermute(send, 'node', [(i, i ^ 2 * step) for i in range(nodes)])  5.34 us
    ppermute x1, starting transfers between devices, body(): low = lax.ppermute(last, 'node', up)  4.91 us
  transfers between devices with their start and end apart: 13, of which 7 were waited for; matrix products, arithmetic and copies ran while one was open for 0% of the time, Pallas kernels for 80%

profile of v2, /device:TPU:0, one launch (start us, length us, event | category | flops | bytes accessed | tf_op | source)
XLA Modules:
  0.0 201.0 jit_solution(8844025022490083735)
XLA Ops:
  0.6 0.5 collective-permute-start
  1.1 0.9 fusion
  2.0 1.0 collective-permute-done.other
  3.0 4.9 %collective-permute-start.1 = (bf16[64,512]{1,0:T(8,128)(2,1)S(1)}, bf16[64,512]{1,0:T(8,128)(2,1)S(1)}, u32[]{:S(2)}, u32[]{:S(2)}) collective-permute-start(bf16[64,512]{1,0:T(8,128)(2,1)S(1)} %get-tuple-element.24), channel_id=1, source_target_pairs={{0,4},{4,8},{8,12},{12,16},{16,20},{20,24},{24,28},{1,5},{5,9},{9,... | collective-permute-start | bytes 196616 | tf_op jit(solution)/shard_map/ppermute | solution.py:174
  8.0 1.3 collective-permute-start.2
  9.3 1.6 collective-permute-start.4
  10.8 152.0 %shard_map.68 = (bf16[38,3,128,128]{3,2,1,0:T(8,128)(2,1)S(1)}, bf16[38,3,128,128]{3,2,1,0:T(8,128)(2,1)S(1)}, bf16[4864,512]{1,0:T(8,128)(2,1)}) custom-call(bf16[38,3,128,128]{3,2,1,0:T(8,128)(2,1)} %refs_0_.1, bf16[38,3,128,128]{3,2,1,0:T(8,128)(2,1)} %refs_1_.1, bf16[4864,512]{1,0:T(8,128)(2,1)} %refs_2_.1), custom_call_target="tpu_custom_call" | custom-call | bytes 124518 | tf_op jit(solution)/shard_map/pallas_call | solution.py:40
  162.9 0.1 collective-permute-start.3
  163.0 1.3 collective-permute-done.3
  164.4 2.4 %copy-done = bf16[4864,512]{1,0:T(8,128)(2,1)S(1)} copy-done((bf16[4864,512]{1,0:T(8,128)(2,1)S(1)}, bf16[4864,512]{1,0:T(8,128)(2,1)}, u32[]{:S(2)}) %copy-start) | copy-done | bytes 4980760
  166.8 4.1 %shard_map.69 = (bf16[4,64,256]{2,1,0:T(8,128)(2,1)S(1)}, f32[4,64,256]{2,1,0:T(8,128)S(1)}) custom-call(s32[3,38]{1,0:T(4,128)S(1)} %bitcast.6, bf16[64,4864]{1,0:T(8,128)(2,1)S(1)} %bitcast.5, bf16[64,4864]{1,0:T(8,128)(2,1)S(1)} %collective-permute-done.other, bf16[64,512]{1,0:T(8,128)(2,1)S(1)} %collective-permute-done.1.low_m, ...), custom_call_target="tpu_custom_call" | custom-call | flops 22313696 | tf_op jit(solution)/shard_map/pallas_call | solution.py:95
  170.9 0.2 collective-permute-start.6
  171.1 0.5 collective-permute-start.7
  171.7 2.6 %collective-permute-start.5 = (bf16[4,64,256]{2,1,0:T(8,128)(2,1)S(1)}, bf16[4,64,256]{2,1,0:T(8,128)(2,1)S(1)}, u32[]{:S(2)}, u32[]{:S(2)}) collective-permute-start(bf16[4,64,256]{2,1,0:T(8,128)(2,1)S(1)} %get-tuple-element.36), channel_id=1, source_target_pairs={{0,4},{4,0},{8,12},{12,8},{16,20},{20,16},{24,28},{28,24},{1,5},{5... | collective-permute-start | bytes 393224 | tf_op jit(solution)/shard_map/ppermute | solution.py:187
  174.3 2.6 %collective-permute-done.7 = bf16[64,1024]{1,0:T(8,128)(2,1)S(1)} collective-permute-done((bf16[64,1024]{1,0:T(8,128)(2,1)S(1)}, bf16[64,1024]{1,0:T(8,128)(2,1)S(1)}, u32[]{:S(2)}, u32[]{:S(2)}) %collective-permute-start.7) | collective-permute-done | bytes 131104 | tf_op jit(solution)/shard_map/ppermute | solution.py:179
  176.9 1.3 collective-permute-done.8
  178.3 4.1 %shard_map.70 = (bf16[4,64,256]{2,1,0:T(8,128)(2,1)S(1)}, f32[4,64,256]{2,1,0:T(8,128)S(1)}) custom-call(s32[3,38]{1,0:T(4,128)S(1)} %bitcast.7, bf16[64,4864]{1,0:T(8,128)(2,1)S(1)} %collective-permute-done.4.mine, bf16[64,4864]{1,0:T(8,128)(2,1)S(1)} %collective-permute-done.6.other, bf16[64,512]{1,0:T(8,128)(2,1)S(1)} %get-tuple-element.49.low_m, ...), custom_call_target="tpu_custom_call" | custom-call | flops 22313696 | tf_op jit(solution)/shard_map/pallas_call | solution.py:95
  182.4 2.7 %collective-permute-start.9 = (bf16[4,64,256]{2,1,0:T(8,128)(2,1)S(1)}, bf16[4,64,256]{2,1,0:T(8,128)(2,1)S(1)}, u32[]{:S(2)}, u32[]{:S(2)}) collective-permute-start(bf16[4,64,256]{2,1,0:T(8,128)(2,1)S(1)} %get-tuple-element.39), channel_id=1, source_target_pairs={{0,4},{4,0},{8,12},{12,8},{16,20},{20,16},{24,28},{28,24},{1,5},{5... | collective-permute-start | bytes 393224 | tf_op jit(solution)/shard_map/ppermute | solution.py:193
  185.1 3.8 %collective-permute-done.9.got_b = bf16[4,64,256]{2,1,0:T(8,128)(2,1)S(1)} collective-permute-done((bf16[4,64,256]{2,1,0:T(8,128)(2,1)S(1)}, bf16[4,64,256]{2,1,0:T(8,128)(2,1)S(1)}, u32[]{:S(2)}, u32[]{:S(2)}) %collective-permute-start.9) | collective-permute-done | bytes 131104 | tf_op jit(solution)/shard_map/ppermute | solution.py:193
  189.0 2.7 %collective-permute-start.10 = (bf16[64,512]{1,0:T(8,128)(2,1)S(1)}, bf16[64,512]{1,0:T(8,128)(2,1)S(1)}, u32[]{:S(2)}, u32[]{:S(2)}) collective-permute-start(bf16[64,512]{1,0:T(8,128)(2,1)S(1)} %get-tuple-element.41), channel_id=1, source_target_pairs={{0,8},{4,12},{8,0},{12,4},{16,24},{20,28},{24,16},{28,20},{1,9},{5... | collective-permute-start | bytes 196616 | tf_op jit(solution)/shard_map/ppermute | solution.py:197
  191.7 2.6 %collective-permute-start.11 = (bf16[64,512]{1,0:T(8,128)(2,1)S(1)}, bf16[64,512]{1,0:T(8,128)(2,1)S(1)}, u32[]{:S(2)}, u32[]{:S(2)}) collective-permute-start(bf16[64,512]{1,0:T(8,128)(2,1)S(1)} %get-tuple-element.42), channel_id=1, source_target_pairs={{0,16},{4,20},{8,24},{12,28},{16,0},{20,4},{24,8},{28,12},{1,17},{... | collective-permute-start | bytes 196616 | tf_op jit(solution)/shard_map/ppermute | solution.py:197
  194.3 4.2 %collective-permute-done.11.refs_1_ = bf16[64,512]{1,0:T(8,128)(2,1)S(1)} collective-permute-done((bf16[64,512]{1,0:T(8,128)(2,1)S(1)}, bf16[64,512]{1,0:T(8,128)(2,1)S(1)}, u32[]{:S(2)}, u32[]{:S(2)}) %collective-permute-start.11) | collective-permute-done | bytes 65568 | tf_op jit(solution)/shard_map/ppermute | solution.py:197
  198.5 1.9 collective-permute-done.12.refs_2_
  200.4 0.7 shard_map.72
  (19 shorter events, 0.1 us)
Async XLA Ops:
  0.6 2.4 %collective-permute-start = (bf16[64,4864]{1,0:T(8,128)(2,1)}, bf16[64,4864]{1,0:T(8,128)(2,1)S(1)}, u32[]{:S(2)}, u32[]{:S(2)}) collective-permute-start(bf16[64,4864]{1,0:T(8,128)(2,1)} %bitcast.2), channel_id=1, source_target_pairs={{0,1},{1,0},{2,3},{3,2},{4,5},{5,4},{6,7},{7,6},{8,9},{9,8},{10,11... | collective-permute-start | bytes 1867784 | tf_op jit(solution)/shard_map/ppermute | solution.py:172
  3.0 161.3 %copy-start.1 = (bf16[4864,64]{0,1:T(8,128)(2,1)S(1)}, bf16[4864,64]{0,1:T(8,128)(2,1)}, u32[]{:S(2)}) copy-start(bf16[4864,64]{0,1:T(8,128)(2,1)} %param.5) | copy-start | bytes 1867780
  3.0 161.3 %copy-start.2 = (s32[38,3]{0,1:T(4,128)S(1)}, s32[38,3]{0,1:T(4,128)}, u32[]{:S(2)}) copy-start(s32[38,3]{0,1:T(4,128)} %param.9) | copy-start | bytes 1372
  3.0 159.8 %collective-permute-start.1 = (bf16[64,512]{1,0:T(8,128)(2,1)S(1)}, bf16[64,512]{1,0:T(8,128)(2,1)S(1)}, u32[]{:S(2)}, u32[]{:S(2)}) collective-permute-start(bf16[64,512]{1,0:T(8,128)(2,1)S(1)} %get-tuple-element.24), channel_id=1, source_target_pairs={{0,4},{4,8},{8,12},{12,16},{16,20},{20,24},{24,28},{1,5},{5,9},{9,... | collective-permute-start | bytes 196616 | tf_op jit(solution)/shard_map/ppermute | solution.py:174
  8.0 154.9 %collective-permute-start.2 = (bf16[64,512]{1,0:T(8,128)(2,1)S(1)}, bf16[64,512]{1,0:T(8,128)(2,1)S(1)}, u32[]{:S(2)}, u32[]{:S(2)}) collective-permute-start(bf16[64,512]{1,0:T(8,128)(2,1)S(1)} %get-tuple-element.25), channel_id=1, source_target_pairs={{4,0},{8,4},{12,8},{16,12},{20,16},{24,20},{28,24},{5,1},{9,5},{13... | collective-permute-start | bytes 196616 | tf_op jit(solution)/shard_map/ppermute | solution.py:175
  9.3 161.6 %collective-permute-start.4 = (bf16[64,4864]{1,0:T(8,128)(2,1)}, bf16[64,4864]{1,0:T(8,128)(2,1)S(1)}, u32[]{:S(2)}, u32[]{:S(2)}) collective-permute-start(bf16[64,4864]{1,0:T(8,128)(2,1)} %bitcast.4), channel_id=1, source_target_pairs={{0,2},{1,3},{2,0},{3,1},{4,6},{5,7},{6,4},{7,5},{8,10},{9,11},{10,... | collective-permute-start | bytes 1867784 | tf_op jit(solution)/shard_map/ppermute | solution.py:171
  162.9 1.4 collective-permute-start.3
  164.4 2.4 %copy-start = (bf16[4864,512]{1,0:T(8,128)(2,1)S(1)}, bf16[4864,512]{1,0:T(8,128)(2,1)}, u32[]{:S(2)}) copy-start(bf16[4864,512]{1,0:T(8,128)(2,1)} %get-tuple-element.33.basis_ref) | copy-start | bytes 14942212
  170.9 7.3 %collective-permute-start.6 = (bf16[64,4864]{1,0:T(8,128)(2,1)S(1)}, bf16[64,4864]{1,0:T(8,128)(2,1)S(1)}, u32[]{:S(2)}, u32[]{:S(2)}) collective-permute-start(bf16[64,4864]{1,0:T(8,128)(2,1)S(1)} %collective-permute-done.4.mine), channel_id=1, source_target_pairs={{0,1},{1,0},{2,3},{3,2},{4,5},{5,4},{6,7},{7,6},{8,9},{9,8},{10,11... | collective-permute-start | bytes 1867784 | tf_op jit(solution)/shard_map/ppermute | solution.py:188
  171.1 5.8 %collective-permute-start.7 = (bf16[64,1024]{1,0:T(8,128)(2,1)S(1)}, bf16[64,1024]{1,0:T(8,128)(2,1)S(1)}, u32[]{:S(2)}, u32[]{:S(2)}) collective-permute-start(bf16[64,1024]{1,0:T(8,128)(2,1)S(1)} %constant_dynamic-update-slice_fusion), channel_id=1, source_target_pairs={{0,2},{1,3},{2,0},{3,1},{4,6},{5,7},{6,4},{7,5},{8,10},{9,11},{10,... | collective-permute-start | bytes 393224 | tf_op jit(solution)/shard_map/ppermute | solution.py:179
  171.7 13.4 %collective-permute-start.5 = (bf16[4,64,256]{2,1,0:T(8,128)(2,1)S(1)}, bf16[4,64,256]{2,1,0:T(8,128)(2,1)S(1)}, u32[]{:S(2)}, u32[]{:S(2)}) collective-permute-start(bf16[4,64,256]{2,1,0:T(8,128)(2,1)S(1)} %get-tuple-element.36), channel_id=1, source_target_pairs={{0,4},{4,0},{8,12},{12,8},{16,20},{20,16},{24,28},{28,24},{1,5},{5... | collective-permute-start | bytes 393224 | tf_op jit(solution)/shard_map/ppermute | solution.py:187
  176.9 1.3 collective-permute-start.8
  182.4 6.5 %collective-permute-start.9 = (bf16[4,64,256]{2,1,0:T(8,128)(2,1)S(1)}, bf16[4,64,256]{2,1,0:T(8,128)(2,1)S(1)}, u32[]{:S(2)}, u32[]{:S(2)}) collective-permute-start(bf16[4,64,256]{2,1,0:T(8,128)(2,1)S(1)} %get-tuple-element.39), channel_id=1, source_target_pairs={{0,4},{4,0},{8,12},{12,8},{16,20},{20,16},{24,28},{28,24},{1,5},{5... | collective-permute-start | bytes 393224 | tf_op jit(solution)/shard_map/ppermute | solution.py:193
  189.0 5.3 %collective-permute-start.10 = (bf16[64,512]{1,0:T(8,128)(2,1)S(1)}, bf16[64,512]{1,0:T(8,128)(2,1)S(1)}, u32[]{:S(2)}, u32[]{:S(2)}) collective-permute-start(bf16[64,512]{1,0:T(8,128)(2,1)S(1)} %get-tuple-element.41), channel_id=1, source_target_pairs={{0,8},{4,12},{8,0},{12,4},{16,24},{20,28},{24,16},{28,20},{1,9},{5... | collective-permute-start | bytes 196616 | tf_op jit(solution)/shard_map/ppermute | solution.py:197
  191.7 6.7 %collective-permute-start.11 = (bf16[64,512]{1,0:T(8,128)(2,1)S(1)}, bf16[64,512]{1,0:T(8,128)(2,1)S(1)}, u32[]{:S(2)}, u32[]{:S(2)}) collective-permute-start(bf16[64,512]{1,0:T(8,128)(2,1)S(1)} %get-tuple-element.42), channel_id=1, source_target_pairs={{0,16},{4,20},{8,24},{12,28},{16,0},{20,4},{24,8},{28,12},{1,17},{... | collective-permute-start | bytes 196616 | tf_op jit(solution)/shard_map/ppermute | solution.py:197
  194.3 6.1 %collective-permute-start.12 = (bf16[64,512]{1,0:T(8,128)(2,1)S(1)}, bf16[64,512]{1,0:T(8,128)(2,1)S(1)}, u32[]{:S(2)}, u32[]{:S(2)}) collective-permute-start(bf16[64,512]{1,0:T(8,128)(2,1)S(1)} %get-tuple-element.43), channel_id=1, source_target_pairs={{0,24},{4,28},{8,16},{12,20},{16,8},{20,12},{24,0},{28,4},{1,25},{... | collective-permute-start | bytes 196616 | tf_op jit(solution)/shard_map/ppermute | solution.py:197

commit v3 on v2

v3 whole, which is shorter than its diff:
```python
import functools

import jax
import jax.numpy as jnp
from jax import lax
from jax.experimental import pallas as pl
from jax.experimental.pallas import tpu as pltpu
from jax.sharding import PartitionSpec as P

BS = 128
HB = 4
MIB = 1024 * 1024
F32 = jnp.float32
BF16 = jnp.bfloat16
VMEM = pl.BlockSpec(memory_space=pltpu.VMEM)
SMEM = pl.BlockSpec(memory_space=pltpu.SMEM)
HBM = pl.BlockSpec(memory_space=pl.ANY)


def params(mib):
    return pltpu.CompilerParams(vmem_limit_bytes=mib * MIB)


def shape(dims, kind):
    return jax.ShapeDtypeStruct(dims, kind)


def cut_kernel(half, panel, ends, first, last, front, sems):
    width, inner = panel.shape
    halo = HB * BS
    copies = [
        (panel.at[:, 0:halo], ends.at[:, 0:halo]),
        (panel.at[:, inner - halo:inner], ends.at[:, halo:2 * halo]),
        (panel.at[:, 0:halo], first),
        (panel.at[:, inner - halo:inner], last),
        (panel.at[:, halo:half], front),
    ]
    copies = [pltpu.make_async_copy(*pair, sems.at[i]) for i, pair in enumerate(copies)]
    for copy in copies:
        copy.start()
    for copy in copies:
        copy.wait()


def cut(panel, half):
    width, inner = panel.shape
    halo = HB * BS
    widths = (2 * halo, halo, halo, half - halo)
    return pl.pallas_call(
        functools.partial(cut_kernel, half),
        out_shape=[shape((width, w), BF16) for w in widths],
        in_specs=[HBM],
        out_specs=[VMEM] * 4,
        scratch_shapes=[pltpu.SemaphoreType.DMA((5,))],
        compiler_params=params(44),
    )(panel)


def load_kernel(*refs):
    count = len(refs) // 2
    sources, targets, sems = refs[:count], refs[count:2 * count], refs[-1]
    copies = []
    for which, (source, target) in enumerate(zip(sources, targets)):
        middle = source.shape[0] // 2
        for part, span in enumerate((pl.ds(0, middle), pl.ds(middle, source.shape[0] - middle))):
            copies.append(pltpu.make_async_copy(source.at[span], target.at[span], sems.at[which, part]))
    for copy in copies:
        copy.start()
    for copy in copies:
        copy.wait()


def load(*arrays):
    size = sum(array.size * array.dtype.itemsize for array in arrays)
    return pl.pallas_call(
        load_kernel,
        out_shape=[shape(array.shape, array.dtype) for array in arrays],
        in_specs=[HBM] * len(arrays),
        out_specs=[VMEM] * len(arrays),
        scratch_shapes=[pltpu.SemaphoreType.DMA((len(arrays), 2))],
        compiler_params=params(48),
        cost_estimate=pl.CostEstimate(flops=0, bytes_accessed=size, transcendentals=0),
    )(*arrays)


def project_kernel(spans, places, groups, more, *refs):
    ids_ref, g_ref, c_ref, basis_ref = refs[:4]
    pieces = refs[4:4 + 2 * len(places)]
    rest = list(refs[4 + 2 * len(places):])
    before = rest.pop(0) if more else None
    *outs, ext, prods = rest
    rows, slots = g_ref.shape[0], g_ref.shape[1]
    width = pieces[0].shape[0]
    node = lax.axis_index("node")
    core = lax.axis_index("col") % 2

    for which, parts in enumerate(places):
        for owner, ref in ((core, pieces[2 * which]), (1 - core, pieces[2 * which + 1])):
            at = pl.ds(pl.multiple_of(owner * width, width), width)
            for source, target, count in parts:
                ext[at, target:target + count] = ref[:, source:source + count]

    offset = node * rows - HB
    at = 0
    total = None
    for lo, hi in spans:
        begin = at
        for row in range(lo, hi):
            near = []
            for slot in range(slots):
                local = jnp.clip(ids_ref[slot, row] - offset, 0, rows + 2 * HB - 1)
                near.append(ext[:, pl.ds(pl.multiple_of(local * BS, BS), BS)])
            near = jnp.concatenate(near, axis=1)
            both = jnp.concatenate(
                [jnp.concatenate([ref[row, slot] for slot in range(slots)], axis=1) for ref in (g_ref, c_ref)], axis=0
            )
            prod = lax.dot_general(both, near, (((1,), (1,)), ((), ())), preferred_element_type=F32).astype(BF16)
            prods[at:at + BS, 0:2 * width] = prod[0:BS]
            prods[at:at + BS, 2 * width:4 * width] = prod[BS:2 * BS]
            at += BS
        part = lax.dot_general(
            basis_ref[lo * BS:hi * BS, :], prods[begin:at, :], (((0,), (0,)), ((), ())), preferred_element_type=F32
        )
        total = part if total is None else total + part
    if before is not None:
        total = total + before[...]
    if len(outs) == 1:
        outs[0][...] = total
        return
    send_ref, keep_ref = outs
    states, columns = total.shape
    total = total.reshape(groups, 2, states // (2 * groups), columns)
    odd = node % 2 == 1
    keep_ref[...] = jnp.where(odd, total[:, 1], total[:, 0])
    send_ref[...] = jnp.where(odd, total[:, 0], total[:, 1]).astype(BF16)


def project(fixed, pieces, spans, groups, before=None, last=True):
    ids, g_blocks, c_blocks, basis = fixed
    rows, slots = g_blocks.shape[0], g_blocks.shape[1]
    width = pieces[0][0].shape[0]
    states = basis.shape[1]
    piece = (groups, states // (2 * groups), 4 * width)
    whole = shape((states, 4 * width), F32)
    arrays = [array for mine, other, _ in pieces for array in (mine, other)]
    more = [] if before is None else [before]
    count = sum(hi - lo for lo, hi in spans)
    return pl.pallas_call(
        functools.partial(project_kernel, spans, [parts for _, _, parts in pieces], groups, before is not None),
        out_shape=(shape(piece, BF16), shape(piece, F32)) if last else (whole,),
        in_specs=[SMEM] + [VMEM] * (3 + len(arrays) + len(more)),
        out_specs=(VMEM, VMEM) if last else (VMEM,),
        scratch_shapes=[
            pltpu.VMEM((2 * width, (rows + 2 * HB) * BS), BF16),
            pltpu.VMEM((count * BS, 4 * width), BF16),
        ],
        compiler_params=params(14),
        cost_estimate=pl.CostEstimate(flops=count, bytes_accessed=count, transcendentals=0),
    )(ids, g_blocks, c_blocks, basis, *arrays, *more)


def spread_kernel(groups, keep_a, got_a, keep_b, got_b, keep_ref, *send_refs):
    here = lax.axis_index("node") // 2
    half = keep_a.shape[2]
    for step in range(groups):
        at = here ^ step
        for lo, keep, got in ((0, keep_a, got_a), (half, keep_b, got_b)):
            value = keep[at] + got[at].astype(F32)
            if step == 0:
                keep_ref[:, lo:lo + half] = value
            else:
                send_refs[step - 1][:, lo:lo + half] = value.astype(BF16)


def spread(groups, keep_a, got_a, keep_b, got_b):
    piece = (keep_a.shape[1], 2 * keep_a.shape[2])
    return pl.pallas_call(
        functools.partial(spread_kernel, groups),
        out_shape=[shape(piece, F32)] + [shape(piece, BF16)] * (groups - 1),
        in_specs=[VMEM] * 4,
        out_specs=[VMEM] * groups,
        compiler_params=params(4),
    )(keep_a, got_a, keep_b, got_b)


def finish_kernel(keep, *refs):
    got, (out_g, out_c) = refs[:-2], refs[-2:]
    total = keep[...]
    for ref in got:
        total = total + ref[...].astype(F32)
    first = lax.axis_index("col") // 2
    quarter = total.shape[1] // 4
    for place, base in ((first, 0), (1 - first, 2 * quarter)):
        at = pl.ds(pl.multiple_of(place * quarter, quarter), quarter)
        out_g[:, at] = total[:, base:base + quarter]
        out_c[:, at] = total[:, base + quarter:base + 2 * quarter]


def finish(keep, got):
    piece = shape((keep.shape[0], keep.shape[1] // 2), F32)
    return pl.pallas_call(
        finish_kernel,
        out_shape=(piece, piece),
        in_specs=[VMEM] * (1 + len(got)),
        out_specs=(VMEM, VMEM),
        compiler_params=params(4),
    )(keep, *got)


def body(panel, basis, g_blocks, c_blocks, block_cols):
    nodes, cols = lax.axis_size("node"), lax.axis_size("col")
    rows = g_blocks.shape[0]
    groups = nodes // 2
    halo = HB * BS
    inner = rows * BS
    half = inner - halo
    ids = block_cols.T
    mine = panel.T

    def across(array):
        return lax.ppermute(array, "col", [(i, i ^ 2) for i in range(cols)])

    def cores(array):
        return lax.ppermute(array, "col", [(i, i ^ 1) for i in range(cols)])

    def up(array):
        return lax.ppermute(array, "node", [(i, i + 1) for i in range(nodes - 1)])

    def down(array):
        return lax.ppermute(array, "node", [(i + 1, i) for i in range(nodes - 1)])

    def swap(array, step):
        return lax.ppermute(array, "node", [(i, i ^ step) for i in range(nodes)])

    other = cores(mine)
    ends, first, last, front = cut(mine, half)
    far_ends, far_front = across(ends), across(front)
    other, first, last = lax.optimization_barrier((other, first, last))
    low, high = up(last), down(first)
    (basis,), (g_blocks,), (c_blocks,) = load(basis), load(g_blocks), load(c_blocks)
    far_ends, g_blocks, c_blocks, basis = lax.optimization_barrier((far_ends, g_blocks, c_blocks, basis))
    fixed = (ids, g_blocks, c_blocks, basis)
    far_low, far_high = up(far_ends[:, halo:]), down(far_ends[:, :halo])
    middle = [(mine, other, [(0, halo, inner)])]
    part = project(fixed, middle, [(HB, rows - HB)], groups, last=False)[0]
    rim = jnp.concatenate([low, high, far_low, far_high, far_ends], axis=1)
    rim_other = cores(rim)
    own_rim = [(rim, rim_other, [(0, 0, halo), (halo, halo + inner, halo)])]
    far_rim = [
        (
            rim,
            rim_other,
            [
                (2 * halo, 0, halo),
                (3 * halo, halo + inner, halo),
                (4 * halo, halo, halo),
                (5 * halo, inner, halo),
            ],
        )
    ]
    send_a, keep_a = project(fixed, middle + own_rim, [(0, HB), (rows - HB, rows)], groups, before=part)
    send_a, far_front = lax.optimization_barrier((send_a, far_front))
    got_a = swap(send_a, 1)
    far_middle = [
        (far_front, cores(far_front), [(0, 2 * halo, half - halo)]),
    ]
    send_b, keep_b = project(fixed, far_rim + far_middle, [(0, rows)], groups)
    got_b = swap(send_b, 1)
    keep, *sends = spread(groups, keep_a, got_a, keep_b, got_b)
    return finish(keep, [swap(send, 2 * step) for step, send in enumerate(sends, 1)])


def solution(mesh):
    in_specs = (
        P("node", "col"),
        P("node", "col"),
        P("node", None, None, None),
        P("node", None, None, None),
        P("node", None),
    )
    out_specs = (P(("col", "node"), None), P(("col", "node"), None))
    return jax.shard_map(body, mesh=mesh, in_specs=in_specs, out_specs=out_specs, check_vma=False)
```

time: 201 us -> 56.6 us (0.28)
  Pallas kernels: 161 us -> 16.7 us
  starting transfers between devices: 19.8 us -> 23.7 us
  waiting for transfers between devices: 16.1 us -> 13.9 us
  local copies, waits for them, and re-layouts: 3.33 us -> 1.14 us
    pallas_call x5 -> x9, Pallas kernels: 161 us -> 16.7 us  [the longest x3 9.14 us: project(): pl.pallas_call(functools.partial(project_kernel, spans, [parts for _, _,...]
    ppermute x13 -> x14, starting transfers between devices: 19.8 us -> 23.7 us  [the longest x5 8.91 us: swap(): return lax.ppermute(array, 'node', [(i, i ^ step) for i in range(nodes)])]
    ppermute x13 -> x14, waiting for transfers between devices: 16.1 us -> 13.9 us  [the longest x5 8.62 us: swap(): return lax.ppermute(array, 'node', [(i, i ^ step) for i in range(nodes)])]
  transfers between devices with their start and end apart: 13 -> 14, of which waited for: 7 -> 4; matrix products, arithmetic and copies ran while one was open for 0% -> 0% of each run, Pallas kernels for 80% -> 28%
where the time goes in v3:
time: 56.6 us; the launch traced here: 56.3 us
  starting transfers between devices  23.7 us (42%)
  Pallas kernels  16.7 us (30%)
  waiting for transfers between devices  13.9 us (25%)
  local copies, waits for them, and re-layouts  1.14 us (2%)
  between operations  0.86 us (2%)
    pallas_call x3, Pallas kernels, project(): pl.pallas_call(functools.partial(project_kernel, spans, [parts for _, _,...  9.14 us
    ppermute x5, starting transfers between devices, swap(): return lax.ppermute(array, 'node', [(i, i ^ step) for i in range(nodes)])  8.91 us
    ppermute x5, waiting for transfers between devices, swap(): return lax.ppermute(array, 'node', [(i, i ^ step) for i in range(nodes)])  8.62 us
    ppermute x2, starting transfers between devices, up(): return lax.ppermute(array, 'node', [(i, i + 1) for i in range(nodes - 1)])  8.43 us
    pallas_call x3, Pallas kernels, load(): pl.pallas_call(load_kernel, out_shape=[shape(array.shape, array.dtype) fo...  6.71 us
    ppermute x2, waiting for transfers between devices, down(): return lax.ppermute(array, 'node', [(i + 1, i) for i in range(nodes - 1)])  5.24 us
    ppermute x2, starting transfers between devices, across(): return lax.ppermute(array, 'col', [(i, i ^ 2) for i in range(cols)])  2.65 us
    ppermute x2, starting transfers between devices, down(): return lax.ppermute(array, 'node', [(i + 1, i) for i in range(nodes - 1)])  2.58 us
  transfers between devices with their start and end apart: 14, of which 4 were waited for; matrix products, arithmetic and copies ran while one was open for 0% of the time, Pallas kernels for 28%

profile of v3, /device:TPU:0, one launch (start us, length us, event | category | flops | bytes accessed | tf_op | source)
XLA Modules:
  0.0 56.3 jit_solution(1091847521827601363)
XLA Ops:
  0.6 0.5 collective-permute-start.1
  1.1 1.1 %copy-done = bf16[4864,64]{0,1:T(8,128)(2,1)S(1)} copy-done((bf16[4864,64]{0,1:T(8,128)(2,1)S(1)}, bf16[4864,64]{0,1:T(8,128)(2,1)}, u32[]{:S(2)}) %copy-start) | copy-done | bytes 622616
  2.4 2.6 %collective-permute-start = (bf16[64,1024]{1,0:T(8,128)(2,1)S(1)}, bf16[64,1024]{1,0:T(8,128)(2,1)S(1)}, u32[]{:S(2)}, u32[]{:S(2)}) collective-permute-start(bf16[64,1024]{1,0:T(8,128)(2,1)S(1)} %get-tuple-element.23), channel_id=1, source_target_pairs={{0,2},{1,3},{2,0},{3,1},{4,6},{5,7},{6,4},{7,5},{8,10},{9,11},{10,... | collective-permute-start | bytes 393224 | tf_op jit(solution)/shard_map/ppermute | solution.py:221
  5.0 2.1 %shard_map.69.refs_1_ = bf16[38,3,128,128]{3,2,1,0:T(8,128)(2,1)S(1)} custom-call(bf16[38,3,128,128]{3,2,1,0:T(8,128)(2,1)} %refs_0_.3), custom_call_target="tpu_custom_call" | custom-call | bytes 3735552 | tf_op jit(solution)/shard_map/pallas_call | solution.py:75
  7.1 2.1 %shard_map.70.refs_2_ = bf16[38,3,128,128]{3,2,1,0:T(8,128)(2,1)S(1)} custom-call(bf16[38,3,128,128]{3,2,1,0:T(8,128)(2,1)} %refs_0_.4), custom_call_target="tpu_custom_call" | custom-call | bytes 3735552 | tf_op jit(solution)/shard_map/pallas_call | solution.py:75
  9.2 2.5 %shard_map.71.refs_3_ = bf16[4864,512]{1,0:T(8,128)(2,1)S(1)} custom-call(bf16[4864,512]{1,0:T(8,128)(2,1)} %refs_0_.5), custom_call_target="tpu_custom_call" | custom-call | bytes 4980736 | tf_op jit(solution)/shard_map/pallas_call | solution.py:75
  11.8 3.9 %collective-permute-start.2 = (bf16[64,512]{1,0:T(8,128)(2,1)S(1)}, bf16[64,512]{1,0:T(8,128)(2,1)S(1)}, u32[]{:S(2)}, u32[]{:S(2)}) collective-permute-start(bf16[64,512]{1,0:T(8,128)(2,1)S(1)} %get-tuple-element.30), channel_id=1, source_target_pairs={{0,4},{4,8},{8,12},{12,16},{16,20},{20,24},{24,28},{1,5},{5,9},{9,... | collective-permute-start | bytes 196616 | tf_op jit(solution)/shard_map/ppermute | solution.py:227
  15.7 1.3 %collective-permute-start.5 = (bf16[64,512]{1,0:T(8,128)(2,1)S(1)}, bf16[64,512]{1,0:T(8,128)(2,1)S(1)}, u32[]{:S(2)}, u32[]{:S(2)}) collective-permute-start(bf16[64,512]{1,0:T(8,128)(2,1)S(1)} %get-tuple-element.44), channel_id=1, source_target_pairs={{4,0},{8,4},{12,8},{16,12},{20,16},{24,20},{28,24},{5,1},{9,5},{13... | collective-permute-start | bytes 196616 | tf_op jit(solution)/shard_map/ppermute | solution.py:230
  17.0 4.5 %collective-permute-start.4 = (bf16[64,512]{1,0:T(8,128)(2,1)S(1)}, bf16[64,512]{1,0:T(8,128)(2,1)S(1)}, u32[]{:S(2)}, u32[]{:S(2)}) collective-permute-start(bf16[64,512]{1,0:T(8,128)(2,1)S(1)} %get-tuple-element.45), channel_id=1, source_target_pairs={{0,4},{4,8},{8,12},{12,16},{16,20},{20,24},{24,28},{1,5},{5,9},{9,... | collective-permute-start | bytes 196616 | tf_op jit(solution)/shard_map/ppermute | solution.py:227
  21.6 1.3 %collective-permute-start.3 = (bf16[64,512]{1,0:T(8,128)(2,1)S(1)}, bf16[64,512]{1,0:T(8,128)(2,1)S(1)}, u32[]{:S(2)}, u32[]{:S(2)}) collective-permute-start(bf16[64,512]{1,0:T(8,128)(2,1)S(1)} %get-tuple-element.31), channel_id=1, source_target_pairs={{4,0},{8,4},{12,8},{16,12},{20,16},{24,20},{28,24},{5,1},{9,5},{13... | collective-permute-start | bytes 196616 | tf_op jit(solution)/shard_map/ppermute | solution.py:230
  22.9 5.2 %collective-permute-done.3 = bf16[64,512]{1,0:T(8,128)(2,1)S(1)} collective-permute-done((bf16[64,512]{1,0:T(8,128)(2,1)S(1)}, bf16[64,512]{1,0:T(8,128)(2,1)S(1)}, u32[]{:S(2)}, u32[]{:S(2)}) %collective-permute-start.3) | collective-permute-done | bytes 65568 | tf_op jit(solution)/shard_map/ppermute | solution.py:230
  28.3 3.4 %shard_map.72.refs_8_ = f32[512,256]{1,0:T(8,128)S(1)} custom-call(s32[3,38]{1,0:T(4,128)S(1)} %bitcast.6, bf16[38,3,128,128]{3,2,1,0:T(8,128)(2,1)S(1)} %shard_map.69.refs_1_, bf16[38,3,128,128]{3,2,1,0:T(8,128)(2,1)S(1)} %shard_map.70.refs_2_, bf16[4864,512]{1,0:T(8,128)(2,1)S(1)} %shard_map.71.refs_3_, bf16[64,4864]{1,0:T(8,128)(2,1)S(1)} %bitcast.4, ...), custom_call_target="tpu_custom_call" | custom-call | flops 30 | bytes 30 | tf_op jit(solution)/shard_map/pallas_call | solution.py:148
  31.7 1.6 %shard_map.73 = (bf16[4,64,256]{2,1,0:T(8,128)(2,1)S(1)}, f32[4,64,256]{2,1,0:T(8,128)S(1)}) custom-call(s32[3,38]{1,0:T(4,128)S(1)} %bitcast.7, bf16[38,3,128,128]{3,2,1,0:T(8,128)(2,1)S(1)} %shard_map.69.refs_1_, bf16[38,3,128,128]{3,2,1,0:T(8,128)(2,1)S(1)} %shard_map.70.refs_2_, bf16[4864,512]{1,0:T(8,128)(2,1)S(1)} %shard_map.71.refs_3_, ...), custom_call_target="tpu_custom_call" | custom-call | flops 8 | bytes 8 | tf_op jit(solution)/shard_map/pallas_call | solution.py:148
  33.4 0.5 collective-permute-start.9
  33.9 2.9 %collective-permute-start.8 = (bf16[4,64,256]{2,1,0:T(8,128)(2,1)S(1)}, bf16[4,64,256]{2,1,0:T(8,128)(2,1)S(1)}, u32[]{:S(2)}, u32[]{:S(2)}) collective-permute-start(bf16[4,64,256]{2,1,0:T(8,128)(2,1)S(1)} %get-tuple-element.36), channel_id=1, source_target_pairs={{0,4},{4,0},{8,12},{12,8},{16,20},{20,16},{24,28},{28,24},{1,5},{5... | collective-permute-start | bytes 393224 | tf_op jit(solution)/shard_map/ppermute | solution.py:233
  36.8 4.1 %shard_map.74 = (bf16[4,64,256]{2,1,0:T(8,128)(2,1)S(1)}, f32[4,64,256]{2,1,0:T(8,128)S(1)}) custom-call(s32[3,38]{1,0:T(4,128)S(1)} %bitcast.8, bf16[38,3,128,128]{3,2,1,0:T(8,128)(2,1)S(1)} %shard_map.69.refs_1_, bf16[38,3,128,128]{3,2,1,0:T(8,128)(2,1)S(1)} %shard_map.70.refs_2_, bf16[4864,512]{1,0:T(8,128)(2,1)S(1)} %shard_map.71.refs_3_, ...), custom_call_target="tpu_custom_call" | custom-call | flops 38 | bytes 38 | tf_op jit(solution)/shard_map/pallas_call | solution.py:148
  41.0 1.6 %collective-permute-start.10 = (bf16[4,64,256]{2,1,0:T(8,128)(2,1)S(1)}, bf16[4,64,256]{2,1,0:T(8,128)(2,1)S(1)}, u32[]{:S(2)}, u32[]{:S(2)}) collective-permute-start(bf16[4,64,256]{2,1,0:T(8,128)(2,1)S(1)} %get-tuple-element.39), channel_id=1, source_target_pairs={{0,4},{4,0},{8,12},{12,8},{16,20},{20,16},{24,28},{28,24},{1,5},{5... | collective-permute-start | bytes 393224 | tf_op jit(solution)/shard_map/ppermute | solution.py:233
  42.5 4.0 %collective-permute-done.10.got_b = bf16[4,64,256]{2,1,0:T(8,128)(2,1)S(1)} collective-permute-done((bf16[4,64,256]{2,1,0:T(8,128)(2,1)S(1)}, bf16[4,64,256]{2,1,0:T(8,128)(2,1)S(1)}, u32[]{:S(2)}, u32[]{:S(2)}) %collective-permute-start.10) | collective-permute-done | bytes 131104 | tf_op jit(solution)/shard_map/ppermute | solution.py:233
  46.6 1.6 %collective-permute-start.11 = (bf16[64,512]{1,0:T(8,128)(2,1)S(1)}, bf16[64,512]{1,0:T(8,128)(2,1)S(1)}, u32[]{:S(2)}, u32[]{:S(2)}) collective-permute-start(bf16[64,512]{1,0:T(8,128)(2,1)S(1)} %get-tuple-element.41), channel_id=1, source_target_pairs={{0,8},{4,12},{8,0},{12,4},{16,24},{20,28},{24,16},{28,20},{1,9},{5... | collective-permute-start | bytes 196616 | tf_op jit(solution)/shard_map/ppermute | solution.py:233
  48.2 1.1 %collective-permute-start.12 = (bf16[64,512]{1,0:T(8,128)(2,1)S(1)}, bf16[64,512]{1,0:T(8,128)(2,1)S(1)}, u32[]{:S(2)}, u32[]{:S(2)}) collective-permute-start(bf16[64,512]{1,0:T(8,128)(2,1)S(1)} %get-tuple-element.42), channel_id=1, source_target_pairs={{0,16},{4,20},{8,24},{12,28},{16,0},{20,4},{24,8},{28,12},{1,17},{... | collective-permute-start | bytes 196616 | tf_op jit(solution)/shard_map/ppermute | solution.py:233
  49.3 1.7 %collective-permute-start.13 = (bf16[64,512]{1,0:T(8,128)(2,1)S(1)}, bf16[64,512]{1,0:T(8,128)(2,1)S(1)}, u32[]{:S(2)}, u32[]{:S(2)}) collective-permute-start(bf16[64,512]{1,0:T(8,128)(2,1)S(1)} %get-tuple-element.43), channel_id=1, source_target_pairs={{0,24},{4,28},{8,16},{12,20},{16,8},{20,12},{24,0},{28,4},{1,25},{... | collective-permute-start | bytes 196616 | tf_op jit(solution)/shard_map/ppermute | solution.py:233
  51.0 0.5 collective-permute-done.11.refs_0_
  51.6 4.1 %collective-permute-done.12.refs_1_ = bf16[64,512]{1,0:T(8,128)(2,1)S(1)} collective-permute-done((bf16[64,512]{1,0:T(8,128)(2,1)S(1)}, bf16[64,512]{1,0:T(8,128)(2,1)S(1)}, u32[]{:S(2)}, u32[]{:S(2)}) %collective-permute-start.12) | collective-permute-done | bytes 65568 | tf_op jit(solution)/shard_map/ppermute | solution.py:233
  55.6 0.7 %shard_map.76 = (f32[64,256]{1,0:T(8,128)}, f32[64,256]{1,0:T(8,128)}) custom-call(f32[64,512]{1,0:T(8,128)S(1)} %get-tuple-element.40.keep, bf16[64,512]{1,0:T(8,128)(2,1)S(1)} %collective-permute-done.11.refs_0_, bf16[64,512]{1,0:T(8,128)(2,1)S(1)} %collective-permute-done.12.refs_1_, bf16[64,512]{1,0:T(8,128)(2,1)S(1)} %collective-permute-done.13.refs_2_), custom_call_target="tpu_custom_call" | custom-call | tf_op jit(solution)/shard_map/pallas_call | solution.py:201
  (25 shorter events, 0.4 us)
Async XLA Ops:
  0.6 11.2 %collective-permute-start.1 = (bf16[64,4864]{1,0:T(8,128)(2,1)}, bf16[64,4864]{1,0:T(8,128)(2,1)S(1)}, u32[]{:S(2)}, u32[]{:S(2)}) collective-permute-start(bf16[64,4864]{1,0:T(8,128)(2,1)} %bitcast.2), channel_id=1, source_target_pairs={{0,1},{1,0},{2,3},{3,2},{4,5},{5,4},{6,7},{7,6},{8,9},{9,8},{10,11... | collective-permute-start | bytes 1867784 | tf_op jit(solution)/shard_map/ppermute | solution.py:224
  1.1 1.1 %copy-start = (bf16[4864,64]{0,1:T(8,128)(2,1)S(1)}, bf16[4864,64]{0,1:T(8,128)(2,1)}, u32[]{:S(2)}) copy-start(bf16[4864,64]{0,1:T(8,128)(2,1)} %param.5) | copy-start | bytes 1867780
  2.4 9.4 %collective-permute-start = (bf16[64,1024]{1,0:T(8,128)(2,1)S(1)}, bf16[64,1024]{1,0:T(8,128)(2,1)S(1)}, u32[]{:S(2)}, u32[]{:S(2)}) collective-permute-start(bf16[64,1024]{1,0:T(8,128)(2,1)S(1)} %get-tuple-element.23), channel_id=1, source_target_pairs={{0,2},{1,3},{2,0},{3,1},{4,6},{5,7},{6,4},{7,5},{8,10},{9,11},{10,... | collective-permute-start | bytes 393224 | tf_op jit(solution)/shard_map/ppermute | solution.py:221
  4.9 28.4 %collective-permute-start.7 = (bf16[64,3840]{1,0:T(8,128)(2,1)S(1)}, bf16[64,3840]{1,0:T(8,128)(2,1)S(1)}, u32[]{:S(2)}, u32[]{:S(2)}) collective-permute-start(bf16[64,3840]{1,0:T(8,128)(2,1)S(1)} %get-tuple-element.35), channel_id=1, source_target_pairs={{0,2},{1,3},{2,0},{3,1},{4,6},{5,7},{6,4},{7,5},{8,10},{9,11},{10,... | collective-permute-start | bytes 1474568 | tf_op jit(solution)/shard_map/ppermute | solution.py:221
  9.2 19.1 %copy-start.1 = (bf16[4864,64]{0,1:T(8,128)(2,1)S(1)}, bf16[4864,64]{0,1:T(8,128)(2,1)}, u32[]{:S(2)}) copy-start(bf16[4864,64]{0,1:T(8,128)(2,1)} %param.5) | copy-start | bytes 1867780
  9.2 19.1 %copy-start.2 = (s32[38,3]{0,1:T(4,128)S(1)}, s32[38,3]{0,1:T(4,128)}, u32[]{:S(2)}) copy-start(s32[38,3]{0,1:T(4,128)} %param.9) | copy-start | bytes 1372
  11.8 11.1 %collective-permute-start.2 = (bf16[64,512]{1,0:T(8,128)(2,1)S(1)}, bf16[64,512]{1,0:T(8,128)(2,1)S(1)}, u32[]{:S(2)}, u32[]{:S(2)}) collective-permute-start(bf16[64,512]{1,0:T(8,128)(2,1)S(1)} %get-tuple-element.30), channel_id=1, source_target_pairs={{0,4},{4,8},{8,12},{12,16},{16,20},{20,24},{24,28},{1,5},{5,9},{9,... | collective-permute-start | bytes 196616 | tf_op jit(solution)/shard_map/ppermute | solution.py:227
  15.7 12.5 %collective-permute-start.5 = (bf16[64,512]{1,0:T(8,128)(2,1)S(1)}, bf16[64,512]{1,0:T(8,128)(2,1)S(1)}, u32[]{:S(2)}, u32[]{:S(2)}) collective-permute-start(bf16[64,512]{1,0:T(8,128)(2,1)S(1)} %get-tuple-element.44), channel_id=1, source_target_pairs={{4,0},{8,4},{12,8},{16,12},{20,16},{24,20},{28,24},{5,1},{9,5},{13... | collective-permute-start | bytes 196616 | tf_op jit(solution)/shard_map/ppermute | solution.py:230
  17.0 11.1 %collective-permute-start.4 = (bf16[64,512]{1,0:T(8,128)(2,1)S(1)}, bf16[64,512]{1,0:T(8,128)(2,1)S(1)}, u32[]{:S(2)}, u32[]{:S(2)}) collective-permute-start(bf16[64,512]{1,0:T(8,128)(2,1)S(1)} %get-tuple-element.45), channel_id=1, source_target_pairs={{0,4},{4,8},{8,12},{12,16},{16,20},{20,24},{24,28},{1,5},{5,9},{9,... | collective-permute-start | bytes 196616 | tf_op jit(solution)/shard_map/ppermute | solution.py:227
  21.6 6.6 %collective-permute-start.3 = (bf16[64,512]{1,0:T(8,128)(2,1)S(1)}, bf16[64,512]{1,0:T(8,128)(2,1)S(1)}, u32[]{:S(2)}, u32[]{:S(2)}) collective-permute-start(bf16[64,512]{1,0:T(8,128)(2,1)S(1)} %get-tuple-element.31), channel_id=1, source_target_pairs={{4,0},{8,4},{12,8},{16,12},{20,16},{24,20},{28,24},{5,1},{9,5},{13... | collective-permute-start | bytes 196616 | tf_op jit(solution)/shard_map/ppermute | solution.py:230
  28.2 3.5 %collective-permute-start.6 = (bf16[64,3072]{1,0:T(8,128)(2,1)S(1)}, bf16[64,3072]{1,0:T(8,128)(2,1)S(1)}, u32[]{:S(2)}, u32[]{:S(2)}) collective-permute-start(bf16[64,3072]{1,0:T(8,128)(2,1)S(1)} %constant_dynamic-update-slice_fusion.refs_6_.refs_4_), channel_id=1, source_target_pairs={{0,1},{1,0},{2,3},{3,2},{4,5},{5,4},{6,7},{7,6},{8,9},{9,8},{10,11... | collective-permute-start | bytes 1179656 | tf_op jit(solution)/shard_map/ppermute | solution.py:224
  33.4 3.5 %collective-permute-start.9 = (bf16[64,3840]{1,0:T(8,128)(2,1)S(1)}, bf16[64,3840]{1,0:T(8,128)(2,1)S(1)}, u32[]{:S(2)}, u32[]{:S(2)}) collective-permute-start(bf16[64,3840]{1,0:T(8,128)(2,1)S(1)} %collective-permute-done.7.refs_6_), channel_id=1, source_target_pairs={{0,1},{1,0},{2,3},{3,2},{4,5},{5,4},{6,7},{7,6},{8,9},{9,8},{10,11... | collective-permute-start | bytes 1474568 | tf_op jit(solution)/shard_map/ppermute | solution.py:224
  33.9 8.6 %collective-permute-start.8 = (bf16[4,64,256]{2,1,0:T(8,128)(2,1)S(1)}, bf16[4,64,256]{2,1,0:T(8,128)(2,1)S(1)}, u32[]{:S(2)}, u32[]{:S(2)}) collective-permute-start(bf16[4,64,256]{2,1,0:T(8,128)(2,1)S(1)} %get-tuple-element.36), channel_id=1, source_target_pairs={{0,4},{4,0},{8,12},{12,8},{16,20},{20,16},{24,28},{28,24},{1,5},{5... | collective-permute-start | bytes 393224 | tf_op jit(solution)/shard_map/ppermute | solution.py:233
  41.0 5.6 %collective-permute-start.10 = (bf16[4,64,256]{2,1,0:T(8,128)(2,1)S(1)}, bf16[4,64,256]{2,1,0:T(8,128)(2,1)S(1)}, u32[]{:S(2)}, u32[]{:S(2)}) collective-permute-start(bf16[4,64,256]{2,1,0:T(8,128)(2,1)S(1)} %get-tuple-element.39), channel_id=1, source_target_pairs={{0,4},{4,0},{8,12},{12,8},{16,20},{20,16},{24,28},{28,24},{1,5},{5... | collective-permute-start | bytes 393224 | tf_op jit(solution)/shard_map/ppermute | solution.py:233
  46.6 5.0 %collective-permute-start.11 = (bf16[64,512]{1,0:T(8,128)(2,1)S(1)}, bf16[64,512]{1,0:T(8,128)(2,1)S(1)}, u32[]{:S(2)}, u32[]{:S(2)}) collective-permute-start(bf16[64,512]{1,0:T(8,128)(2,1)S(1)} %get-tuple-element.41), channel_id=1, source_target_pairs={{0,8},{4,12},{8,0},{12,4},{16,24},{20,28},{24,16},{28,20},{1,9},{5... | collective-permute-start | bytes 196616 | tf_op jit(solution)/shard_map/ppermute | solution.py:233
  48.2 7.4 %collective-permute-start.12 = (bf16[64,512]{1,0:T(8,128)(2,1)S(1)}, bf16[64,512]{1,0:T(8,128)(2,1)S(1)}, u32[]{:S(2)}, u32[]{:S(2)}) collective-permute-start(bf16[64,512]{1,0:T(8,128)(2,1)S(1)} %get-tuple-element.42), channel_id=1, source_target_pairs={{0,16},{4,20},{8,24},{12,28},{16,0},{20,4},{24,8},{28,12},{1,17},{... | collective-permute-start | bytes 196616 | tf_op jit(solution)/shard_map/ppermute | solution.py:233
  49.3 6.3 %collective-permute-start.13 = (bf16[64,512]{1,0:T(8,128)(2,1)S(1)}, bf16[64,512]{1,0:T(8,128)(2,1)S(1)}, u32[]{:S(2)}, u32[]{:S(2)}) collective-permute-start(bf16[64,512]{1,0:T(8,128)(2,1)S(1)} %get-tuple-element.43), channel_id=1, source_target_pairs={{0,24},{4,28},{8,16},{12,20},{16,8},{20,12},{24,0},{28,4},{1,25},{... | collective-permute-start | bytes 196616 | tf_op jit(solution)/shard_map/ppermute | solution.py:233

commit v4 on v3

v4 whole, which is shorter than its diff:
```python
import functools

import jax
import jax.numpy as jnp
from jax import lax
from jax.experimental import pallas as pl
from jax.experimental.pallas import tpu as pltpu
from jax.sharding import PartitionSpec as P

BS = 128
HB = 4
ROWS_OF_CORE = 64
FETCHES = 4
MIB = 1024 * 1024
F32 = jnp.float32
BF16 = jnp.bfloat16
VMEM = pl.BlockSpec(memory_space=pltpu.VMEM)
SMEM = pl.BlockSpec(memory_space=pltpu.SMEM)
HBM = pl.BlockSpec(memory_space=pl.ANY)


def params(mib):
    return pltpu.CompilerParams(vmem_limit_bytes=mib * MIB)


def shape(dims, kind):
    return jax.ShapeDtypeStruct(dims, kind)


def cut_kernel(panel, ends, middle, sems):
    inner = panel.shape[1]
    halo = HB * BS
    odd = lax.axis_index("node") % 2
    to_pair = pl.multiple_of((1 - odd) * (inner - halo), BS)
    to_next = pl.multiple_of(odd * (inner - halo), BS)
    copies = [
        (panel.at[:, pl.ds(to_pair, halo)], ends.at[:, 0:halo]),
        (panel.at[:, pl.ds(to_next, halo)], ends.at[:, halo:2 * halo]),
        (panel.at[:, halo:inner - halo], middle),
    ]
    copies = [pltpu.make_async_copy(*pair, sems.at[i]) for i, pair in enumerate(copies)]
    for copy in copies:
        copy.start()
    for copy in copies:
        copy.wait()


def cut(panel):
    width, inner = panel.shape
    halo = HB * BS
    return pl.pallas_call(
        cut_kernel,
        out_shape=[shape((width, w), BF16) for w in (2 * halo, inner - 2 * halo)],
        in_specs=[HBM],
        out_specs=[VMEM] * 2,
        scratch_shapes=[pltpu.SemaphoreType.DMA((3,))],
        compiler_params=params(58),
    )(panel)


def project_kernel(spans, places, groups, more, fetch, *refs):
    ids_ref, g_ref, c_ref, basis_ref = refs[:4]
    pieces = refs[4:4 + 2 * len(places)]
    rest = list(refs[4 + 2 * len(places):])
    before = rest.pop(0) if more else None
    rows, slots = g_ref.shape[0], g_ref.shape[1]
    width = ROWS_OF_CORE
    node = lax.axis_index("node")
    core = lax.axis_index("col") % 2
    odd = node % 2
    arrivals = {}
    sems = rest.pop()
    basis_new = rest.pop()
    if fetch:
        g_new, c_new = rest[1:3]
        del rest[1:3]
        edges = [rows * i // FETCHES for i in range(FETCHES + 1)]
        for step, (lo, hi) in enumerate(zip(edges[:-1], edges[1:])):
            arrivals[lo] = [
                pltpu.make_async_copy(old.at[lo:hi], new.at[lo:hi], sems.at[step, which])
                for which, (old, new) in enumerate(((g_ref, g_new), (c_ref, c_new)))
            ]
        for batch in arrivals.values():
            for copy in batch:
                copy.start()
        g_ref, c_ref = g_new, c_new
    basis_copies = []
    at = 0
    for step, (lo, hi) in enumerate(spans):
        target = basis_new.at[at:at + (hi - lo) * BS]
        basis_copies.append(pltpu.make_async_copy(basis_ref.at[lo * BS:hi * BS], target, sems.at[step, 2]))
        basis_copies[-1].start()
        at += (hi - lo) * BS
    *outs, ext, prods = rest

    for which, (base, parts) in enumerate(places):
        for owner, ref in ((core, pieces[2 * which]), (1 - core, pieces[2 * which + 1])):
            at = pl.ds(pl.multiple_of(owner * width, width), width)
            for source, even_target, odd_target, count in parts:
                target = even_target
                if odd_target != even_target:
                    target = pl.multiple_of(even_target + odd * (odd_target - even_target), BS)
                ext[at, pl.ds(target, count)] = ref[base:base + width, source:source + count]

    offset = node * rows - HB
    at = 0
    total = None
    for step, (lo, hi) in enumerate(spans):
        begin = at
        for row in range(lo, hi):
            for first in [first for first in arrivals if first <= row]:
                for copy in arrivals.pop(first):
                    copy.wait()
            near = []
            for slot in range(slots):
                local = jnp.clip(ids_ref[slot, row] - offset, 0, rows + 2 * HB - 1)
                near.append(ext[:, pl.ds(pl.multiple_of(local * BS, BS), BS)])
            near = jnp.concatenate(near, axis=1)
            both = jnp.concatenate(
                [jnp.concatenate([ref[row, slot] for slot in range(slots)], axis=1) for ref in (g_ref, c_ref)], axis=0
            )
            prod = lax.dot_general(both, near, (((1,), (1,)), ((), ())), preferred_element_type=F32).astype(BF16)
            prods[at:at + BS, 0:2 * width] = prod[0:BS]
            prods[at:at + BS, 2 * width:4 * width] = prod[BS:2 * BS]
            at += BS
        basis_copies[step].wait()
        part = lax.dot_general(
            basis_new[begin:at, :], prods[begin:at, :], (((0,), (0,)), ((), ())), preferred_element_type=F32
        )
        total = part if total is None else total + part
    for batch in arrivals.values():
        for copy in batch:
            copy.wait()
    if before is not None:
        total = total + before[...]
    if len(outs) == 1:
        outs[0][...] = total
        return
    send_ref, keep_ref = outs
    states, columns = total.shape
    total = total.reshape(groups, 2, states // (2 * groups), columns)
    keep_ref[...] = jnp.where(odd == 1, total[:, 1], total[:, 0])
    send_ref[...] = jnp.where(odd == 1, total[:, 0], total[:, 1]).astype(BF16)


def project(fixed, pieces, spans, groups, before=None, first=False):
    ids, g_blocks, c_blocks, basis = fixed
    rows, slots = g_blocks.shape[0], g_blocks.shape[1]
    width = ROWS_OF_CORE
    states = basis.shape[1]
    piece = (groups, states // (2 * groups), 4 * width)
    arrays = [array for mine, other, _, _ in pieces for array in (mine, other)]
    more = [] if before is None else [before]
    count = sum(hi - lo for lo, hi in spans)
    scratch = [
        pltpu.VMEM((2 * width, (rows + 2 * HB) * BS), BF16),
        pltpu.VMEM((count * BS, 4 * width), BF16),
        pltpu.VMEM((count * BS, states), BF16),
        pltpu.SemaphoreType.DMA((FETCHES, 3)),
    ]
    if first:
        outs = [shape((states, 4 * width), F32), shape(g_blocks.shape, BF16), shape(c_blocks.shape, BF16)]
    else:
        outs = [shape(piece, BF16), shape(piece, F32)]
    places = [(base, parts) for _, _, base, parts in pieces]
    return pl.pallas_call(
        functools.partial(project_kernel, spans, places, groups, before is not None, first),
        out_shape=outs,
        in_specs=[SMEM] + [HBM if first else VMEM] * 2 + [HBM] + [VMEM] * (len(arrays) + len(more)),
        out_specs=[VMEM] * len(outs),
        scratch_shapes=scratch,
        compiler_params=params(42),
        cost_estimate=pl.CostEstimate(flops=count, bytes_accessed=count, transcendentals=0),
    )(ids, g_blocks, c_blocks, basis, *arrays, *more)


def spread_kernel(groups, keep_a, got_a, keep_b, got_b, keep_ref, *send_refs):
    here = lax.axis_index("node") // 2
    half = keep_a.shape[2]
    for step in range(groups):
        at = here ^ step
        for lo, keep, got in ((0, keep_a, got_a), (half, keep_b, got_b)):
            value = keep[at] + got[at].astype(F32)
            if step == 0:
                keep_ref[:, lo:lo + half] = value
            else:
                send_refs[step - 1][:, lo:lo + half] = value.astype(BF16)


def spread(groups, keep_a, got_a, keep_b, got_b):
    piece = (keep_a.shape[1], 2 * keep_a.shape[2])
    return pl.pallas_call(
        functools.partial(spread_kernel, groups),
        out_shape=[shape(piece, F32)] + [shape(piece, BF16)] * (groups - 1),
        in_specs=[VMEM] * 4,
        out_specs=[VMEM] * groups,
        compiler_params=params(4),
    )(keep_a, got_a, keep_b, got_b)


def finish_kernel(keep, *refs):
    got, (out_g, out_c) = refs[:-2], refs[-2:]
    total = keep[...]
    for ref in got:
        total = total + ref[...].astype(F32)
    first = lax.axis_index("col") // 2
    quarter = total.shape[1] // 4
    for place, base in ((first, 0), (1 - first, 2 * quarter)):
        at = pl.ds(pl.multiple_of(place * quarter, quarter), quarter)
        out_g[:, at] = total[:, base:base + quarter]
        out_c[:, at] = total[:, base + quarter:base + 2 * quarter]


def finish(keep, got):
    piece = shape((keep.shape[0], keep.shape[1] // 2), F32)
    return pl.pallas_call(
        finish_kernel,
        out_shape=(piece, piece),
        in_specs=[VMEM] * (1 + len(got)),
        out_specs=(VMEM, VMEM),
        compiler_params=params(4),
    )(keep, *got)


def body(panel, basis, g_blocks, c_blocks, block_cols):
    nodes, cols = lax.axis_size("node"), lax.axis_size("col")
    rows = g_blocks.shape[0]
    groups = nodes // 2
    halo = HB * BS
    inner = rows * BS
    ids = block_cols.T
    mine = panel.T

    def across(array):
        return lax.ppermute(array, "col", [(i, i ^ 2) for i in range(cols)])

    def cores(array):
        return lax.ppermute(array, "col", [(i, i ^ 1) for i in range(cols)])

    def swap(array, step):
        return lax.ppermute(array, "node", [(i, i ^ step) for i in range(nodes)])

    def swap_next(array):
        pairs = [(i, i + 1) for i in range(1, nodes - 1, 2)]
        return lax.ppermute(array, "node", pairs + [(j, i) for i, j in pairs])

    other = cores(mine)
    ends, middle = cut(mine)
    far_ends, far_middle = across(ends), across(middle)
    all_ends = jnp.concatenate([ends, far_ends], axis=0)
    rim = jnp.concatenate([swap(all_ends[:, :halo], 1), swap_next(all_ends[:, halo:])], axis=1)
    own = [(mine, other, 0, [(0, halo, halo, inner)])]
    part, g_blocks, c_blocks = project(
        (ids, g_blocks, c_blocks, basis), own, [(HB, rows - HB)], groups, first=True
    )
    part, far_middle = lax.optimization_barrier((part, far_middle))
    fixed = (ids, g_blocks, c_blocks, basis)
    rim_other = cores(rim)
    rim_parts = [(0, halo + inner, 0, halo), (halo, 0, halo + inner, halo)]
    send_a, keep_a = project(
        fixed, own + [(rim, rim_other, 0, rim_parts)], [(0, HB), (rows - HB, rows)], groups, before=part
    )
    got_a = swap(send_a, 1)
    far = [
        (rim, rim_other, ROWS_OF_CORE, rim_parts),
        (far_ends, cores(far_ends), 0, [(0, inner, halo, halo), (halo, halo, inner, halo)]),
        (far_middle, cores(far_middle), 0, [(0, 2 * halo, 2 * halo, inner - 2 * halo)]),
    ]
    send_b, keep_b = project(fixed, far, [(0, rows)], groups)
    got_b = swap(send_b, 1)
    keep, *sends = spread(groups, keep_a, got_a, keep_b, got_b)
    return finish(keep, [swap(send, 2 * step) for step, send in enumerate(sends, 1)])


def solution(mesh):
    in_specs = (
        P("node", "col"),
        P("node", "col"),
        P("node", None, None, None),
        P("node", None, None, None),
        P("node", None),
    )
    out_specs = (P(("col", "node"), None), P(("col", "node"), None))
    return jax.shard_map(body, mesh=mesh, in_specs=in_specs, out_specs=out_specs, check_vma=False)
```

time: 56.6 us -> 52.6 us (0.929)
  starting transfers between devices: 23.7 us -> 15.5 us
  Pallas kernels: 16.7 us -> 18.6 us
  local copies, waits for them, and re-layouts: 1.14 us -> 2.72 us
  waiting for transfers between devices: 13.9 us -> 14.7 us
    ppermute x4 -> x1, starting transfers between devices: 11 us -> 0.66 us  [swap_next(): return lax.ppermute(array, 'node', pairs + [(j, i) for i, j in pairs])]
    ppermute x4 -> x1, waiting for transfers between devices: 5.25 us -> 0.01 us  [swap_next(): return lax.ppermute(array, 'node', pairs + [(j, i) for i, j in pairs])]
    ppermute x2, waiting for transfers between devices: 0.01 us -> 3.57 us  [across(): return lax.ppermute(array, 'col', [(i, i ^ 2) for i in range(cols)])]
    ppermute x5 -> x6, starting transfers between devices: 8.91 us -> 10.9 us  [swap(): return lax.ppermute(array, 'node', [(i, i ^ step) for i in range(nodes)])]
    pallas_call x7 -> x4, Pallas kernels: 16 us -> 17.9 us  [the longest x3 16 us: project(): pl.pallas_call(functools.partial(project_kernel, spans, places, groups, b...]
    unnamed x10 -> x6, local copies, waits for them, and re-layouts: 1.11 us -> 2.68 us
    ppermute x3 -> x4, waiting for transfers between devices: 0.01 us -> 1.54 us  [cores(): return lax.ppermute(array, 'col', [(i, i ^ 1) for i in range(cols)])]
    ppermute x5 -> x6, waiting for transfers between devices: 8.62 us -> 9.63 us  [swap(): return lax.ppermute(array, 'node', [(i, i ^ step) for i in range(nodes)])]
  transfers between devices with their start and end apart: 14 -> 13, of which waited for: 4 -> 6; matrix products, arithmetic and copies ran while one was open for 0% -> 2% of each run, Pallas kernels for 28% -> 34%
where the time goes in v4:
time: 52.6 us; the launch traced here: 52.3 us
  Pallas kernels  18.6 us (35%)
  starting transfers between devices  15.5 us (29%)
  waiting for transfers between devices  14.7 us (28%)
  local copies, waits for them, and re-layouts  2.72 us (5%)
  between operations  0.76 us (1%)
    pallas_call x3, Pallas kernels, project(): pl.pallas_call(functools.partial(project_kernel, spans, places, groups, b...  16 us
    ppermute x6, starting transfers between devices, swap(): return lax.ppermute(array, 'node', [(i, i ^ step) for i in range(nodes)])  10.9 us
    ppermute x6, waiting for transfers between devices, swap(): return lax.ppermute(array, 'node', [(i, i ^ step) for i in range(nodes)])  9.63 us
    ppermute x2, waiting for transfers between devices, across(): return lax.ppermute(array, 'col', [(i, i ^ 2) for i in range(cols)])  3.57 us
    unnamed x6, local copies, waits for them, and re-layouts  2.68 us
    ppermute x2, starting transfers between devices, across(): return lax.ppermute(array, 'col', [(i, i ^ 2) for i in range(cols)])  2.66 us
    pallas_call x1, Pallas kernels, cut(): pl.pallas_call(cut_kernel, out_shape=[shape((width, w), BF16) for w in (2...  1.96 us
    ppermute x4, waiting for transfers between devices, cores(): return lax.ppermute(array, 'col', [(i, i ^ 1) for i in range(cols)])  1.54 us
  transfers between devices with their start and end apart: 13, of which 6 were waited for; matrix products, arithmetic and copies ran while one was open for 2% of the time, Pallas kernels for 34%

profile of v4, /device:TPU:0, one launch (start us, length us, event | category | flops | bytes accessed | tf_op | source)
XLA Modules:
  0.0 52.3 jit_solution(9593570696446562463)
XLA Ops:
  0.6 0.5 collective-permute-start
  1.1 2.0 %shard_map.69 = (bf16[64,1024]{1,0:T(8,128)(2,1)}, bf16[64,3840]{1,0:T(8,128)(2,1)}) custom-call(bf16[64,4864]{1,0:T(8,128)(2,1)} %bitcast.3), custom_call_target="tpu_custom_call" | custom-call | tf_op jit(solution)/shard_map/pallas_call | solution.py:51
  3.1 2.6 %collective-permute-start.1 = (bf16[64,1024]{1,0:T(8,128)(2,1)}, bf16[64,1024]{1,0:T(8,128)(2,1)S(1)}, u32[]{:S(2)}, u32[]{:S(2)}) collective-permute-start(bf16[64,1024]{1,0:T(8,128)(2,1)} %get-tuple-element.19), channel_id=1, source_target_pairs={{0,2},{1,3},{2,0},{3,1},{4,6},{5,7},{6,4},{7,5},{8,10},{9,11},{10,... | collective-permute-start | bytes 393224 | tf_op jit(solution)/shard_map/ppermute | solution.py:235
  5.8 0.9 %constant_dynamic-update-slice_fusion.1 = bf16[128,1024]{1,0:T(8,128)(2,1)S(1)} fusion(bf16[64,1024]{1,0:T(8,128)(2,1)} %get-tuple-element.19), kind=kLoop, calls=%fused_computation.1 | loop fusion | bytes 262144
  6.7 3.6 %collective-permute-done.1.refs_6_ = bf16[64,1024]{1,0:T(8,128)(2,1)S(1)} collective-permute-done((bf16[64,1024]{1,0:T(8,128)(2,1)}, bf16[64,1024]{1,0:T(8,128)(2,1)S(1)}, u32[]{:S(2)}, u32[]{:S(2)}) %collective-permute-start.1) | collective-permute-done | bytes 131104 | tf_op jit(solution)/shard_map/ppermute | solution.py:235
  10.3 2.0 %collective-permute-start.2 = (bf16[128,512]{1,0:T(8,128)(2,1)S(1)}, bf16[128,512]{1,0:T(8,128)(2,1)S(1)}, u32[]{:S(2)}, u32[]{:S(2)}) collective-permute-start(bf16[128,512]{1,0:T(8,128)(2,1)S(1)} %get-tuple-element.33), channel_id=1, source_target_pairs={{0,4},{4,0},{8,12},{12,8},{16,20},{20,16},{24,28},{28,24},{1,5},{5... | collective-permute-start | bytes 393224 | tf_op jit(solution)/shard_map/ppermute | solution.py:241
  12.3 0.7 %collective-permute-start.3 = (bf16[128,512]{1,0:T(8,128)(2,1)S(1)}, bf16[128,512]{1,0:T(8,128)(2,1)S(1)}, u32[]{:S(2)}, u32[]{:S(2)}) collective-permute-start(bf16[128,512]{1,0:T(8,128)(2,1)S(1)} %get-tuple-element.32), channel_id=1, source_target_pairs={{4,8},{12,16},{20,24},{8,4},{16,12},{24,20},{5,9},{13,17},{21,25},... | collective-permute-start | bytes 393224 | tf_op jit(solution)/shard_map/ppermute | solution.py:245
  13.0 1.1 %copy-done = bf16[4864,64]{0,1:T(8,128)(2,1)S(1)} copy-done((bf16[4864,64]{0,1:T(8,128)(2,1)S(1)}, bf16[4864,64]{0,1:T(8,128)(2,1)}, u32[]{:S(2)}) %copy-start) | copy-done | bytes 622616
  14.1 0.7 %copy-done.1 = s32[38,3]{0,1:T(4,128)S(1)} copy-done((s32[38,3]{0,1:T(4,128)S(1)}, s32[38,3]{0,1:T(4,128)}, u32[]{:S(2)}) %copy-start.1) | copy-done | bytes 480
  14.8 6.3 %shard_map.68 = (f32[512,256]{1,0:T(8,128)S(1)}, bf16[38,3,128,128]{3,2,1,0:T(8,128)(2,1)S(1)}, bf16[38,3,128,128]{3,2,1,0:T(8,128)(2,1)S(1)}) custom-call(s32[3,38]{1,0:T(4,128)S(1)} %bitcast.6, bf16[38,3,128,128]{3,2,1,0:T(8,128)(2,1)} %refs_1_.1, bf16[38,3,128,128]{3,2,1,0:T(8,128)(2,1)} %refs_2_.1, bf16[4864,512]{1,0:T(8,128)(2,1)} %refs_3_.5, ...), custom_call_target="tpu_custom_call" | custom-call | flops 30 | bytes 30 | tf_op jit(solution)/shard_map/pallas_call | solution.py:166
  21.2 0.6 %collective-permute-start.4 = (bf16[128,1024]{1,0:T(8,128)(2,1)S(1)}, bf16[128,1024]{1,0:T(8,128)(2,1)S(1)}, u32[]{:S(2)}, u32[]{:S(2)}) collective-permute-start(bf16[128,1024]{1,0:T(8,128)(2,1)S(1)} %constant_dynamic-update-slice_fusion.2.refs_6_.refs_4_), channel_id=1, source_target_pairs={{0,1},{1,0},{2,3},{3,2},{4,5},{5,4},{6,7},{7,6},{8,9},{9,8},{10,11... | collective-permute-start | bytes 786440 | tf_op jit(solution)/shard_map/ppermute | solution.py:238
  21.8 1.5 %collective-permute-done.4.refs_7_.refs_5_ = bf16[128,1024]{1,0:T(8,128)(2,1)S(1)} collective-permute-done((bf16[128,1024]{1,0:T(8,128)(2,1)S(1)}, bf16[128,1024]{1,0:T(8,128)(2,1)S(1)}, u32[]{:S(2)}, u32[]{:S(2)}) %collective-permute-start.4) | collective-permute-done | bytes 262176 | tf_op jit(solution)/shard_map/ppermute | solution.py:238
  23.4 2.8 %shard_map.70 = (bf16[4,64,256]{2,1,0:T(8,128)(2,1)S(1)}, f32[4,64,256]{2,1,0:T(8,128)S(1)}) custom-call(s32[3,38]{1,0:T(4,128)S(1)} %bitcast.7, bf16[38,3,128,128]{3,2,1,0:T(8,128)(2,1)S(1)} %get-tuple-element.17.refs_1_, bf16[38,3,128,128]{3,2,1,0:T(8,128)(2,1)S(1)} %get-tuple-element.18.refs_2_, bf16[4864,512]{1,0:T(8,128)(2,1)} %refs_3_.5, ...), custom_call_target="tpu_custom_call" | custom-call | flops 8 | bytes 8 | tf_op jit(solution)/shard_map/pallas_call | solution.py:166
  26.2 4.3 %collective-permute-start.6 = (bf16[4,64,256]{2,1,0:T(8,128)(2,1)S(1)}, bf16[4,64,256]{2,1,0:T(8,128)(2,1)S(1)}, u32[]{:S(2)}, u32[]{:S(2)}) collective-permute-start(bf16[4,64,256]{2,1,0:T(8,128)(2,1)S(1)} %get-tuple-element.24), channel_id=1, source_target_pairs={{0,4},{4,0},{8,12},{12,8},{16,20},{20,16},{24,28},{28,24},{1,5},{5... | collective-permute-start | bytes 393224 | tf_op jit(solution)/shard_map/ppermute | solution.py:241
  30.6 6.8 %shard_map.71 = (bf16[4,64,256]{2,1,0:T(8,128)(2,1)S(1)}, f32[4,64,256]{2,1,0:T(8,128)S(1)}) custom-call(s32[3,38]{1,0:T(4,128)S(1)} %bitcast.8, bf16[38,3,128,128]{3,2,1,0:T(8,128)(2,1)S(1)} %get-tuple-element.17.refs_1_, bf16[38,3,128,128]{3,2,1,0:T(8,128)(2,1)S(1)} %get-tuple-element.18.refs_2_, bf16[4864,512]{1,0:T(8,128)(2,1)} %refs_3_.5, ...), custom_call_target="tpu_custom_call" | custom-call | flops 38 | bytes 38 | tf_op jit(solution)/shard_map/pallas_call | solution.py:166
  37.4 0.1 collective-permute-start.9
  37.5 5.2 %collective-permute-done.9.got_b = bf16[4,64,256]{2,1,0:T(8,128)(2,1)S(1)} collective-permute-done((bf16[4,64,256]{2,1,0:T(8,128)(2,1)S(1)}, bf16[4,64,256]{2,1,0:T(8,128)(2,1)S(1)}, u32[]{:S(2)}, u32[]{:S(2)}) %collective-permute-start.9) | collective-permute-done | bytes 131104 | tf_op jit(solution)/shard_map/ppermute | solution.py:241
  42.8 1.7 %collective-permute-start.10 = (bf16[64,512]{1,0:T(8,128)(2,1)S(1)}, bf16[64,512]{1,0:T(8,128)(2,1)S(1)}, u32[]{:S(2)}, u32[]{:S(2)}) collective-permute-start(bf16[64,512]{1,0:T(8,128)(2,1)S(1)} %get-tuple-element.29), channel_id=1, source_target_pairs={{0,8},{4,12},{8,0},{12,4},{16,24},{20,28},{24,16},{28,20},{1,9},{5... | collective-permute-start | bytes 196616 | tf_op jit(solution)/shard_map/ppermute | solution.py:241
  44.4 1.1 %collective-permute-start.11 = (bf16[64,512]{1,0:T(8,128)(2,1)S(1)}, bf16[64,512]{1,0:T(8,128)(2,1)S(1)}, u32[]{:S(2)}, u32[]{:S(2)}) collective-permute-start(bf16[64,512]{1,0:T(8,128)(2,1)S(1)} %get-tuple-element.30), channel_id=1, source_target_pairs={{0,16},{4,20},{8,24},{12,28},{16,0},{20,4},{24,8},{28,12},{1,17},{... | collective-permute-start | bytes 196616 | tf_op jit(solution)/shard_map/ppermute | solution.py:241
  45.5 1.7 %collective-permute-start.12 = (bf16[64,512]{1,0:T(8,128)(2,1)S(1)}, bf16[64,512]{1,0:T(8,128)(2,1)S(1)}, u32[]{:S(2)}, u32[]{:S(2)}) collective-permute-start(bf16[64,512]{1,0:T(8,128)(2,1)S(1)} %get-tuple-element.31), channel_id=1, source_target_pairs={{0,24},{4,28},{8,16},{12,20},{16,8},{20,12},{24,0},{28,4},{1,25},{... | collective-permute-start | bytes 196616 | tf_op jit(solution)/shard_map/ppermute | solution.py:241
  47.2 0.5 collective-permute-done.10.refs_0_
  47.8 3.1 %collective-permute-done.11.refs_1_ = bf16[64,512]{1,0:T(8,128)(2,1)S(1)} collective-permute-done((bf16[64,512]{1,0:T(8,128)(2,1)S(1)}, bf16[64,512]{1,0:T(8,128)(2,1)S(1)}, u32[]{:S(2)}, u32[]{:S(2)}) %collective-permute-start.11) | collective-permute-done | bytes 65568 | tf_op jit(solution)/shard_map/ppermute | solution.py:241
  50.9 0.8 %collective-permute-done.12.refs_2_ = bf16[64,512]{1,0:T(8,128)(2,1)S(1)} collective-permute-done((bf16[64,512]{1,0:T(8,128)(2,1)S(1)}, bf16[64,512]{1,0:T(8,128)(2,1)S(1)}, u32[]{:S(2)}, u32[]{:S(2)}) %collective-permute-start.12) | collective-permute-done | bytes 65568 | tf_op jit(solution)/shard_map/ppermute | solution.py:241
  51.7 0.7 %shard_map.73 = (f32[64,256]{1,0:T(8,128)}, f32[64,256]{1,0:T(8,128)}) custom-call(f32[64,512]{1,0:T(8,128)S(1)} %get-tuple-element.28.keep, bf16[64,512]{1,0:T(8,128)(2,1)S(1)} %collective-permute-done.10.refs_0_, bf16[64,512]{1,0:T(8,128)(2,1)S(1)} %collective-permute-done.11.refs_1_, bf16[64,512]{1,0:T(8,128)(2,1)S(1)} %collective-permute-done.12.refs_2_), custom_call_target="tpu_custom_call" | custom-call | tf_op jit(solution)/shard_map/pallas_call | solution.py:216
  (17 shorter events, 0.4 us)
Async XLA Ops:
  0.6 12.4 %collective-permute-start = (bf16[64,4864]{1,0:T(8,128)(2,1)}, bf16[64,4864]{1,0:T(8,128)(2,1)S(1)}, u32[]{:S(2)}, u32[]{:S(2)}) collective-permute-start(bf16[64,4864]{1,0:T(8,128)(2,1)} %bitcast.2), channel_id=1, source_target_pairs={{0,1},{1,0},{2,3},{3,2},{4,5},{5,4},{6,7},{7,6},{8,9},{9,8},{10,11... | collective-permute-start | bytes 1867784 | tf_op jit(solution)/shard_map/ppermute | solution.py:238
  3.1 7.1 %collective-permute-start.1 = (bf16[64,1024]{1,0:T(8,128)(2,1)}, bf16[64,1024]{1,0:T(8,128)(2,1)S(1)}, u32[]{:S(2)}, u32[]{:S(2)}) collective-permute-start(bf16[64,1024]{1,0:T(8,128)(2,1)} %get-tuple-element.19), channel_id=1, source_target_pairs={{0,2},{1,3},{2,0},{3,1},{4,6},{5,7},{6,4},{7,5},{8,10},{9,11},{10,... | collective-permute-start | bytes 393224 | tf_op jit(solution)/shard_map/ppermute | solution.py:235
  5.7 15.4 %collective-permute-start.5 = (bf16[64,3840]{1,0:T(8,128)(2,1)}, bf16[64,3840]{1,0:T(8,128)(2,1)S(1)}, u32[]{:S(2)}, u32[]{:S(2)}) collective-permute-start(bf16[64,3840]{1,0:T(8,128)(2,1)} %get-tuple-element.21), channel_id=1, source_target_pairs={{0,2},{1,3},{2,0},{3,1},{4,6},{5,7},{6,4},{7,5},{8,10},{9,11},{10,... | collective-permute-start | bytes 1474568 | tf_op jit(solution)/shard_map/ppermute | solution.py:235
  10.3 10.9 %collective-permute-start.2 = (bf16[128,512]{1,0:T(8,128)(2,1)S(1)}, bf16[128,512]{1,0:T(8,128)(2,1)S(1)}, u32[]{:S(2)}, u32[]{:S(2)}) collective-permute-start(bf16[128,512]{1,0:T(8,128)(2,1)S(1)} %get-tuple-element.33), channel_id=1, source_target_pairs={{0,4},{4,0},{8,12},{12,8},{16,20},{20,16},{24,28},{28,24},{1,5},{5... | collective-permute-start | bytes 393224 | tf_op jit(solution)/shard_map/ppermute | solution.py:241
  12.3 8.8 %collective-permute-start.3 = (bf16[128,512]{1,0:T(8,128)(2,1)S(1)}, bf16[128,512]{1,0:T(8,128)(2,1)S(1)}, u32[]{:S(2)}, u32[]{:S(2)}) collective-permute-start(bf16[128,512]{1,0:T(8,128)(2,1)S(1)} %get-tuple-element.32), channel_id=1, source_target_pairs={{4,8},{12,16},{20,24},{8,4},{16,12},{24,20},{5,9},{13,17},{21,25},... | collective-permute-start | bytes 393224 | tf_op jit(solution)/shard_map/ppermute | solution.py:245
  13.0 1.1 %copy-start = (bf16[4864,64]{0,1:T(8,128)(2,1)S(1)}, bf16[4864,64]{0,1:T(8,128)(2,1)}, u32[]{:S(2)}) copy-start(bf16[4864,64]{0,1:T(8,128)(2,1)} %param.5) | copy-start | bytes 1867780
  14.1 0.7 %copy-start.1 = (s32[38,3]{0,1:T(4,128)S(1)}, s32[38,3]{0,1:T(4,128)}, u32[]{:S(2)}) copy-start(s32[38,3]{0,1:T(4,128)} %param.9) | copy-start | bytes 1372
  21.1 9.5 %collective-permute-start.8 = (bf16[64,3840]{1,0:T(8,128)(2,1)S(1)}, bf16[64,3840]{1,0:T(8,128)(2,1)S(1)}, u32[]{:S(2)}, u32[]{:S(2)}) collective-permute-start(bf16[64,3840]{1,0:T(8,128)(2,1)S(1)} %collective-permute-done.5.refs_8_), channel_id=1, source_target_pairs={{0,1},{1,0},{2,3},{3,2},{4,5},{5,4},{6,7},{7,6},{8,9},{9,8},{10,11... | collective-permute-start | bytes 1474568 | tf_op jit(solution)/shard_map/ppermute | solution.py:238
  21.2 2.2 %collective-permute-start.4 = (bf16[128,1024]{1,0:T(8,128)(2,1)S(1)}, bf16[128,1024]{1,0:T(8,128)(2,1)S(1)}, u32[]{:S(2)}, u32[]{:S(2)}) collective-permute-start(bf16[128,1024]{1,0:T(8,128)(2,1)S(1)} %constant_dynamic-update-slice_fusion.2.refs_6_.refs_4_), channel_id=1, source_target_pairs={{0,1},{1,0},{2,3},{3,2},{4,5},{5,4},{6,7},{7,6},{8,9},{9,8},{10,11... | collective-permute-start | bytes 786440 | tf_op jit(solution)/shard_map/ppermute | solution.py:238
  21.8 8.8 %collective-permute-start.7 = (bf16[64,1024]{1,0:T(8,128)(2,1)S(1)}, bf16[64,1024]{1,0:T(8,128)(2,1)S(1)}, u32[]{:S(2)}, u32[]{:S(2)}) collective-permute-start(bf16[64,1024]{1,0:T(8,128)(2,1)S(1)} %collective-permute-done.1.refs_6_), channel_id=1, source_target_pairs={{0,1},{1,0},{2,3},{3,2},{4,5},{5,4},{6,7},{7,6},{8,9},{9,8},{10,11... | collective-permute-start | bytes 393224 | tf_op jit(solution)/shard_map/ppermute | solution.py:238
  26.2 11.3 %collective-permute-start.6 = (bf16[4,64,256]{2,1,0:T(8,128)(2,1)S(1)}, bf16[4,64,256]{2,1,0:T(8,128)(2,1)S(1)}, u32[]{:S(2)}, u32[]{:S(2)}) collective-permute-start(bf16[4,64,256]{2,1,0:T(8,128)(2,1)S(1)} %get-tuple-element.24), channel_id=1, source_target_pairs={{0,4},{4,0},{8,12},{12,8},{16,20},{20,16},{24,28},{28,24},{1,5},{5... | collective-permute-start | bytes 393224 | tf_op jit(solution)/shard_map/ppermute | solution.py:241
  37.4 5.3 %collective-permute-start.9 = (bf16[4,64,256]{2,1,0:T(8,128)(2,1)S(1)}, bf16[4,64,256]{2,1,0:T(8,128)(2,1)S(1)}, u32[]{:S(2)}, u32[]{:S(2)}) collective-permute-start(bf16[4,64,256]{2,1,0:T(8,128)(2,1)S(1)} %get-tuple-element.27), channel_id=1, source_target_pairs={{0,4},{4,0},{8,12},{12,8},{16,20},{20,16},{24,28},{28,24},{1,5},{5... | collective-permute-start | bytes 393224 | tf_op jit(solution)/shard_map/ppermute | solution.py:241
  42.8 5.0 %collective-permute-start.10 = (bf16[64,512]{1,0:T(8,128)(2,1)S(1)}, bf16[64,512]{1,0:T(8,128)(2,1)S(1)}, u32[]{:S(2)}, u32[]{:S(2)}) collective-permute-start(bf16[64,512]{1,0:T(8,128)(2,1)S(1)} %get-tuple-element.29), channel_id=1, source_target_pairs={{0,8},{4,12},{8,0},{12,4},{16,24},{20,28},{24,16},{28,20},{1,9},{5... | collective-permute-start | bytes 196616 | tf_op jit(solution)/shard_map/ppermute | solution.py:241
  44.4 6.4 %collective-permute-start.11 = (bf16[64,512]{1,0:T(8,128)(2,1)S(1)}, bf16[64,512]{1,0:T(8,128)(2,1)S(1)}, u32[]{:S(2)}, u32[]{:S(2)}) collective-permute-start(bf16[64,512]{1,0:T(8,128)(2,1)S(1)} %get-tuple-element.30), channel_id=1, source_target_pairs={{0,16},{4,20},{8,24},{12,28},{16,0},{20,4},{24,8},{28,12},{1,17},{... | collective-permute-start | bytes 196616 | tf_op jit(solution)/shard_map/ppermute | solution.py:241
  45.5 6.1 %collective-permute-start.12 = (bf16[64,512]{1,0:T(8,128)(2,1)S(1)}, bf16[64,512]{1,0:T(8,128)(2,1)S(1)}, u32[]{:S(2)}, u32[]{:S(2)}) collective-permute-start(bf16[64,512]{1,0:T(8,128)(2,1)S(1)} %get-tuple-element.31), channel_id=1, source_target_pairs={{0,24},{4,28},{8,16},{12,20},{16,8},{20,12},{24,0},{28,4},{1,25},{... | collective-permute-start | bytes 196616 | tf_op jit(solution)/shard_map/ppermute | solution.py:241

commit v5 on v4

--- a/solution.py
+++ b/solution.py
@@ -10,7 +10,6 @@
 BS = 128
 HB = 4
 ROWS_OF_CORE = 64
-FETCHES = 4
 MIB = 1024 * 1024
 F32 = jnp.float32
 BF16 = jnp.bfloat16
@@ -54,44 +53,47 @@
         in_specs=[HBM],
         out_specs=[VMEM] * 2,
         scratch_shapes=[pltpu.SemaphoreType.DMA((3,))],
-        compiler_params=params(58),
+        compiler_params=params(44),
     )(panel)
 
 
-def project_kernel(spans, places, groups, more, fetch, *refs):
+def load_kernel(*refs):
+    count = len(refs) // 2
+    sources, targets, sems = refs[:count], refs[count:2 * count], refs[-1]
+    copies = []
+    for which, (source, target) in enumerate(zip(sources, targets)):
+        middle = source.shape[0] // 2
+        for part, span in enumerate((pl.ds(0, middle), pl.ds(middle, source.shape[0] - middle))):
+            copies.append(pltpu.make_async_copy(source.at[span], target.at[span], sems.at[which, part]))
+    for copy in copies:
+        copy.start()
+    for copy in copies:
+        copy.wait()
+
+
+def load(*arrays):
+    size = sum(array.size * array.dtype.itemsize for array in arrays)
+    return pl.pallas_call(
+        load_kernel,
+        out_shape=[shape(array.shape, array.dtype) for array in arrays],
+        in_specs=[HBM] * len(arrays),
+        out_specs=[VMEM] * len(arrays),
+        scratch_shapes=[pltpu.SemaphoreType.DMA((len(arrays), 2))],
+        compiler_params=params(45),
+        cost_estimate=pl.CostEstimate(flops=0, bytes_accessed=size, transcendentals=0),
+    )(*arrays)
+
+
+def project_kernel(spans, places, groups, more, *refs):
     ids_ref, g_ref, c_ref, basis_ref = refs[:4]
     pieces = refs[4:4 + 2 * len(places)]
     rest = list(refs[4 + 2 * len(places):])
     before = rest.pop(0) if more else None
-    rows, slots = g_ref.shape[0], g_ref.shape[1]
+    *outs, ext, prods = rest
+    slots = g_ref.shape[1]
     width = ROWS_OF_CORE
-    node = lax.axis_index("node")
     core = lax.axis_index("col") % 2
-    odd = node % 2
-    arrivals = {}
-    sems = rest.pop()
-    basis_new = rest.pop()
-    if fetch:
-        g_new, c_new = rest[1:3]
-        del rest[1:3]
-        edges = [rows * i // FETCHES for i in range(FETCHES + 1)]
-        for step, (lo, hi) in enumerate(zip(edges[:-1], edges[1:])):
-            arrivals[lo] = [
-                pltpu.make_async_copy(old.at[lo:hi], new.at[lo:hi], sems.at[step, which])
-                for which, (old, new) in enumerate(((g_ref, g_new), (c_ref, c_new)))
-            ]
-        for batch in arrivals.values():
-            for copy in batch:
-                copy.start()
-        g_ref, c_ref = g_new, c_new
-    basis_copies = []
-    at = 0
-    for step, (lo, hi) in enumerate(spans):
-        target = basis_new.at[at:at + (hi - lo) * BS]
-        basis_copies.append(pltpu.make_async_copy(basis_ref.at[lo * BS:hi * BS], target, sems.at[step, 2]))
-        basis_copies[-1].start()
-        at += (hi - lo) * BS
-    *outs, ext, prods = rest
+    odd = lax.axis_index("node") % 2
 
     for which, (base, parts) in enumerate(places):
         for owner, ref in ((core, pieces[2 * which]), (1 - core, pieces[2 * which + 1])):
@@ -102,20 +104,14 @@
                     target = pl.multiple_of(even_target + odd * (odd_target - even_target), BS)
                 ext[at, pl.ds(target, count)] = ref[base:base + width, source:source + count]
 
-    offset = node * rows - HB
     at = 0
     total = None
-    for step, (lo, hi) in enumerate(spans):
+    for lo, hi in spans:
         begin = at
         for row in range(lo, hi):
-            for first in [first for first in arrivals if first <= row]:
-                for copy in arrivals.pop(first):
-                    copy.wait()
-            near = []
-            for slot in range(slots):
-                local = jnp.clip(ids_ref[slot, row] - offset, 0, rows + 2 * HB - 1)
-                near.append(ext[:, pl.ds(pl.multiple_of(local * BS, BS), BS)])
-            near = jnp.concatenate(near, axis=1)
+            near = jnp.concatenate(
+                [ext[:, pl.ds(pl.multiple_of(ids_ref[slot, row] * BS, BS), BS)] for slot in range(slots)], axis=1
+            )
             both = jnp.concatenate(
                 [jnp.concatenate([ref[row, slot] for slot in range(slots)], axis=1) for ref in (g_ref, c_ref)], axis=0
             )
@@ -123,14 +119,10 @@
             prods[at:at + BS, 0:2 * width] = prod[0:BS]
             prods[at:at + BS, 2 * width:4 * width] = prod[BS:2 * BS]
             at += BS
-        basis_copies[step].wait()
         part = lax.dot_general(
-            basis_new[begin:at, :], prods[begin:at, :], (((0,), (0,)), ((), ())), preferred_element_type=F32
+            basis_ref[lo * BS:hi * BS, :], prods[begin:at, :], (((0,), (0,)), ((), ())), preferred_element_type=F32
         )
         total = part if total is None else total + part
-    for batch in arrivals.values():
-        for copy in batch:
-            copy.wait()
     if before is not None:
         total = total + before[...]
     if len(outs) == 1:
@@ -143,7 +135,7 @@
     send_ref[...] = jnp.where(odd == 1, total[:, 0], total[:, 1]).astype(BF16)
 
 
-def project(fixed, pieces, spans, groups, before=None, first=False):
+def project(fixed, pieces, spans, groups, before=None, last=True):
     ids, g_blocks, c_blocks, basis = fixed
     rows, slots = g_blocks.shape[0], g_blocks.shape[1]
     width = ROWS_OF_CORE
@@ -152,24 +144,18 @@
     arrays = [array for mine, other, _, _ in pieces for array in (mine, other)]
     more = [] if before is None else [before]
     count = sum(hi - lo for lo, hi in spans)
-    scratch = [
-        pltpu.VMEM((2 * width, (rows + 2 * HB) * BS), BF16),
-        pltpu.VMEM((count * BS, 4 * width), BF16),
-        pltpu.VMEM((count * BS, states), BF16),
-        pltpu.SemaphoreType.DMA((FETCHES, 3)),
-    ]
-    if first:
-        outs = [shape((states, 4 * width), F32), shape(g_blocks.shape, BF16), shape(c_blocks.shape, BF16)]
-    else:
-        outs = [shape(piece, BF16), shape(piece, F32)]
+    outs = [shape(piece, BF16), shape(piece, F32)] if last else [shape((states, 4 * width), F32)]
     places = [(base, parts) for _, _, base, parts in pieces]
     return pl.pallas_call(
-        functools.partial(project_kernel, spans, places, groups, before is not None, first),
+        functools.partial(project_kernel, spans, places, groups, before is not None),
         out_shape=outs,
-        in_specs=[SMEM] + [HBM if first else VMEM] * 2 + [HBM] + [VMEM] * (len(arrays) + len(more)),
+        in_specs=[SMEM] + [VMEM] * (3 + len(arrays) + len(more)),
         out_specs=[VMEM] * len(outs),
-        scratch_shapes=scratch,
-        compiler_params=params(42),
+        scratch_shapes=[
+            pltpu.VMEM((2 * width, (rows + 2 * HB) * BS), BF16),
+            pltpu.VMEM((count * BS, 4 * width), BF16),
+        ],
+        compiler_params=params(14),
         cost_estimate=pl.CostEstimate(flops=count, bytes_accessed=count, transcendentals=0),
     )(ids, g_blocks, c_blocks, basis, *arrays, *more)
 
@@ -228,8 +214,6 @@
     groups = nodes // 2
     halo = HB * BS
     inner = rows * BS
-    ids = block_cols.T
-    mine = panel.T
 
     def across(array):
         return lax.ppermute(array, "col", [(i, i ^ 2) for i in range(cols)])
@@ -244,17 +228,21 @@
         pairs = [(i, i + 1) for i in range(1, nodes - 1, 2)]
         return lax.ppermute(array, "node", pairs + [(j, i) for i, j in pairs])
 
-    other = cores(mine)
-    ends, middle = cut(mine)
+    ends, middle = cut(panel.T)
     far_ends, far_middle = across(ends), across(middle)
+    own = [
+        (ends, cores(ends), 0, [(0, inner, halo, halo), (halo, halo, inner, halo)]),
+        (middle, cores(middle), 0, [(0, 2 * halo, 2 * halo, inner - 2 * halo)]),
+    ]
+    g_blocks, c_blocks = load(g_blocks, c_blocks)
+    (basis,) = load(basis)
+    ids = jnp.clip(block_cols.T - (lax.axis_index("node") * rows - HB), 0, rows + 2 * HB - 1)
+    far_ends, g_blocks, c_blocks, basis, ids = lax.optimization_barrier((far_ends, g_blocks, c_blocks, basis, ids))
     all_ends = jnp.concatenate([ends, far_ends], axis=0)
     rim = jnp.concatenate([swap(all_ends[:, :halo], 1), swap_next(all_ends[:, halo:])], axis=1)
-    own = [(mine, other, 0, [(0, halo, halo, inner)])]
-    part, g_blocks, c_blocks = project(
-        (ids, g_blocks, c_blocks, basis), own, [(HB, rows - HB)], groups, first=True
-    )
+    fixed = (ids, g_blocks, c_blocks, basis)
+    (part,) = project(fixed, own, [(HB, rows - HB)], groups, last=False)
     part, far_middle = lax.optimization_barrier((part, far_middle))
-    fixed = (ids, g_blocks, c_blocks, basis)
     rim_other = cores(rim)
     rim_parts = [(0, halo + inner, 0, halo), (halo, 0, halo + inner, halo)]
     send_a, keep_a = project(

time: 52.6 us -> 46.1 us (0.88)
  Pallas kernels: 18.6 us -> 15.7 us
  waiting for transfers between devices: 14.7 us -> 12.5 us
  local copies, waits for them, and re-layouts: 2.72 us -> 1.13 us
  other arithmetic: 0 us -> 0.69 us
    pallas_call x3, Pallas kernels: 16 us -> 9.17 us  [project(): pl.pallas_call(functools.partial(project_kernel, spans, places, groups, b...]
    pallas_call x0 -> x2, Pallas kernels: none -> 5.7 us  [load(): pl.pallas_call(load_kernel, out_shape=[shape(array.shape, array.dtype) fo...]
    ppermute x2, waiting for transfers between devices: 3.57 us -> 0.8 us  [across(): return lax.ppermute(array, 'col', [(i, i ^ 2) for i in range(cols)])]
    pallas_call x1, Pallas kernels: 1.96 us -> 0.1 us  [cut(): pl.pallas_call(cut_kernel, out_shape=[shape((width, w), BF16) for w in (2...]
    unnamed x6 -> x4, local copies, waits for them, and re-layouts: 2.68 us -> 1.09 us
    ppermute x6, starting transfers between devices: 10.9 us -> 10.2 us  [swap(): return lax.ppermute(array, 'node', [(i, i ^ step) for i in range(nodes)])]
    min x0 -> x1, other arithmetic: none -> 0.69 us  [body(): jnp.clip(block_cols.T - (lax.axis_index('node') * rows - HB), 0, rows + 2...]
    ppermute x4 -> x5, starting transfers between devices: 1.22 us -> 1.16 us  [cores(): return lax.ppermute(array, 'col', [(i, i ^ 1) for i in range(cols)])]
  transfers between devices with their start and end apart: 13 -> 14, of which waited for: 6 -> 6; matrix products, arithmetic and copies ran while one was open for 2% -> 2% of each run, Pallas kernels for 34% -> 32%
where the time goes in v5:
time: 46.1 us; the launch traced here: 45.9 us
  Pallas kernels  15.7 us (34%)
  starting transfers between devices  15.1 us (33%)
  waiting for transfers between devices  12.5 us (27%)
  local copies, waits for them, and re-layouts  1.13 us (2%)
  between operations  0.77 us (2%)
  other arithmetic  0.69 us (1%)
    ppermute x6, starting transfers between devices, swap(): return lax.ppermute(array, 'node', [(i, i ^ step) for i in range(nodes)])  10.2 us
    ppermute x6, waiting for transfers between devices, swap(): return lax.ppermute(array, 'node', [(i, i ^ step) for i in range(nodes)])  10.1 us
    pallas_call x3, Pallas kernels, project(): pl.pallas_call(functools.partial(project_kernel, spans, places, groups, b...  9.17 us
    pallas_call x2, Pallas kernels, load(): pl.pallas_call(load_kernel, out_shape=[shape(array.shape, array.dtype) fo...  5.7 us
    ppermute x2, starting transfers between devices, across(): return lax.ppermute(array, 'col', [(i, i ^ 2) for i in range(cols)])  3.08 us
    ppermute x5, waiting for transfers between devices, cores(): return lax.ppermute(array, 'col', [(i, i ^ 1) for i in range(cols)])  1.55 us
    ppermute x5, starting transfers between devices, cores(): return lax.ppermute(array, 'col', [(i, i ^ 1) for i in range(cols)])  1.16 us
    unnamed x4, local copies, waits for them, and re-layouts  1.09 us
  transfers between devices with their start and end apart: 14, of which 6 were waited for; matrix products, arithmetic and copies ran while one was open for 2% of the time, Pallas kernels for 32%

profile of v5, /device:TPU:0, one launch (start us, length us, event | category | flops | bytes accessed | tf_op | source)
XLA Modules:
  0.0 45.9 jit_solution(2861077191110968977)
XLA Ops:
  0.6 1.1 %copy-done = bf16[4864,64]{0,1:T(8,128)(2,1)S(1)} copy-done((bf16[4864,64]{0,1:T(8,128)(2,1)S(1)}, bf16[4864,64]{0,1:T(8,128)(2,1)}, u32[]{:S(2)}) %copy-start) | copy-done | bytes 622616
  1.7 0.1 shard_map.68
  1.8 3.0 %collective-permute-start = (bf16[64,1024]{1,0:T(8,128)(2,1)S(1)}, bf16[64,1024]{1,0:T(8,128)(2,1)S(1)}, u32[]{:S(2)}, u32[]{:S(2)}) collective-permute-start(bf16[64,1024]{1,0:T(8,128)(2,1)S(1)} %get-tuple-element.21.refs_4_), channel_id=1, source_target_pairs={{0,2},{1,3},{2,0},{3,1},{4,6},{5,7},{6,4},{7,5},{8,10},{9,11},{10,... | collective-permute-start | bytes 393224 | tf_op jit(solution)/shard_map/ppermute | solution.py:219
  4.8 0.5 %collective-permute-start.2 = (bf16[64,3840]{1,0:T(8,128)(2,1)S(1)}, bf16[64,3840]{1,0:T(8,128)(2,1)S(1)}, u32[]{:S(2)}, u32[]{:S(2)}) collective-permute-start(bf16[64,3840]{1,0:T(8,128)(2,1)S(1)} %get-tuple-element.28.refs_6_), channel_id=1, source_target_pairs={{0,1},{1,0},{2,3},{3,2},{4,5},{5,4},{6,7},{7,6},{8,9},{9,8},{10,11... | collective-permute-start | bytes 1474568 | tf_op jit(solution)/shard_map/ppermute | solution.py:222
  5.4 0.7 %clamp_bitcast_fusion.refs_0_ = s32[3,38]{1,0:T(4,128)S(1)} fusion(s32[38,3]{0,1:T(4,128)} %param.9, s32[]{:T(128)S(6)} %sub.10), kind=kLoop, calls=%fused_computation.4 | loop fusion | flops 228 | bytes 916 | tf_op jit(solution)/shard_map/jit(clip)/min | solution.py:239
  6.1 2.5 %shard_map.70.refs_3_ = bf16[4864,512]{1,0:T(8,128)(2,1)S(1)} custom-call(bf16[4864,512]{1,0:T(8,128)(2,1)} %refs_0_.3), custom_call_target="tpu_custom_call" | custom-call | bytes 4980736 | tf_op jit(solution)/shard_map/pallas_call | solution.py:76
  8.6 3.2 %shard_map.69 = (bf16[38,3,128,128]{3,2,1,0:T(8,128)(2,1)S(1)}, bf16[38,3,128,128]{3,2,1,0:T(8,128)(2,1)S(1)}) custom-call(bf16[38,3,128,128]{3,2,1,0:T(8,128)(2,1)} %refs_0_.2, bf16[38,3,128,128]{3,2,1,0:T(8,128)(2,1)} %refs_1_.1), custom_call_target="tpu_custom_call" | custom-call | bytes 7471104 | tf_op jit(solution)/shard_map/pallas_call | solution.py:76
  11.9 2.0 %collective-permute-start.3 = (bf16[128,512]{1,0:T(8,128)(2,1)S(1)}, bf16[128,512]{1,0:T(8,128)(2,1)S(1)}, u32[]{:S(2)}, u32[]{:S(2)}) collective-permute-start(bf16[128,512]{1,0:T(8,128)(2,1)S(1)} %get-tuple-element.41), channel_id=1, source_target_pairs={{0,4},{4,0},{8,12},{12,8},{16,20},{20,16},{24,28},{28,24},{1,5},{5... | collective-permute-start | bytes 393224 | tf_op jit(solution)/shard_map/ppermute | solution.py:225
  13.9 0.7 %collective-permute-start.4 = (bf16[128,512]{1,0:T(8,128)(2,1)S(1)}, bf16[128,512]{1,0:T(8,128)(2,1)S(1)}, u32[]{:S(2)}, u32[]{:S(2)}) collective-permute-start(bf16[128,512]{1,0:T(8,128)(2,1)S(1)} %get-tuple-element.40), channel_id=1, source_target_pairs={{4,8},{12,16},{20,24},{8,4},{16,12},{24,20},{5,9},{13,17},{21,25},... | collective-permute-start | bytes 393224 | tf_op jit(solution)/shard_map/ppermute | solution.py:229
  14.6 3.4 %shard_map.71.refs_10_ = f32[512,256]{1,0:T(8,128)S(1)} custom-call(s32[3,38]{1,0:T(4,128)S(1)} %clamp_bitcast_fusion.refs_0_, bf16[38,3,128,128]{3,2,1,0:T(8,128)(2,1)S(1)} %get-tuple-element.25.refs_1_, bf16[38,3,128,128]{3,2,1,0:T(8,128)(2,1)S(1)} %get-tuple-element.26.refs_2_, bf16[4864,512]{1,0:T(8,128)(2,1)S(1)} %shard_map.70.refs_3_, ...), custom_call_target="tpu_custom_call" | custom-call | flops 30 | bytes 30 | tf_op jit(solution)/shard_map/pallas_call | solution.py:149
  18.0 0.8 %collective-permute-done.6.refs_8_ = bf16[64,3840]{1,0:T(8,128)(2,1)S(1)} collective-permute-done((bf16[64,3840]{1,0:T(8,128)(2,1)S(1)}, bf16[64,3840]{1,0:T(8,128)(2,1)S(1)}, u32[]{:S(2)}, u32[]{:S(2)}) %collective-permute-start.6) | collective-permute-done | bytes 491552 | tf_op jit(solution)/shard_map/ppermute | solution.py:219
  18.9 0.6 %collective-permute-start.5 = (bf16[128,1024]{1,0:T(8,128)(2,1)S(1)}, bf16[128,1024]{1,0:T(8,128)(2,1)S(1)}, u32[]{:S(2)}, u32[]{:S(2)}) collective-permute-start(bf16[128,1024]{1,0:T(8,128)(2,1)S(1)} %constant_dynamic-update-slice_fusion.2.refs_8_.refs_4_), channel_id=1, source_target_pairs={{0,1},{1,0},{2,3},{3,2},{4,5},{5,4},{6,7},{7,6},{8,9},{9,8},{10,11... | collective-permute-start | bytes 786440 | tf_op jit(solution)/shard_map/ppermute | solution.py:222
  19.5 1.5 %collective-permute-done.5.refs_9_.refs_5_ = bf16[128,1024]{1,0:T(8,128)(2,1)S(1)} collective-permute-done((bf16[128,1024]{1,0:T(8,128)(2,1)S(1)}, bf16[128,1024]{1,0:T(8,128)(2,1)S(1)}, u32[]{:S(2)}, u32[]{:S(2)}) %collective-permute-start.5) | collective-permute-done | bytes 262176 | tf_op jit(solution)/shard_map/ppermute | solution.py:222
  21.1 1.6 %shard_map.72 = (bf16[4,64,256]{2,1,0:T(8,128)(2,1)S(1)}, f32[4,64,256]{2,1,0:T(8,128)S(1)}) custom-call(s32[3,38]{1,0:T(4,128)S(1)} %clamp_bitcast_fusion.refs_0_, bf16[38,3,128,128]{3,2,1,0:T(8,128)(2,1)S(1)} %get-tuple-element.25.refs_1_, bf16[38,3,128,128]{3,2,1,0:T(8,128)(2,1)S(1)} %get-tuple-element.26.refs_2_, ...), custom_call_target="tpu_custom_call" | custom-call | flops 8 | bytes 8 | tf_op jit(solution)/shard_map/pallas_call | solution.py:149
  22.7 3.6 %collective-permute-start.7 = (bf16[4,64,256]{2,1,0:T(8,128)(2,1)S(1)}, bf16[4,64,256]{2,1,0:T(8,128)(2,1)S(1)}, u32[]{:S(2)}, u32[]{:S(2)}) collective-permute-start(bf16[4,64,256]{2,1,0:T(8,128)(2,1)S(1)} %get-tuple-element.32), channel_id=1, source_target_pairs={{0,4},{4,0},{8,12},{12,8},{16,20},{20,16},{24,28},{28,24},{1,5},{5... | collective-permute-start | bytes 393224 | tf_op jit(solution)/shard_map/ppermute | solution.py:225
  26.3 4.1 %shard_map.73 = (bf16[4,64,256]{2,1,0:T(8,128)(2,1)S(1)}, f32[4,64,256]{2,1,0:T(8,128)S(1)}) custom-call(s32[3,38]{1,0:T(4,128)S(1)} %clamp_bitcast_fusion.refs_0_, bf16[38,3,128,128]{3,2,1,0:T(8,128)(2,1)S(1)} %get-tuple-element.25.refs_1_, bf16[38,3,128,128]{3,2,1,0:T(8,128)(2,1)S(1)} %get-tuple-element.26.refs_2_, ...), custom_call_target="tpu_custom_call" | custom-call | flops 38 | bytes 38 | tf_op jit(solution)/shard_map/pallas_call | solution.py:149
  30.5 5.2 %collective-permute-done.10.got_b = bf16[4,64,256]{2,1,0:T(8,128)(2,1)S(1)} collective-permute-done((bf16[4,64,256]{2,1,0:T(8,128)(2,1)S(1)}, bf16[4,64,256]{2,1,0:T(8,128)(2,1)S(1)}, u32[]{:S(2)}, u32[]{:S(2)}) %collective-permute-start.10) | collective-permute-done | bytes 131104 | tf_op jit(solution)/shard_map/ppermute | solution.py:225
  35.8 1.6 %collective-permute-start.11 = (bf16[64,512]{1,0:T(8,128)(2,1)S(1)}, bf16[64,512]{1,0:T(8,128)(2,1)S(1)}, u32[]{:S(2)}, u32[]{:S(2)}) collective-permute-start(bf16[64,512]{1,0:T(8,128)(2,1)S(1)} %get-tuple-element.37), channel_id=1, source_target_pairs={{0,8},{4,12},{8,0},{12,4},{16,24},{20,28},{24,16},{28,20},{1,9},{5... | collective-permute-start | bytes 196616 | tf_op jit(solution)/shard_map/ppermute | solution.py:225
  37.5 1.5 %collective-permute-start.12 = (bf16[64,512]{1,0:T(8,128)(2,1)S(1)}, bf16[64,512]{1,0:T(8,128)(2,1)S(1)}, u32[]{:S(2)}, u32[]{:S(2)}) collective-permute-start(bf16[64,512]{1,0:T(8,128)(2,1)S(1)} %get-tuple-element.38), channel_id=1, source_target_pairs={{0,16},{4,20},{8,24},{12,28},{16,0},{20,4},{24,8},{28,12},{1,17},{... | collective-permute-start | bytes 196616 | tf_op jit(solution)/shard_map/ppermute | solution.py:225
  39.0 1.3 %collective-permute-start.13 = (bf16[64,512]{1,0:T(8,128)(2,1)S(1)}, bf16[64,512]{1,0:T(8,128)(2,1)S(1)}, u32[]{:S(2)}, u32[]{:S(2)}) collective-permute-start(bf16[64,512]{1,0:T(8,128)(2,1)S(1)} %get-tuple-element.39), channel_id=1, source_target_pairs={{0,24},{4,28},{8,16},{12,20},{16,8},{20,12},{24,0},{28,4},{1,25},{... | collective-permute-start | bytes 196616 | tf_op jit(solution)/shard_map/ppermute | solution.py:225
  40.3 0.5 %collective-permute-done.11.refs_0_ = bf16[64,512]{1,0:T(8,128)(2,1)S(1)} collective-permute-done((bf16[64,512]{1,0:T(8,128)(2,1)S(1)}, bf16[64,512]{1,0:T(8,128)(2,1)S(1)}, u32[]{:S(2)}, u32[]{:S(2)}) %collective-permute-start.11) | collective-permute-done | bytes 65568 | tf_op jit(solution)/shard_map/ppermute | solution.py:225
  40.8 3.3 %collective-permute-done.12.refs_1_ = bf16[64,512]{1,0:T(8,128)(2,1)S(1)} collective-permute-done((bf16[64,512]{1,0:T(8,128)(2,1)S(1)}, bf16[64,512]{1,0:T(8,128)(2,1)S(1)}, u32[]{:S(2)}, u32[]{:S(2)}) %collective-permute-start.12) | collective-permute-done | bytes 65568 | tf_op jit(solution)/shard_map/ppermute | solution.py:225
  44.0 1.1 %collective-permute-done.13.refs_2_ = bf16[64,512]{1,0:T(8,128)(2,1)S(1)} collective-permute-done((bf16[64,512]{1,0:T(8,128)(2,1)S(1)}, bf16[64,512]{1,0:T(8,128)(2,1)S(1)}, u32[]{:S(2)}, u32[]{:S(2)}) %collective-permute-start.13) | collective-permute-done | bytes 65568 | tf_op jit(solution)/shard_map/ppermute | solution.py:225
  45.2 0.7 %shard_map.75 = (f32[64,256]{1,0:T(8,128)}, f32[64,256]{1,0:T(8,128)}) custom-call(f32[64,512]{1,0:T(8,128)S(1)} %get-tuple-element.36.keep, bf16[64,512]{1,0:T(8,128)(2,1)S(1)} %collective-permute-done.11.refs_0_, bf16[64,512]{1,0:T(8,128)(2,1)S(1)} %collective-permute-done.12.refs_1_, bf16[64,512]{1,0:T(8,128)(2,1)S(1)} %collective-permute-done.13.refs_2_), custom_call_target="tpu_custom_call" | custom-call | tf_op jit(solution)/shard_map/pallas_call | solution.py:202
  (20 shorter events, 0.4 us)
Async XLA Ops:
  0.6 1.1 %copy-start = (bf16[4864,64]{0,1:T(8,128)(2,1)S(1)}, bf16[4864,64]{0,1:T(8,128)(2,1)}, u32[]{:S(2)}) copy-start(bf16[4864,64]{0,1:T(8,128)(2,1)} %param.5) | copy-start | bytes 1867780
  1.8 10.0 %collective-permute-start = (bf16[64,1024]{1,0:T(8,128)(2,1)S(1)}, bf16[64,1024]{1,0:T(8,128)(2,1)S(1)}, u32[]{:S(2)}, u32[]{:S(2)}) collective-permute-start(bf16[64,1024]{1,0:T(8,128)(2,1)S(1)} %get-tuple-element.21.refs_4_), channel_id=1, source_target_pairs={{0,2},{1,3},{2,0},{3,1},{4,6},{5,7},{6,4},{7,5},{8,10},{9,11},{10,... | collective-permute-start | bytes 393224 | tf_op jit(solution)/shard_map/ppermute | solution.py:219
  4.8 9.8 %collective-permute-start.1 = (bf16[64,1024]{1,0:T(8,128)(2,1)S(1)}, bf16[64,1024]{1,0:T(8,128)(2,1)S(1)}, u32[]{:S(2)}, u32[]{:S(2)}) collective-permute-start(bf16[64,1024]{1,0:T(8,128)(2,1)S(1)} %get-tuple-element.21.refs_4_), channel_id=1, source_target_pairs={{0,1},{1,0},{2,3},{3,2},{4,5},{5,4},{6,7},{7,6},{8,9},{9,8},{10,11... | collective-permute-start | bytes 393224 | tf_op jit(solution)/shard_map/ppermute | solution.py:222
  4.8 9.8 %collective-permute-start.2 = (bf16[64,3840]{1,0:T(8,128)(2,1)S(1)}, bf16[64,3840]{1,0:T(8,128)(2,1)S(1)}, u32[]{:S(2)}, u32[]{:S(2)}) collective-permute-start(bf16[64,3840]{1,0:T(8,128)(2,1)S(1)} %get-tuple-element.28.refs_6_), channel_id=1, source_target_pairs={{0,1},{1,0},{2,3},{3,2},{4,5},{5,4},{6,7},{7,6},{8,9},{9,8},{10,11... | collective-permute-start | bytes 1474568 | tf_op jit(solution)/shard_map/ppermute | solution.py:222
  5.3 13.5 %collective-permute-start.6 = (bf16[64,3840]{1,0:T(8,128)(2,1)S(1)}, bf16[64,3840]{1,0:T(8,128)(2,1)S(1)}, u32[]{:S(2)}, u32[]{:S(2)}) collective-permute-start(bf16[64,3840]{1,0:T(8,128)(2,1)S(1)} %get-tuple-element.28.refs_6_), channel_id=1, source_target_pairs={{0,2},{1,3},{2,0},{3,1},{4,6},{5,7},{6,4},{7,5},{8,10},{9,11},{10,... | collective-permute-start | bytes 1474568 | tf_op jit(solution)/shard_map/ppermute | solution.py:219
  11.9 7.0 %collective-permute-start.3 = (bf16[128,512]{1,0:T(8,128)(2,1)S(1)}, bf16[128,512]{1,0:T(8,128)(2,1)S(1)}, u32[]{:S(2)}, u32[]{:S(2)}) collective-permute-start(bf16[128,512]{1,0:T(8,128)(2,1)S(1)} %get-tuple-element.41), channel_id=1, source_target_pairs={{0,4},{4,0},{8,12},{12,8},{16,20},{20,16},{24,28},{28,24},{1,5},{5... | collective-permute-start | bytes 393224 | tf_op jit(solution)/shard_map/ppermute | solution.py:225
  13.9 4.9 %collective-permute-start.4 = (bf16[128,512]{1,0:T(8,128)(2,1)S(1)}, bf16[128,512]{1,0:T(8,128)(2,1)S(1)}, u32[]{:S(2)}, u32[]{:S(2)}) collective-permute-start(bf16[128,512]{1,0:T(8,128)(2,1)S(1)} %get-tuple-element.40), channel_id=1, source_target_pairs={{4,8},{12,16},{20,24},{8,4},{16,12},{24,20},{5,9},{13,17},{21,25},... | collective-permute-start | bytes 393224 | tf_op jit(solution)/shard_map/ppermute | solution.py:229
  18.8 7.5 %collective-permute-start.9 = (bf16[64,3840]{1,0:T(8,128)(2,1)S(1)}, bf16[64,3840]{1,0:T(8,128)(2,1)S(1)}, u32[]{:S(2)}, u32[]{:S(2)}) collective-permute-start(bf16[64,3840]{1,0:T(8,128)(2,1)S(1)} %collective-permute-done.6.refs_8_), channel_id=1, source_target_pairs={{0,1},{1,0},{2,3},{3,2},{4,5},{5,4},{6,7},{7,6},{8,9},{9,8},{10,11... | collective-permute-start | bytes 1474568 | tf_op jit(solution)/shard_map/ppermute | solution.py:222
  18.9 2.2 %collective-permute-start.5 = (bf16[128,1024]{1,0:T(8,128)(2,1)S(1)}, bf16[128,1024]{1,0:T(8,128)(2,1)S(1)}, u32[]{:S(2)}, u32[]{:S(2)}) collective-permute-start(bf16[128,1024]{1,0:T(8,128)(2,1)S(1)} %constant_dynamic-update-slice_fusion.2.refs_8_.refs_4_), channel_id=1, source_target_pairs={{0,1},{1,0},{2,3},{3,2},{4,5},{5,4},{6,7},{7,6},{8,9},{9,8},{10,11... | collective-permute-start | bytes 786440 | tf_op jit(solution)/shard_map/ppermute | solution.py:222
  19.5 6.8 %collective-permute-start.8 = (bf16[64,1024]{1,0:T(8,128)(2,1)S(1)}, bf16[64,1024]{1,0:T(8,128)(2,1)S(1)}, u32[]{:S(2)}, u32[]{:S(2)}) collective-permute-start(bf16[64,1024]{1,0:T(8,128)(2,1)S(1)} %collective-permute-done.refs_6_), channel_id=1, source_target_pairs={{0,1},{1,0},{2,3},{3,2},{4,5},{5,4},{6,7},{7,6},{8,9},{9,8},{10,11... | collective-permute-start | bytes 393224 | tf_op jit(solution)/shard_map/ppermute | solution.py:222
  22.7 7.8 %collective-permute-start.7 = (bf16[4,64,256]{2,1,0:T(8,128)(2,1)S(1)}, bf16[4,64,256]{2,1,0:T(8,128)(2,1)S(1)}, u32[]{:S(2)}, u32[]{:S(2)}) collective-permute-start(bf16[4,64,256]{2,1,0:T(8,128)(2,1)S(1)} %get-tuple-element.32), channel_id=1, source_target_pairs={{0,4},{4,0},{8,12},{12,8},{16,20},{20,16},{24,28},{28,24},{1,5},{5... | collective-permute-start | bytes 393224 | tf_op jit(solution)/shard_map/ppermute | solution.py:225
  30.5 5.3 %collective-permute-start.10 = (bf16[4,64,256]{2,1,0:T(8,128)(2,1)S(1)}, bf16[4,64,256]{2,1,0:T(8,128)(2,1)S(1)}, u32[]{:S(2)}, u32[]{:S(2)}) collective-permute-start(bf16[4,64,256]{2,1,0:T(8,128)(2,1)S(1)} %get-tuple-element.35), channel_id=1, source_target_pairs={{0,4},{4,0},{8,12},{12,8},{16,20},{20,16},{24,28},{28,24},{1,5},{5... | collective-permute-start | bytes 393224 | tf_op jit(solution)/shard_map/ppermute | solution.py:225
  35.8 5.0 %collective-permute-start.11 = (bf16[64,512]{1,0:T(8,128)(2,1)S(1)}, bf16[64,512]{1,0:T(8,128)(2,1)S(1)}, u32[]{:S(2)}, u32[]{:S(2)}) collective-permute-start(bf16[64,512]{1,0:T(8,128)(2,1)S(1)} %get-tuple-element.37), channel_id=1, source_target_pairs={{0,8},{4,12},{8,0},{12,4},{16,24},{20,28},{24,16},{28,20},{1,9},{5... | collective-permute-start | bytes 196616 | tf_op jit(solution)/shard_map/ppermute | solution.py:225
  37.5 6.6 %collective-permute-start.12 = (bf16[64,512]{1,0:T(8,128)(2,1)S(1)}, bf16[64,512]{1,0:T(8,128)(2,1)S(1)}, u32[]{:S(2)}, u32[]{:S(2)}) collective-permute-start(bf16[64,512]{1,0:T(8,128)(2,1)S(1)} %get-tuple-element.38), channel_id=1, source_target_pairs={{0,16},{4,20},{8,24},{12,28},{16,0},{20,4},{24,8},{28,12},{1,17},{... | collective-permute-start | bytes 196616 | tf_op jit(solution)/shard_map/ppermute | solution.py:225
  39.0 6.2 %collective-permute-start.13 = (bf16[64,512]{1,0:T(8,128)(2,1)S(1)}, bf16[64,512]{1,0:T(8,128)(2,1)S(1)}, u32[]{:S(2)}, u32[]{:S(2)}) collective-permute-start(bf16[64,512]{1,0:T(8,128)(2,1)S(1)} %get-tuple-element.39), channel_id=1, source_target_pairs={{0,24},{4,28},{8,16},{12,20},{16,8},{20,12},{24,0},{28,4},{1,25},{... | collective-permute-start | bytes 196616 | tf_op jit(solution)/shard_map/ppermute | solution.py:225

commit v6 on v5

--- a/solution.py
+++ b/solution.py
@@ -160,52 +160,49 @@
     )(ids, g_blocks, c_blocks, basis, *arrays, *more)
 
 
-def spread_kernel(groups, keep_a, got_a, keep_b, got_b, keep_ref, *send_refs):
+def spread_kernel(groups, keep, got, keep_ref, *send_refs):
     here = lax.axis_index("node") // 2
-    half = keep_a.shape[2]
     for step in range(groups):
-        at = here ^ step
-        for lo, keep, got in ((0, keep_a, got_a), (half, keep_b, got_b)):
-            value = keep[at] + got[at].astype(F32)
-            if step == 0:
-                keep_ref[:, lo:lo + half] = value
-            else:
-                send_refs[step - 1][:, lo:lo + half] = value.astype(BF16)
-
-
-def spread(groups, keep_a, got_a, keep_b, got_b):
-    piece = (keep_a.shape[1], 2 * keep_a.shape[2])
+        value = keep[here ^ step] + got[here ^ step].astype(F32)
+        if step == 0:
+            keep_ref[...] = value
+        else:
+            send_refs[step - 1][...] = value.astype(BF16)
+
+
+def spread(groups, keep, got):
+    piece = keep.shape[1:]
     return pl.pallas_call(
         functools.partial(spread_kernel, groups),
         out_shape=[shape(piece, F32)] + [shape(piece, BF16)] * (groups - 1),
-        in_specs=[VMEM] * 4,
+        in_specs=[VMEM] * 2,
         out_specs=[VMEM] * groups,
         compiler_params=params(4),
-    )(keep_a, got_a, keep_b, got_b)
-
-
-def finish_kernel(keep, *refs):
-    got, (out_g, out_c) = refs[:-2], refs[-2:]
-    total = keep[...]
-    for ref in got:
-        total = total + ref[...].astype(F32)
+    )(keep, got)
+
+
+def finish_kernel(count, *refs):
+    out_g, out_c = refs[-2:]
+    quarter = out_g.shape[1] // 2
     first = lax.axis_index("col") // 2
-    quarter = total.shape[1] // 4
-    for place, base in ((first, 0), (1 - first, 2 * quarter)):
+    for place, half in ((first, refs[:count]), (1 - first, refs[count:2 * count])):
+        total = half[0][...]
+        for ref in half[1:]:
+            total = total + ref[...].astype(F32)
         at = pl.ds(pl.multiple_of(place * quarter, quarter), quarter)
-        out_g[:, at] = total[:, base:base + quarter]
-        out_c[:, at] = total[:, base + quarter:base + 2 * quarter]
-
-
-def finish(keep, got):
-    piece = shape((keep.shape[0], keep.shape[1] // 2), F32)
-    return pl.pallas_call(
-        finish_kernel,
+        out_g[:, at] = total[:, 0:quarter]
+        out_c[:, at] = total[:, quarter:2 * quarter]
+
+
+def finish(own, far):
+    piece = shape(own[0].shape, F32)
+    return pl.pallas_call(
+        functools.partial(finish_kernel, len(own)),
         out_shape=(piece, piece),
-        in_specs=[VMEM] * (1 + len(got)),
+        in_specs=[VMEM] * (len(own) + len(far)),
         out_specs=(VMEM, VMEM),
         compiler_params=params(4),
-    )(keep, *got)
+    )(*own, *far)
 
 
 def body(panel, basis, g_blocks, c_blocks, block_cols):
@@ -256,8 +253,11 @@
     ]
     send_b, keep_b = project(fixed, far, [(0, rows)], groups)
     got_b = swap(send_b, 1)
-    keep, *sends = spread(groups, keep_a, got_a, keep_b, got_b)
-    return finish(keep, [swap(send, 2 * step) for step, send in enumerate(sends, 1)])
+    halves = []
+    for keep, got in ((keep_a, got_a), (keep_b, got_b)):
+        keep, *sends = spread(groups, keep, got)
+        halves.append([keep] + [swap(send, 2 * step) for step, send in enumerate(sends, 1)])
+    return finish(*halves)
 
 
 def solution(mesh):

time: 46.1 us -> 46.5 us (level)
  starting transfers between devices: 15.1 us -> 20 us
  waiting for transfers between devices: 12.5 us -> 8.06 us
    ppermute x6 -> x9, starting transfers between devices: 10.2 us -> 15 us  [swap(): return lax.ppermute(array, 'node', [(i, i ^ step) for i in range(nodes)])]
    ppermute x6 -> x9, waiting for transfers between devices: 10.1 us -> 5.72 us  [swap(): return lax.ppermute(array, 'node', [(i, i ^ step) for i in range(nodes)])]
  transfers between devices with their start and end apart: 14 -> 17, of which waited for: 6 -> 6; matrix products, arithmetic and copies ran while one was open for 2% -> 2% of each run, Pallas kernels for 32% -> 32%
where the time goes in v6:
time: 46.5 us; the launch traced here: 46.3 us
  starting transfers between devices  20 us (43%)
  Pallas kernels  15.7 us (34%)
  waiting for transfers between devices  8.06 us (17%)
  local copies, waits for them, and re-layouts  1.13 us (2%)
  between operations  0.78 us (2%)
  other arithmetic  0.69 us (1%)
    ppermute x9, starting transfers between devices, swap(): return lax.ppermute(array, 'node', [(i, i ^ step) for i in range(nodes)])  15 us
    pallas_call x3, Pallas kernels, project(): pl.pallas_call(functools.partial(project_kernel, spans, places, groups, b...  9.18 us
    ppermute x9, waiting for transfers between devices, swap(): return lax.ppermute(array, 'node', [(i, i ^ step) for i in range(nodes)])  5.72 us
    pallas_call x2, Pallas kernels, load(): pl.pallas_call(load_kernel, out_shape=[shape(array.shape, array.dtype) fo...  5.7 us
    ppermute x2, starting transfers between devices, across(): return lax.ppermute(array, 'col', [(i, i ^ 2) for i in range(cols)])  3.08 us
    ppermute x5, waiting for transfers between devices, cores(): return lax.ppermute(array, 'col', [(i, i ^ 1) for i in range(cols)])  1.55 us
    ppermute x5, starting transfers between devices, cores(): return lax.ppermute(array, 'col', [(i, i ^ 1) for i in range(cols)])  1.16 us
    unnamed x4, local copies, waits for them, and re-layouts  1.09 us
  transfers between devices with their start and end apart: 17, of which 6 were waited for; matrix products, arithmetic and copies ran while one was open for 2% of the time, Pallas kernels for 32%

profile of v6, /device:TPU:0, one launch (start us, length us, event | category | flops | bytes accessed | tf_op | source)
XLA Modules:
  0.0 46.3 jit_solution(17070626103997467691)
XLA Ops:
  0.6 1.1 %copy-done = bf16[4864,64]{0,1:T(8,128)(2,1)S(1)} copy-done((bf16[4864,64]{0,1:T(8,128)(2,1)S(1)}, bf16[4864,64]{0,1:T(8,128)(2,1)}, u32[]{:S(2)}) %copy-start) | copy-done | bytes 622616
  1.8 3.0 %collective-permute-start = (bf16[64,1024]{1,0:T(8,128)(2,1)S(1)}, bf16[64,1024]{1,0:T(8,128)(2,1)S(1)}, u32[]{:S(2)}, u32[]{:S(2)}) collective-permute-start(bf16[64,1024]{1,0:T(8,128)(2,1)S(1)} %get-tuple-element.25.refs_4_), channel_id=1, source_target_pairs={{0,2},{1,3},{2,0},{3,1},{4,6},{5,7},{6,4},{7,5},{8,10},{9,11},{10,... | collective-permute-start | bytes 393224 | tf_op jit(solution)/shard_map/ppermute | solution.py:216
  4.8 0.5 %collective-permute-start.2 = (bf16[64,3840]{1,0:T(8,128)(2,1)S(1)}, bf16[64,3840]{1,0:T(8,128)(2,1)S(1)}, u32[]{:S(2)}, u32[]{:S(2)}) collective-permute-start(bf16[64,3840]{1,0:T(8,128)(2,1)S(1)} %get-tuple-element.32.refs_6_), channel_id=1, source_target_pairs={{0,1},{1,0},{2,3},{3,2},{4,5},{5,4},{6,7},{7,6},{8,9},{9,8},{10,11... | collective-permute-start | bytes 1474568 | tf_op jit(solution)/shard_map/ppermute | solution.py:219
  5.4 0.7 %clamp_bitcast_fusion.refs_0_ = s32[3,38]{1,0:T(4,128)S(1)} fusion(s32[38,3]{0,1:T(4,128)} %param.9, s32[]{:T(128)S(6)} %sub.10), kind=kLoop, calls=%fused_computation.4 | loop fusion | flops 228 | bytes 916 | tf_op jit(solution)/shard_map/jit(clip)/min | solution.py:236
  6.1 2.5 %shard_map.70.refs_3_ = bf16[4864,512]{1,0:T(8,128)(2,1)S(1)} custom-call(bf16[4864,512]{1,0:T(8,128)(2,1)} %refs_0_.3), custom_call_target="tpu_custom_call" | custom-call | bytes 4980736 | tf_op jit(solution)/shard_map/pallas_call | solution.py:76
  8.6 3.2 %shard_map.69 = (bf16[38,3,128,128]{3,2,1,0:T(8,128)(2,1)S(1)}, bf16[38,3,128,128]{3,2,1,0:T(8,128)(2,1)S(1)}) custom-call(bf16[38,3,128,128]{3,2,1,0:T(8,128)(2,1)} %refs_0_.2, bf16[38,3,128,128]{3,2,1,0:T(8,128)(2,1)} %refs_1_.1), custom_call_target="tpu_custom_call" | custom-call | bytes 7471104 | tf_op jit(solution)/shard_map/pallas_call | solution.py:76
  11.9 2.0 %collective-permute-start.3 = (bf16[128,512]{1,0:T(8,128)(2,1)S(1)}, bf16[128,512]{1,0:T(8,128)(2,1)S(1)}, u32[]{:S(2)}, u32[]{:S(2)}) collective-permute-start(bf16[128,512]{1,0:T(8,128)(2,1)S(1)} %get-tuple-element.49), channel_id=1, source_target_pairs={{0,4},{4,0},{8,12},{12,8},{16,20},{20,16},{24,28},{28,24},{1,5},{5... | collective-permute-start | bytes 393224 | tf_op jit(solution)/shard_map/ppermute | solution.py:222
  13.9 0.7 %collective-permute-start.4 = (bf16[128,512]{1,0:T(8,128)(2,1)S(1)}, bf16[128,512]{1,0:T(8,128)(2,1)S(1)}, u32[]{:S(2)}, u32[]{:S(2)}) collective-permute-start(bf16[128,512]{1,0:T(8,128)(2,1)S(1)} %get-tuple-element.48), channel_id=1, source_target_pairs={{4,8},{12,16},{20,24},{8,4},{16,12},{24,20},{5,9},{13,17},{21,25},... | collective-permute-start | bytes 393224 | tf_op jit(solution)/shard_map/ppermute | solution.py:226
  14.6 3.4 %shard_map.71.refs_10_ = f32[512,256]{1,0:T(8,128)S(1)} custom-call(s32[3,38]{1,0:T(4,128)S(1)} %clamp_bitcast_fusion.refs_0_, bf16[38,3,128,128]{3,2,1,0:T(8,128)(2,1)S(1)} %get-tuple-element.29.refs_1_, bf16[38,3,128,128]{3,2,1,0:T(8,128)(2,1)S(1)} %get-tuple-element.30.refs_2_, bf16[4864,512]{1,0:T(8,128)(2,1)S(1)} %shard_map.70.refs_3_, ...), custom_call_target="tpu_custom_call" | custom-call | flops 30 | bytes 30 | tf_op jit(solution)/shard_map/pallas_call | solution.py:149
  18.1 0.8 %collective-permute-done.6.refs_8_ = bf16[64,3840]{1,0:T(8,128)(2,1)S(1)} collective-permute-done((bf16[64,3840]{1,0:T(8,128)(2,1)S(1)}, bf16[64,3840]{1,0:T(8,128)(2,1)S(1)}, u32[]{:S(2)}, u32[]{:S(2)}) %collective-permute-start.6) | collective-permute-done | bytes 491552 | tf_op jit(solution)/shard_map/ppermute | solution.py:216
  18.9 0.6 %collective-permute-start.5 = (bf16[128,1024]{1,0:T(8,128)(2,1)S(1)}, bf16[128,1024]{1,0:T(8,128)(2,1)S(1)}, u32[]{:S(2)}, u32[]{:S(2)}) collective-permute-start(bf16[128,1024]{1,0:T(8,128)(2,1)S(1)} %constant_dynamic-update-slice_fusion.2.refs_8_.refs_4_), channel_id=1, source_target_pairs={{0,1},{1,0},{2,3},{3,2},{4,5},{5,4},{6,7},{7,6},{8,9},{9,8},{10,11... | collective-permute-start | bytes 786440 | tf_op jit(solution)/shard_map/ppermute | solution.py:219
  19.5 1.5 %collective-permute-done.5.refs_9_.refs_5_ = bf16[128,1024]{1,0:T(8,128)(2,1)S(1)} collective-permute-done((bf16[128,1024]{1,0:T(8,128)(2,1)S(1)}, bf16[128,1024]{1,0:T(8,128)(2,1)S(1)}, u32[]{:S(2)}, u32[]{:S(2)}) %collective-permute-start.5) | collective-permute-done | bytes 262176 | tf_op jit(solution)/shard_map/ppermute | solution.py:219
  21.1 1.6 %shard_map.72 = (bf16[4,64,256]{2,1,0:T(8,128)(2,1)S(1)}, f32[4,64,256]{2,1,0:T(8,128)S(1)}) custom-call(s32[3,38]{1,0:T(4,128)S(1)} %clamp_bitcast_fusion.refs_0_, bf16[38,3,128,128]{3,2,1,0:T(8,128)(2,1)S(1)} %get-tuple-element.29.refs_1_, bf16[38,3,128,128]{3,2,1,0:T(8,128)(2,1)S(1)} %get-tuple-element.30.refs_2_, ...), custom_call_target="tpu_custom_call" | custom-call | flops 8 | bytes 8 | tf_op jit(solution)/shard_map/pallas_call | solution.py:149
  22.7 3.6 %collective-permute-start.7 = (bf16[4,64,256]{2,1,0:T(8,128)(2,1)S(1)}, bf16[4,64,256]{2,1,0:T(8,128)(2,1)S(1)}, u32[]{:S(2)}, u32[]{:S(2)}) collective-permute-start(bf16[4,64,256]{2,1,0:T(8,128)(2,1)S(1)} %get-tuple-element.36), channel_id=1, source_target_pairs={{0,4},{4,0},{8,12},{12,8},{16,20},{20,16},{24,28},{28,24},{1,5},{5... | collective-permute-start | bytes 393224 | tf_op jit(solution)/shard_map/ppermute | solution.py:222
  26.3 4.1 %shard_map.74 = (bf16[4,64,256]{2,1,0:T(8,128)(2,1)S(1)}, f32[4,64,256]{2,1,0:T(8,128)S(1)}) custom-call(s32[3,38]{1,0:T(4,128)S(1)} %clamp_bitcast_fusion.refs_0_, bf16[38,3,128,128]{3,2,1,0:T(8,128)(2,1)S(1)} %get-tuple-element.29.refs_1_, bf16[38,3,128,128]{3,2,1,0:T(8,128)(2,1)S(1)} %get-tuple-element.30.refs_2_, ...), custom_call_target="tpu_custom_call" | custom-call | flops 38 | bytes 38 | tf_op jit(solution)/shard_map/pallas_call | solution.py:149
  30.6 2.3 %collective-permute-start.8 = (bf16[64,256]{1,0:T(8,128)(2,1)S(1)}, bf16[64,256]{1,0:T(8,128)(2,1)S(1)}, u32[]{:S(2)}, u32[]{:S(2)}) collective-permute-start(bf16[64,256]{1,0:T(8,128)(2,1)S(1)} %get-tuple-element.38), channel_id=1, source_target_pairs={{0,8},{4,12},{8,0},{12,4},{16,24},{20,28},{24,16},{28,20},{1,9},{5... | collective-permute-start | bytes 98312 | tf_op jit(solution)/shard_map/ppermute | solution.py:222
  32.9 2.6 %collective-permute-start.9 = (bf16[64,256]{1,0:T(8,128)(2,1)S(1)}, bf16[64,256]{1,0:T(8,128)(2,1)S(1)}, u32[]{:S(2)}, u32[]{:S(2)}) collective-permute-start(bf16[64,256]{1,0:T(8,128)(2,1)S(1)} %get-tuple-element.39), channel_id=1, source_target_pairs={{0,16},{4,20},{8,24},{12,28},{16,0},{20,4},{24,8},{28,12},{1,17},{... | collective-permute-start | bytes 98312 | tf_op jit(solution)/shard_map/ppermute | solution.py:222
  35.5 0.3 collective-permute-done.13.got
  35.8 1.6 %collective-permute-start.14 = (bf16[64,256]{1,0:T(8,128)(2,1)S(1)}, bf16[64,256]{1,0:T(8,128)(2,1)S(1)}, u32[]{:S(2)}, u32[]{:S(2)}) collective-permute-start(bf16[64,256]{1,0:T(8,128)(2,1)S(1)} %get-tuple-element.45), channel_id=1, source_target_pairs={{0,8},{4,12},{8,0},{12,4},{16,24},{20,28},{24,16},{28,20},{1,9},{5... | collective-permute-start | bytes 98312 | tf_op jit(solution)/shard_map/ppermute | solution.py:222
  37.5 2.5 %collective-permute-start.15 = (bf16[64,256]{1,0:T(8,128)(2,1)S(1)}, bf16[64,256]{1,0:T(8,128)(2,1)S(1)}, u32[]{:S(2)}, u32[]{:S(2)}) collective-permute-start(bf16[64,256]{1,0:T(8,128)(2,1)S(1)} %get-tuple-element.46), channel_id=1, source_target_pairs={{0,16},{4,20},{8,24},{12,28},{16,0},{20,4},{24,8},{28,12},{1,17},{... | collective-permute-start | bytes 98312 | tf_op jit(solution)/shard_map/ppermute | solution.py:222
  40.3 0.9 %collective-permute-done.10.refs_3_ = bf16[64,256]{1,0:T(8,128)(2,1)S(1)} collective-permute-done((bf16[64,256]{1,0:T(8,128)(2,1)S(1)}, bf16[64,256]{1,0:T(8,128)(2,1)S(1)}, u32[]{:S(2)}, u32[]{:S(2)}) %collective-permute-start.10) | collective-permute-done | bytes 32800 | tf_op jit(solution)/shard_map/ppermute | solution.py:222
  41.2 1.3 %collective-permute-done.15.refs_6_ = bf16[64,256]{1,0:T(8,128)(2,1)S(1)} collective-permute-done((bf16[64,256]{1,0:T(8,128)(2,1)S(1)}, bf16[64,256]{1,0:T(8,128)(2,1)S(1)}, u32[]{:S(2)}, u32[]{:S(2)}) %collective-permute-start.15) | collective-permute-done | bytes 32800 | tf_op jit(solution)/shard_map/ppermute | solution.py:222
  42.5 3.1 %collective-permute-done.16.refs_7_ = bf16[64,256]{1,0:T(8,128)(2,1)S(1)} collective-permute-done((bf16[64,256]{1,0:T(8,128)(2,1)S(1)}, bf16[64,256]{1,0:T(8,128)(2,1)S(1)}, u32[]{:S(2)}, u32[]{:S(2)}) %collective-permute-start.16) | collective-permute-done | bytes 32800 | tf_op jit(solution)/shard_map/ppermute | solution.py:222
  45.7 0.7 %shard_map.76 = (f32[64,256]{1,0:T(8,128)}, f32[64,256]{1,0:T(8,128)}) custom-call(f32[64,256]{1,0:T(8,128)S(1)} %get-tuple-element.37.refs_0_, bf16[64,256]{1,0:T(8,128)(2,1)S(1)} %collective-permute-done.8.refs_1_, bf16[64,256]{1,0:T(8,128)(2,1)S(1)} %collective-permute-done.9.refs_2_, bf16[64,256]{1,0:T(8,128)(2,1)S(1)} %collective-permute-done.10.refs_3_, ...), custom_call_target="tpu_custom_call" | custom-call | tf_op jit(solution)/shard_map/pallas_call | solution.py:199
  (27 shorter events, 0.8 us)
Async XLA Ops:
  0.6 1.1 %copy-start = (bf16[4864,64]{0,1:T(8,128)(2,1)S(1)}, bf16[4864,64]{0,1:T(8,128)(2,1)}, u32[]{:S(2)}) copy-start(bf16[4864,64]{0,1:T(8,128)(2,1)} %param.5) | copy-start | bytes 1867780
  1.8 10.0 %collective-permute-start = (bf16[64,1024]{1,0:T(8,128)(2,1)S(1)}, bf16[64,1024]{1,0:T(8,128)(2,1)S(1)}, u32[]{:S(2)}, u32[]{:S(2)}) collective-permute-start(bf16[64,1024]{1,0:T(8,128)(2,1)S(1)} %get-tuple-element.25.refs_4_), channel_id=1, source_target_pairs={{0,2},{1,3},{2,0},{3,1},{4,6},{5,7},{6,4},{7,5},{8,10},{9,11},{10,... | collective-permute-start | bytes 393224 | tf_op jit(solution)/shard_map/ppermute | solution.py:216
  4.8 9.8 %collective-permute-start.1 = (bf16[64,1024]{1,0:T(8,128)(2,1)S(1)}, bf16[64,1024]{1,0:T(8,128)(2,1)S(1)}, u32[]{:S(2)}, u32[]{:S(2)}) collective-permute-start(bf16[64,1024]{1,0:T(8,128)(2,1)S(1)} %get-tuple-element.25.refs_4_), channel_id=1, source_target_pairs={{0,1},{1,0},{2,3},{3,2},{4,5},{5,4},{6,7},{7,6},{8,9},{9,8},{10,11... | collective-permute-start | bytes 393224 | tf_op jit(solution)/shard_map/ppermute | solution.py:219
  4.8 9.8 %collective-permute-start.2 = (bf16[64,3840]{1,0:T(8,128)(2,1)S(1)}, bf16[64,3840]{1,0:T(8,128)(2,1)S(1)}, u32[]{:S(2)}, u32[]{:S(2)}) collective-permute-start(bf16[64,3840]{1,0:T(8,128)(2,1)S(1)} %get-tuple-element.32.refs_6_), channel_id=1, source_target_pairs={{0,1},{1,0},{2,3},{3,2},{4,5},{5,4},{6,7},{7,6},{8,9},{9,8},{10,11... | collective-permute-start | bytes 1474568 | tf_op jit(solution)/shard_map/ppermute | solution.py:219
  5.3 13.5 %collective-permute-start.6 = (bf16[64,3840]{1,0:T(8,128)(2,1)S(1)}, bf16[64,3840]{1,0:T(8,128)(2,1)S(1)}, u32[]{:S(2)}, u32[]{:S(2)}) collective-permute-start(bf16[64,3840]{1,0:T(8,128)(2,1)S(1)} %get-tuple-element.32.refs_6_), channel_id=1, source_target_pairs={{0,2},{1,3},{2,0},{3,1},{4,6},{5,7},{6,4},{7,5},{8,10},{9,11},{10,... | collective-permute-start | bytes 1474568 | tf_op jit(solution)/shard_map/ppermute | solution.py:216
  11.9 7.0 %collective-permute-start.3 = (bf16[128,512]{1,0:T(8,128)(2,1)S(1)}, bf16[128,512]{1,0:T(8,128)(2,1)S(1)}, u32[]{:S(2)}, u32[]{:S(2)}) collective-permute-start(bf16[128,512]{1,0:T(8,128)(2,1)S(1)} %get-tuple-element.49), channel_id=1, source_target_pairs={{0,4},{4,0},{8,12},{12,8},{16,20},{20,16},{24,28},{28,24},{1,5},{5... | collective-permute-start | bytes 393224 | tf_op jit(solution)/shard_map/ppermute | solution.py:222
  13.9 4.9 %collective-permute-start.4 = (bf16[128,512]{1,0:T(8,128)(2,1)S(1)}, bf16[128,512]{1,0:T(8,128)(2,1)S(1)}, u32[]{:S(2)}, u32[]{:S(2)}) collective-permute-start(bf16[128,512]{1,0:T(8,128)(2,1)S(1)} %get-tuple-element.48), channel_id=1, source_target_pairs={{4,8},{12,16},{20,24},{8,4},{16,12},{24,20},{5,9},{13,17},{21,25},... | collective-permute-start | bytes 393224 | tf_op jit(solution)/shard_map/ppermute | solution.py:226
  18.8 7.5 %collective-permute-start.12 = (bf16[64,3840]{1,0:T(8,128)(2,1)S(1)}, bf16[64,3840]{1,0:T(8,128)(2,1)S(1)}, u32[]{:S(2)}, u32[]{:S(2)}) collective-permute-start(bf16[64,3840]{1,0:T(8,128)(2,1)S(1)} %collective-permute-done.6.refs_8_), channel_id=1, source_target_pairs={{0,1},{1,0},{2,3},{3,2},{4,5},{5,4},{6,7},{7,6},{8,9},{9,8},{10,11... | collective-permute-start | bytes 1474568 | tf_op jit(solution)/shard_map/ppermute | solution.py:219
  18.9 2.2 %collective-permute-start.5 = (bf16[128,1024]{1,0:T(8,128)(2,1)S(1)}, bf16[128,1024]{1,0:T(8,128)(2,1)S(1)}, u32[]{:S(2)}, u32[]{:S(2)}) collective-permute-start(bf16[128,1024]{1,0:T(8,128)(2,1)S(1)} %constant_dynamic-update-slice_fusion.2.refs_8_.refs_4_), channel_id=1, source_target_pairs={{0,1},{1,0},{2,3},{3,2},{4,5},{5,4},{6,7},{7,6},{8,9},{9,8},{10,11... | collective-permute-start | bytes 786440 | tf_op jit(solution)/shard_map/ppermute | solution.py:219
  19.5 6.9 %collective-permute-start.11 = (bf16[64,1024]{1,0:T(8,128)(2,1)S(1)}, bf16[64,1024]{1,0:T(8,128)(2,1)S(1)}, u32[]{:S(2)}, u32[]{:S(2)}) collective-permute-start(bf16[64,1024]{1,0:T(8,128)(2,1)S(1)} %collective-permute-done.refs_6_), channel_id=1, source_target_pairs={{0,1},{1,0},{2,3},{3,2},{4,5},{5,4},{6,7},{7,6},{8,9},{9,8},{10,11... | collective-permute-start | bytes 393224 | tf_op jit(solution)/shard_map/ppermute | solution.py:219
  22.7 7.8 %collective-permute-start.7 = (bf16[4,64,256]{2,1,0:T(8,128)(2,1)S(1)}, bf16[4,64,256]{2,1,0:T(8,128)(2,1)S(1)}, u32[]{:S(2)}, u32[]{:S(2)}) collective-permute-start(bf16[4,64,256]{2,1,0:T(8,128)(2,1)S(1)} %get-tuple-element.36), channel_id=1, source_target_pairs={{0,4},{4,0},{8,12},{12,8},{16,20},{20,16},{24,28},{28,24},{1,5},{5... | collective-permute-start | bytes 393224 | tf_op jit(solution)/shard_map/ppermute | solution.py:222
  30.5 5.3 %collective-permute-start.13 = (bf16[4,64,256]{2,1,0:T(8,128)(2,1)S(1)}, bf16[4,64,256]{2,1,0:T(8,128)(2,1)S(1)}, u32[]{:S(2)}, u32[]{:S(2)}) collective-permute-start(bf16[4,64,256]{2,1,0:T(8,128)(2,1)S(1)} %get-tuple-element.43), channel_id=1, source_target_pairs={{0,4},{4,0},{8,12},{12,8},{16,20},{20,16},{24,28},{28,24},{1,5},{5... | collective-permute-start | bytes 393224 | tf_op jit(solution)/shard_map/ppermute | solution.py:222
  30.6 9.3 %collective-permute-start.8 = (bf16[64,256]{1,0:T(8,128)(2,1)S(1)}, bf16[64,256]{1,0:T(8,128)(2,1)S(1)}, u32[]{:S(2)}, u32[]{:S(2)}) collective-permute-start(bf16[64,256]{1,0:T(8,128)(2,1)S(1)} %get-tuple-element.38), channel_id=1, source_target_pairs={{0,8},{4,12},{8,0},{12,4},{16,24},{20,28},{24,16},{28,20},{1,9},{5... | collective-permute-start | bytes 98312 | tf_op jit(solution)/shard_map/ppermute | solution.py:222
  32.9 7.4 %collective-permute-start.9 = (bf16[64,256]{1,0:T(8,128)(2,1)S(1)}, bf16[64,256]{1,0:T(8,128)(2,1)S(1)}, u32[]{:S(2)}, u32[]{:S(2)}) collective-permute-start(bf16[64,256]{1,0:T(8,128)(2,1)S(1)} %get-tuple-element.39), channel_id=1, source_target_pairs={{0,16},{4,20},{8,24},{12,28},{16,0},{20,4},{24,8},{28,12},{1,17},{... | collective-permute-start | bytes 98312 | tf_op jit(solution)/shard_map/ppermute | solution.py:222
  35.5 5.7 %collective-permute-start.10 = (bf16[64,256]{1,0:T(8,128)(2,1)S(1)}, bf16[64,256]{1,0:T(8,128)(2,1)S(1)}, u32[]{:S(2)}, u32[]{:S(2)}) collective-permute-start(bf16[64,256]{1,0:T(8,128)(2,1)S(1)} %get-tuple-element.40), channel_id=1, source_target_pairs={{0,24},{4,28},{8,16},{12,20},{16,8},{20,12},{24,0},{28,4},{1,25},{... | collective-permute-start | bytes 98312 | tf_op jit(solution)/shard_map/ppermute | solution.py:222
  35.8 5.4 %collective-permute-start.14 = (bf16[64,256]{1,0:T(8,128)(2,1)S(1)}, bf16[64,256]{1,0:T(8,128)(2,1)S(1)}, u32[]{:S(2)}, u32[]{:S(2)}) collective-permute-start(bf16[64,256]{1,0:T(8,128)(2,1)S(1)} %get-tuple-element.45), channel_id=1, source_target_pairs={{0,8},{4,12},{8,0},{12,4},{16,24},{20,28},{24,16},{28,20},{1,9},{5... | collective-permute-start | bytes 98312 | tf_op jit(solution)/shard_map/ppermute | solution.py:222
  37.5 5.1 %collective-permute-start.15 = (bf16[64,256]{1,0:T(8,128)(2,1)S(1)}, bf16[64,256]{1,0:T(8,128)(2,1)S(1)}, u32[]{:S(2)}, u32[]{:S(2)}) collective-permute-start(bf16[64,256]{1,0:T(8,128)(2,1)S(1)} %get-tuple-element.46), channel_id=1, source_target_pairs={{0,16},{4,20},{8,24},{12,28},{16,0},{20,4},{24,8},{28,12},{1,17},{... | collective-permute-start | bytes 98312 | tf_op jit(solution)/shard_map/ppermute | solution.py:222
  40.0 5.7 %collective-permute-start.16 = (bf16[64,256]{1,0:T(8,128)(2,1)S(1)}, bf16[64,256]{1,0:T(8,128)(2,1)S(1)}, u32[]{:S(2)}, u32[]{:S(2)}) collective-permute-start(bf16[64,256]{1,0:T(8,128)(2,1)S(1)} %get-tuple-element.47), channel_id=1, source_target_pairs={{0,24},{4,28},{8,16},{12,20},{16,8},{20,12},{24,0},{28,4},{1,25},{... | collective-permute-start | bytes 98312 | tf_op jit(solution)/shard_map/ppermute | solution.py:222

commit v7 on v6

--- a/solution.py
+++ b/solution.py
@@ -234,7 +234,7 @@
     g_blocks, c_blocks = load(g_blocks, c_blocks)
     (basis,) = load(basis)
     ids = jnp.clip(block_cols.T - (lax.axis_index("node") * rows - HB), 0, rows + 2 * HB - 1)
-    far_ends, g_blocks, c_blocks, basis, ids = lax.optimization_barrier((far_ends, g_blocks, c_blocks, basis, ids))
+    far_ends, basis, ids = lax.optimization_barrier((far_ends, basis, ids))
     all_ends = jnp.concatenate([ends, far_ends], axis=0)
     rim = jnp.concatenate([swap(all_ends[:, :halo], 1), swap_next(all_ends[:, halo:])], axis=1)
     fixed = (ids, g_blocks, c_blocks, basis)

time: 46.5 us -> 45.4 us (0.976)
  waiting for transfers between devices: 8.06 us -> 7.17 us
    ppermute x9, waiting for transfers between devices: 5.72 us -> 4.83 us  [swap(): return lax.ppermute(array, 'node', [(i, i ^ step) for i in range(nodes)])]
  transfers between devices with their start and end apart: 17 -> 17, of which waited for: 6 -> 8; matrix products, arithmetic and copies ran while one was open for 2% -> 2% of each run, Pallas kernels for 32% -> 33%
where the time goes in v7:
time: 45.4 us; the launch traced here: 45.2 us
  starting transfers between devices  19.7 us (43%)
  Pallas kernels  15.7 us (35%)
  waiting for transfers between devices  7.17 us (16%)
  local copies, waits for them, and re-layouts  1.13 us (2%)
  between operations  0.77 us (2%)
  other arithmetic  0.69 us (2%)
    ppermute x9, starting transfers between devices, swap(): return lax.ppermute(array, 'node', [(i, i ^ step) for i in range(nodes)])  14.8 us
    pallas_call x3, Pallas kernels, project(): pl.pallas_call(functools.partial(project_kernel, spans, places, groups, b...  9.17 us
    pallas_call x2, Pallas kernels, load(): pl.pallas_call(load_kernel, out_shape=[shape(array.shape, array.dtype) fo...  5.7 us
    ppermute x9, waiting for transfers between devices, swap(): return lax.ppermute(array, 'node', [(i, i ^ step) for i in range(nodes)])  4.83 us
    ppermute x2, starting transfers between devices, across(): return lax.ppermute(array, 'col', [(i, i ^ 2) for i in range(cols)])  3.08 us
    ppermute x5, waiting for transfers between devices, cores(): return lax.ppermute(array, 'col', [(i, i ^ 1) for i in range(cols)])  1.55 us
    ppermute x5, starting transfers between devices, cores(): return lax.ppermute(array, 'col', [(i, i ^ 1) for i in range(cols)])  1.16 us
    unnamed x4, local copies, waits for them, and re-layouts  1.09 us
  transfers between devices with their start and end apart: 17, of which 8 were waited for; matrix products, arithmetic and copies ran while one was open for 2% of the time, Pallas kernels for 33%

profile of v7, /device:TPU:0, one launch (start us, length us, event | category | flops | bytes accessed | tf_op | source)
XLA Modules:
  0.0 45.2 jit_solution(2833412538585268145)
XLA Ops:
  0.6 1.1 %copy-done = bf16[4864,64]{0,1:T(8,128)(2,1)S(1)} copy-done((bf16[4864,64]{0,1:T(8,128)(2,1)S(1)}, bf16[4864,64]{0,1:T(8,128)(2,1)}, u32[]{:S(2)}) %copy-start) | copy-done | bytes 622616
  1.8 3.0 %collective-permute-start = (bf16[64,1024]{1,0:T(8,128)(2,1)S(1)}, bf16[64,1024]{1,0:T(8,128)(2,1)S(1)}, u32[]{:S(2)}, u32[]{:S(2)}) collective-permute-start(bf16[64,1024]{1,0:T(8,128)(2,1)S(1)} %get-tuple-element.23.refs_4_), channel_id=1, source_target_pairs={{0,2},{1,3},{2,0},{3,1},{4,6},{5,7},{6,4},{7,5},{8,10},{9,11},{10,... | collective-permute-start | bytes 393224 | tf_op jit(solution)/shard_map/ppermute | solution.py:216
  5.4 0.7 %clamp_bitcast_fusion.refs_0_ = s32[3,38]{1,0:T(4,128)S(1)} fusion(s32[38,3]{0,1:T(4,128)} %param.9, s32[]{:T(128)S(6)} %sub.10), kind=kLoop, calls=%fused_computation.4 | loop fusion | flops 228 | bytes 916 | tf_op jit(solution)/shard_map/jit(clip)/min | solution.py:236
  6.1 2.5 %shard_map.69.refs_3_ = bf16[4864,512]{1,0:T(8,128)(2,1)S(1)} custom-call(bf16[4864,512]{1,0:T(8,128)(2,1)} %refs_0_.2), custom_call_target="tpu_custom_call" | custom-call | bytes 4980736 | tf_op jit(solution)/shard_map/pallas_call | solution.py:76
  8.8 2.1 %collective-permute-start.3 = (bf16[128,512]{1,0:T(8,128)(2,1)S(1)}, bf16[128,512]{1,0:T(8,128)(2,1)S(1)}, u32[]{:S(2)}, u32[]{:S(2)}) collective-permute-start(bf16[128,512]{1,0:T(8,128)(2,1)S(1)} %get-tuple-element.45), channel_id=1, source_target_pairs={{0,4},{4,0},{8,12},{12,8},{16,20},{20,16},{24,28},{28,24},{1,5},{5... | collective-permute-start | bytes 393224 | tf_op jit(solution)/shard_map/ppermute | solution.py:222
  10.8 0.7 %collective-permute-start.4 = (bf16[128,512]{1,0:T(8,128)(2,1)S(1)}, bf16[128,512]{1,0:T(8,128)(2,1)S(1)}, u32[]{:S(2)}, u32[]{:S(2)}) collective-permute-start(bf16[128,512]{1,0:T(8,128)(2,1)S(1)} %get-tuple-element.44), channel_id=1, source_target_pairs={{4,8},{12,16},{20,24},{8,4},{16,12},{24,20},{5,9},{13,17},{21,25},... | collective-permute-start | bytes 393224 | tf_op jit(solution)/shard_map/ppermute | solution.py:226
  11.5 3.2 %shard_map.70 = (bf16[38,3,128,128]{3,2,1,0:T(8,128)(2,1)S(1)}, bf16[38,3,128,128]{3,2,1,0:T(8,128)(2,1)S(1)}) custom-call(bf16[38,3,128,128]{3,2,1,0:T(8,128)(2,1)} %refs_0_.3, bf16[38,3,128,128]{3,2,1,0:T(8,128)(2,1)} %refs_1_.1), custom_call_target="tpu_custom_call" | custom-call | bytes 7471104 | tf_op jit(solution)/shard_map/pallas_call | solution.py:76
  14.7 3.4 %shard_map.71.refs_10_ = f32[512,256]{1,0:T(8,128)S(1)} custom-call(s32[3,38]{1,0:T(4,128)S(1)} %clamp_bitcast_fusion.refs_0_, bf16[38,3,128,128]{3,2,1,0:T(8,128)(2,1)S(1)} %get-tuple-element.25.refs_1_, bf16[38,3,128,128]{3,2,1,0:T(8,128)(2,1)S(1)} %get-tuple-element.26.refs_2_, bf16[4864,512]{1,0:T(8,128)(2,1)S(1)} %shard_map.69.refs_3_, ...), custom_call_target="tpu_custom_call" | custom-call | flops 30 | bytes 30 | tf_op jit(solution)/shard_map/pallas_call | solution.py:149
  18.2 0.7 %collective-permute-done.6.refs_8_ = bf16[64,3840]{1,0:T(8,128)(2,1)S(1)} collective-permute-done((bf16[64,3840]{1,0:T(8,128)(2,1)S(1)}, bf16[64,3840]{1,0:T(8,128)(2,1)S(1)}, u32[]{:S(2)}, u32[]{:S(2)}) %collective-permute-start.6) | collective-permute-done | bytes 491552 | tf_op jit(solution)/shard_map/ppermute | solution.py:216
  18.9 0.6 %collective-permute-start.5 = (bf16[128,1024]{1,0:T(8,128)(2,1)S(1)}, bf16[128,1024]{1,0:T(8,128)(2,1)S(1)}, u32[]{:S(2)}, u32[]{:S(2)}) collective-permute-start(bf16[128,1024]{1,0:T(8,128)(2,1)S(1)} %constant_dynamic-update-slice_fusion.2.refs_8_.refs_4_), channel_id=1, source_target_pairs={{0,1},{1,0},{2,3},{3,2},{4,5},{5,4},{6,7},{7,6},{8,9},{9,8},{10,11... | collective-permute-start | bytes 786440 | tf_op jit(solution)/shard_map/ppermute | solution.py:219
  19.5 1.5 %collective-permute-done.5.refs_9_.refs_5_ = bf16[128,1024]{1,0:T(8,128)(2,1)S(1)} collective-permute-done((bf16[128,1024]{1,0:T(8,128)(2,1)S(1)}, bf16[128,1024]{1,0:T(8,128)(2,1)S(1)}, u32[]{:S(2)}, u32[]{:S(2)}) %collective-permute-start.5) | collective-permute-done | bytes 262176 | tf_op jit(solution)/shard_map/ppermute | solution.py:219
  21.1 1.6 %shard_map.72 = (bf16[4,64,256]{2,1,0:T(8,128)(2,1)S(1)}, f32[4,64,256]{2,1,0:T(8,128)S(1)}) custom-call(s32[3,38]{1,0:T(4,128)S(1)} %clamp_bitcast_fusion.refs_0_, bf16[38,3,128,128]{3,2,1,0:T(8,128)(2,1)S(1)} %get-tuple-element.25.refs_1_, bf16[38,3,128,128]{3,2,1,0:T(8,128)(2,1)S(1)} %get-tuple-element.26.refs_2_, ...), custom_call_target="tpu_custom_call" | custom-call | flops 8 | bytes 8 | tf_op jit(solution)/shard_map/pallas_call | solution.py:149
  22.7 3.8 %collective-permute-start.7 = (bf16[4,64,256]{2,1,0:T(8,128)(2,1)S(1)}, bf16[4,64,256]{2,1,0:T(8,128)(2,1)S(1)}, u32[]{:S(2)}, u32[]{:S(2)}) collective-permute-start(bf16[4,64,256]{2,1,0:T(8,128)(2,1)S(1)} %get-tuple-element.32), channel_id=1, source_target_pairs={{0,4},{4,0},{8,12},{12,8},{16,20},{20,16},{24,28},{28,24},{1,5},{5... | collective-permute-start | bytes 393224 | tf_op jit(solution)/shard_map/ppermute | solution.py:222
  26.5 4.1 %shard_map.74 = (bf16[4,64,256]{2,1,0:T(8,128)(2,1)S(1)}, f32[4,64,256]{2,1,0:T(8,128)S(1)}) custom-call(s32[3,38]{1,0:T(4,128)S(1)} %clamp_bitcast_fusion.refs_0_, bf16[38,3,128,128]{3,2,1,0:T(8,128)(2,1)S(1)} %get-tuple-element.25.refs_1_, bf16[38,3,128,128]{3,2,1,0:T(8,128)(2,1)S(1)} %get-tuple-element.26.refs_2_, ...), custom_call_target="tpu_custom_call" | custom-call | flops 38 | bytes 38 | tf_op jit(solution)/shard_map/pallas_call | solution.py:149
  30.7 1.6 %collective-permute-start.8 = (bf16[64,256]{1,0:T(8,128)(2,1)S(1)}, bf16[64,256]{1,0:T(8,128)(2,1)S(1)}, u32[]{:S(2)}, u32[]{:S(2)}) collective-permute-start(bf16[64,256]{1,0:T(8,128)(2,1)S(1)} %get-tuple-element.34), channel_id=1, source_target_pairs={{0,8},{4,12},{8,0},{12,4},{16,24},{20,28},{24,16},{28,20},{1,9},{5... | collective-permute-start | bytes 98312 | tf_op jit(solution)/shard_map/ppermute | solution.py:222
  32.4 1.9 %collective-permute-start.9 = (bf16[64,256]{1,0:T(8,128)(2,1)S(1)}, bf16[64,256]{1,0:T(8,128)(2,1)S(1)}, u32[]{:S(2)}, u32[]{:S(2)}) collective-permute-start(bf16[64,256]{1,0:T(8,128)(2,1)S(1)} %get-tuple-element.35), channel_id=1, source_target_pairs={{0,16},{4,20},{8,24},{12,28},{16,0},{20,4},{24,8},{28,12},{1,17},{... | collective-permute-start | bytes 98312 | tf_op jit(solution)/shard_map/ppermute | solution.py:222
  34.3 0.9 %collective-permute-start.10 = (bf16[64,256]{1,0:T(8,128)(2,1)S(1)}, bf16[64,256]{1,0:T(8,128)(2,1)S(1)}, u32[]{:S(2)}, u32[]{:S(2)}) collective-permute-start(bf16[64,256]{1,0:T(8,128)(2,1)S(1)} %get-tuple-element.36), channel_id=1, source_target_pairs={{0,24},{4,28},{8,16},{12,20},{16,8},{20,12},{24,0},{28,4},{1,25},{... | collective-permute-start | bytes 98312 | tf_op jit(solution)/shard_map/ppermute | solution.py:222
  35.2 0.7 %collective-permute-done.13.got = bf16[4,64,256]{2,1,0:T(8,128)(2,1)S(1)} collective-permute-done((bf16[4,64,256]{2,1,0:T(8,128)(2,1)S(1)}, bf16[4,64,256]{2,1,0:T(8,128)(2,1)S(1)}, u32[]{:S(2)}, u32[]{:S(2)}) %collective-permute-start.13) | collective-permute-done | bytes 131104 | tf_op jit(solution)/shard_map/ppermute | solution.py:222
  36.0 1.6 %collective-permute-start.14 = (bf16[64,256]{1,0:T(8,128)(2,1)S(1)}, bf16[64,256]{1,0:T(8,128)(2,1)S(1)}, u32[]{:S(2)}, u32[]{:S(2)}) collective-permute-start(bf16[64,256]{1,0:T(8,128)(2,1)S(1)} %get-tuple-element.41), channel_id=1, source_target_pairs={{0,8},{4,12},{8,0},{12,4},{16,24},{20,28},{24,16},{28,20},{1,9},{5... | collective-permute-start | bytes 98312 | tf_op jit(solution)/shard_map/ppermute | solution.py:222
  37.6 1.2 %collective-permute-start.15 = (bf16[64,256]{1,0:T(8,128)(2,1)S(1)}, bf16[64,256]{1,0:T(8,128)(2,1)S(1)}, u32[]{:S(2)}, u32[]{:S(2)}) collective-permute-start(bf16[64,256]{1,0:T(8,128)(2,1)S(1)} %get-tuple-element.42), channel_id=1, source_target_pairs={{0,16},{4,20},{8,24},{12,28},{16,0},{20,4},{24,8},{28,12},{1,17},{... | collective-permute-start | bytes 98312 | tf_op jit(solution)/shard_map/ppermute | solution.py:222
  38.8 1.6 %collective-permute-start.16 = (bf16[64,256]{1,0:T(8,128)(2,1)S(1)}, bf16[64,256]{1,0:T(8,128)(2,1)S(1)}, u32[]{:S(2)}, u32[]{:S(2)}) collective-permute-start(bf16[64,256]{1,0:T(8,128)(2,1)S(1)} %get-tuple-element.43), channel_id=1, source_target_pairs={{0,24},{4,28},{8,16},{12,20},{16,8},{20,12},{24,0},{28,4},{1,25},{... | collective-permute-start | bytes 98312 | tf_op jit(solution)/shard_map/ppermute | solution.py:222
  40.6 2.3 %collective-permute-done.15.refs_6_ = bf16[64,256]{1,0:T(8,128)(2,1)S(1)} collective-permute-done((bf16[64,256]{1,0:T(8,128)(2,1)S(1)}, bf16[64,256]{1,0:T(8,128)(2,1)S(1)}, u32[]{:S(2)}, u32[]{:S(2)}) %collective-permute-start.15) | collective-permute-done | bytes 32800 | tf_op jit(solution)/shard_map/ppermute | solution.py:222
  43.0 1.5 %collective-permute-done.16.refs_7_ = bf16[64,256]{1,0:T(8,128)(2,1)S(1)} collective-permute-done((bf16[64,256]{1,0:T(8,128)(2,1)S(1)}, bf16[64,256]{1,0:T(8,128)(2,1)S(1)}, u32[]{:S(2)}, u32[]{:S(2)}) %collective-permute-start.16) | collective-permute-done | bytes 32800 | tf_op jit(solution)/shard_map/ppermute | solution.py:222
  44.5 0.7 %shard_map.76 = (f32[64,256]{1,0:T(8,128)}, f32[64,256]{1,0:T(8,128)}) custom-call(f32[64,256]{1,0:T(8,128)S(1)} %get-tuple-element.33.refs_0_, bf16[64,256]{1,0:T(8,128)(2,1)S(1)} %collective-permute-done.8.refs_1_, bf16[64,256]{1,0:T(8,128)(2,1)S(1)} %collective-permute-done.9.refs_2_, bf16[64,256]{1,0:T(8,128)(2,1)S(1)} %collective-permute-done.10.refs_3_, ...), custom_call_target="tpu_custom_call" | custom-call | tf_op jit(solution)/shard_map/pallas_call | solution.py:199
  (27 shorter events, 1.4 us)
Async XLA Ops:
  0.6 1.1 %copy-start = (bf16[4864,64]{0,1:T(8,128)(2,1)S(1)}, bf16[4864,64]{0,1:T(8,128)(2,1)}, u32[]{:S(2)}) copy-start(bf16[4864,64]{0,1:T(8,128)(2,1)} %param.5) | copy-start | bytes 1867780
  1.8 6.9 %collective-permute-start = (bf16[64,1024]{1,0:T(8,128)(2,1)S(1)}, bf16[64,1024]{1,0:T(8,128)(2,1)S(1)}, u32[]{:S(2)}, u32[]{:S(2)}) collective-permute-start(bf16[64,1024]{1,0:T(8,128)(2,1)S(1)} %get-tuple-element.23.refs_4_), channel_id=1, source_target_pairs={{0,2},{1,3},{2,0},{3,1},{4,6},{5,7},{6,4},{7,5},{8,10},{9,11},{10,... | collective-permute-start | bytes 393224 | tf_op jit(solution)/shard_map/ppermute | solution.py:216
  4.8 9.9 %collective-permute-start.1 = (bf16[64,1024]{1,0:T(8,128)(2,1)S(1)}, bf16[64,1024]{1,0:T(8,128)(2,1)S(1)}, u32[]{:S(2)}, u32[]{:S(2)}) collective-permute-start(bf16[64,1024]{1,0:T(8,128)(2,1)S(1)} %get-tuple-element.23.refs_4_), channel_id=1, source_target_pairs={{0,1},{1,0},{2,3},{3,2},{4,5},{5,4},{6,7},{7,6},{8,9},{9,8},{10,11... | collective-permute-start | bytes 393224 | tf_op jit(solution)/shard_map/ppermute | solution.py:219
  4.8 9.9 %collective-permute-start.2 = (bf16[64,3840]{1,0:T(8,128)(2,1)S(1)}, bf16[64,3840]{1,0:T(8,128)(2,1)S(1)}, u32[]{:S(2)}, u32[]{:S(2)}) collective-permute-start(bf16[64,3840]{1,0:T(8,128)(2,1)S(1)} %get-tuple-element.28.refs_6_), channel_id=1, source_target_pairs={{0,1},{1,0},{2,3},{3,2},{4,5},{5,4},{6,7},{7,6},{8,9},{9,8},{10,11... | collective-permute-start | bytes 1474568 | tf_op jit(solution)/shard_map/ppermute | solution.py:219
  5.3 13.5 %collective-permute-start.6 = (bf16[64,3840]{1,0:T(8,128)(2,1)S(1)}, bf16[64,3840]{1,0:T(8,128)(2,1)S(1)}, u32[]{:S(2)}, u32[]{:S(2)}) collective-permute-start(bf16[64,3840]{1,0:T(8,128)(2,1)S(1)} %get-tuple-element.28.refs_6_), channel_id=1, source_target_pairs={{0,2},{1,3},{2,0},{3,1},{4,6},{5,7},{6,4},{7,5},{8,10},{9,11},{10,... | collective-permute-start | bytes 1474568 | tf_op jit(solution)/shard_map/ppermute | solution.py:216
  8.8 10.1 %collective-permute-start.3 = (bf16[128,512]{1,0:T(8,128)(2,1)S(1)}, bf16[128,512]{1,0:T(8,128)(2,1)S(1)}, u32[]{:S(2)}, u32[]{:S(2)}) collective-permute-start(bf16[128,512]{1,0:T(8,128)(2,1)S(1)} %get-tuple-element.45), channel_id=1, source_target_pairs={{0,4},{4,0},{8,12},{12,8},{16,20},{20,16},{24,28},{28,24},{1,5},{5... | collective-permute-start | bytes 393224 | tf_op jit(solution)/shard_map/ppermute | solution.py:222
  10.8 8.0 %collective-permute-start.4 = (bf16[128,512]{1,0:T(8,128)(2,1)S(1)}, bf16[128,512]{1,0:T(8,128)(2,1)S(1)}, u32[]{:S(2)}, u32[]{:S(2)}) collective-permute-start(bf16[128,512]{1,0:T(8,128)(2,1)S(1)} %get-tuple-element.44), channel_id=1, source_target_pairs={{4,8},{12,16},{20,24},{8,4},{16,12},{24,20},{5,9},{13,17},{21,25},... | collective-permute-start | bytes 393224 | tf_op jit(solution)/shard_map/ppermute | solution.py:226
  18.8 7.6 %collective-permute-start.12 = (bf16[64,3840]{1,0:T(8,128)(2,1)S(1)}, bf16[64,3840]{1,0:T(8,128)(2,1)S(1)}, u32[]{:S(2)}, u32[]{:S(2)}) collective-permute-start(bf16[64,3840]{1,0:T(8,128)(2,1)S(1)} %collective-permute-done.6.refs_8_), channel_id=1, source_target_pairs={{0,1},{1,0},{2,3},{3,2},{4,5},{5,4},{6,7},{7,6},{8,9},{9,8},{10,11... | collective-permute-start | bytes 1474568 | tf_op jit(solution)/shard_map/ppermute | solution.py:219
  18.9 2.2 %collective-permute-start.5 = (bf16[128,1024]{1,0:T(8,128)(2,1)S(1)}, bf16[128,1024]{1,0:T(8,128)(2,1)S(1)}, u32[]{:S(2)}, u32[]{:S(2)}) collective-permute-start(bf16[128,1024]{1,0:T(8,128)(2,1)S(1)} %constant_dynamic-update-slice_fusion.2.refs_8_.refs_4_), channel_id=1, source_target_pairs={{0,1},{1,0},{2,3},{3,2},{4,5},{5,4},{6,7},{7,6},{8,9},{9,8},{10,11... | collective-permute-start | bytes 786440 | tf_op jit(solution)/shard_map/ppermute | solution.py:219
  19.5 7.0 %collective-permute-start.11 = (bf16[64,1024]{1,0:T(8,128)(2,1)S(1)}, bf16[64,1024]{1,0:T(8,128)(2,1)S(1)}, u32[]{:S(2)}, u32[]{:S(2)}) collective-permute-start(bf16[64,1024]{1,0:T(8,128)(2,1)S(1)} %collective-permute-done.refs_6_), channel_id=1, source_target_pairs={{0,1},{1,0},{2,3},{3,2},{4,5},{5,4},{6,7},{7,6},{8,9},{9,8},{10,11... | collective-permute-start | bytes 393224 | tf_op jit(solution)/shard_map/ppermute | solution.py:219
  22.7 8.0 %collective-permute-start.7 = (bf16[4,64,256]{2,1,0:T(8,128)(2,1)S(1)}, bf16[4,64,256]{2,1,0:T(8,128)(2,1)S(1)}, u32[]{:S(2)}, u32[]{:S(2)}) collective-permute-start(bf16[4,64,256]{2,1,0:T(8,128)(2,1)S(1)} %get-tuple-element.32), channel_id=1, source_target_pairs={{0,4},{4,0},{8,12},{12,8},{16,20},{20,16},{24,28},{28,24},{1,5},{5... | collective-permute-start | bytes 393224 | tf_op jit(solution)/shard_map/ppermute | solution.py:222
  30.6 5.3 %collective-permute-start.13 = (bf16[4,64,256]{2,1,0:T(8,128)(2,1)S(1)}, bf16[4,64,256]{2,1,0:T(8,128)(2,1)S(1)}, u32[]{:S(2)}, u32[]{:S(2)}) collective-permute-start(bf16[4,64,256]{2,1,0:T(8,128)(2,1)S(1)} %get-tuple-element.39), channel_id=1, source_target_pairs={{0,4},{4,0},{8,12},{12,8},{16,20},{20,16},{24,28},{28,24},{1,5},{5... | collective-permute-start | bytes 393224 | tf_op jit(solution)/shard_map/ppermute | solution.py:222
  30.7 8.1 %collective-permute-start.8 = (bf16[64,256]{1,0:T(8,128)(2,1)S(1)}, bf16[64,256]{1,0:T(8,128)(2,1)S(1)}, u32[]{:S(2)}, u32[]{:S(2)}) collective-permute-start(bf16[64,256]{1,0:T(8,128)(2,1)S(1)} %get-tuple-element.34), channel_id=1, source_target_pairs={{0,8},{4,12},{8,0},{12,4},{16,24},{20,28},{24,16},{28,20},{1,9},{5... | collective-permute-start | bytes 98312 | tf_op jit(solution)/shard_map/ppermute | solution.py:222
  32.4 8.0 %collective-permute-start.9 = (bf16[64,256]{1,0:T(8,128)(2,1)S(1)}, bf16[64,256]{1,0:T(8,128)(2,1)S(1)}, u32[]{:S(2)}, u32[]{:S(2)}) collective-permute-start(bf16[64,256]{1,0:T(8,128)(2,1)S(1)} %get-tuple-element.35), channel_id=1, source_target_pairs={{0,16},{4,20},{8,24},{12,28},{16,0},{20,4},{24,8},{28,12},{1,17},{... | collective-permute-start | bytes 98312 | tf_op jit(solution)/shard_map/ppermute | solution.py:222
  34.3 6.2 %collective-permute-start.10 = (bf16[64,256]{1,0:T(8,128)(2,1)S(1)}, bf16[64,256]{1,0:T(8,128)(2,1)S(1)}, u32[]{:S(2)}, u32[]{:S(2)}) collective-permute-start(bf16[64,256]{1,0:T(8,128)(2,1)S(1)} %get-tuple-element.36), channel_id=1, source_target_pairs={{0,24},{4,28},{8,16},{12,20},{16,8},{20,12},{24,0},{28,4},{1,25},{... | collective-permute-start | bytes 98312 | tf_op jit(solution)/shard_map/ppermute | solution.py:222
  36.0 4.7 %collective-permute-start.14 = (bf16[64,256]{1,0:T(8,128)(2,1)S(1)}, bf16[64,256]{1,0:T(8,128)(2,1)S(1)}, u32[]{:S(2)}, u32[]{:S(2)}) collective-permute-start(bf16[64,256]{1,0:T(8,128)(2,1)S(1)} %get-tuple-element.41), channel_id=1, source_target_pairs={{0,8},{4,12},{8,0},{12,4},{16,24},{20,28},{24,16},{28,20},{1,9},{5... | collective-permute-start | bytes 98312 | tf_op jit(solution)/shard_map/ppermute | solution.py:222
  37.6 5.4 %collective-permute-start.15 = (bf16[64,256]{1,0:T(8,128)(2,1)S(1)}, bf16[64,256]{1,0:T(8,128)(2,1)S(1)}, u32[]{:S(2)}, u32[]{:S(2)}) collective-permute-start(bf16[64,256]{1,0:T(8,128)(2,1)S(1)} %get-tuple-element.42), channel_id=1, source_target_pairs={{0,16},{4,20},{8,24},{12,28},{16,0},{20,4},{24,8},{28,12},{1,17},{... | collective-permute-start | bytes 98312 | tf_op jit(solution)/shard_map/ppermute | solution.py:222
  38.8 5.7 %collective-permute-start.16 = (bf16[64,256]{1,0:T(8,128)(2,1)S(1)}, bf16[64,256]{1,0:T(8,128)(2,1)S(1)}, u32[]{:S(2)}, u32[]{:S(2)}) collective-permute-start(bf16[64,256]{1,0:T(8,128)(2,1)S(1)} %get-tuple-element.43), channel_id=1, source_target_pairs={{0,24},{4,28},{8,16},{12,20},{16,8},{20,12},{24,0},{28,4},{1,25},{... | collective-permute-start | bytes 98312 | tf_op jit(solution)/shard_map/ppermute | solution.py:222

commit v8 on v7

--- a/solution.py
+++ b/solution.py
@@ -80,7 +80,7 @@
         out_specs=[VMEM] * len(arrays),
         scratch_shapes=[pltpu.SemaphoreType.DMA((len(arrays), 2))],
         compiler_params=params(45),
-        cost_estimate=pl.CostEstimate(flops=0, bytes_accessed=size, transcendentals=0),
+        cost_estimate=pl.CostEstimate(flops=1 * 10**10, bytes_accessed=size, transcendentals=0),
     )(*arrays)
 
 
@@ -231,7 +231,6 @@
         (ends, cores(ends), 0, [(0, inner, halo, halo), (halo, halo, inner, halo)]),
         (middle, cores(middle), 0, [(0, 2 * halo, 2 * halo, inner - 2 * halo)]),
     ]
-    g_blocks, c_blocks = load(g_blocks, c_blocks)
     (basis,) = load(basis)
     ids = jnp.clip(block_cols.T - (lax.axis_index("node") * rows - HB), 0, rows + 2 * HB - 1)
     far_ends, basis, ids = lax.optimization_barrier((far_ends, basis, ids))

time: 45.4 us -> 50.3 us (1.11)
  local copies, waits for them, and re-layouts: 1.13 us -> 9.89 us
  Pallas kernels: 15.7 us -> 12.6 us
  waiting for transfers between devices: 7.17 us -> 6.37 us
  other arithmetic: 0.69 us -> 0.01 us
  starting transfers between devices: 19.7 us -> 20.3 us
    unnamed x4 -> x18, local copies, waits for them, and re-layouts: 1.09 us -> 9.85 us
    pallas_call x2 -> x1, Pallas kernels: 5.7 us -> 2.48 us  [load(): pl.pallas_call(load_kernel, out_shape=[shape(array.shape, array.dtype) fo...]
    ppermute x2, waiting for transfers between devices: 0.79 us -> 0.01 us  [across(): return lax.ppermute(array, 'col', [(i, i ^ 2) for i in range(cols)])]
    min x1, other arithmetic: 0.69 us -> 0.01 us  [body(): jnp.clip(block_cols.T - (lax.axis_index('node') * rows - HB), 0, rows + 2...]
    ppermute x9, starting transfers between devices: 14.8 us -> 15.4 us  [swap(): return lax.ppermute(array, 'node', [(i, i ^ step) for i in range(nodes)])]
  transfers between devices with their start and end apart: 17 -> 17, of which waited for: 8 -> 6; matrix products, arithmetic and copies ran while one was open for 2% -> 0% of each run, Pallas kernels for 33% -> 24%
where the time goes in v8:
time: 50.3 us; the launch traced here: 50 us
  starting transfers between devices  20.3 us (40%)
  Pallas kernels  12.6 us (25%)
  local copies, waits for them, and re-layouts  9.89 us (20%)
  waiting for transfers between devices  6.37 us (13%)
  between operations  0.85 us (2%)
    ppermute x9, starting transfers between devices, swap(): return lax.ppermute(array, 'node', [(i, i ^ step) for i in range(nodes)])  15.4 us
    unnamed x18, local copies, waits for them, and re-layouts  9.85 us
    pallas_call x3, Pallas kernels, project(): pl.pallas_call(functools.partial(project_kernel, spans, places, groups, b...  9.25 us
    ppermute x9, waiting for transfers between devices, swap(): return lax.ppermute(array, 'node', [(i, i ^ step) for i in range(nodes)])  4.83 us
    ppermute x2, starting transfers between devices, across(): return lax.ppermute(array, 'col', [(i, i ^ 2) for i in range(cols)])  3.08 us
    pallas_call x1, Pallas kernels, load(): pl.pallas_call(load_kernel, out_shape=[shape(array.shape, array.dtype) fo...  2.48 us
    ppermute x5, waiting for transfers between devices, cores(): return lax.ppermute(array, 'col', [(i, i ^ 1) for i in range(cols)])  1.52 us
    ppermute x5, starting transfers between devices, cores(): return lax.ppermute(array, 'col', [(i, i ^ 1) for i in range(cols)])  1.21 us
  transfers between devices with their start and end apart: 17, of which 6 were waited for; matrix products, arithmetic and copies ran while one was open for 0% of the time, Pallas kernels for 24%

profile of v8, /device:TPU:0, one launch (start us, length us, event | category | flops | bytes accessed | tf_op | source)
XLA Modules:
  0.0 50.0 jit_solution(1443634808066064607)
XLA Ops:
  0.6 1.1 %copy-done.6 = bf16[4864,64]{0,1:T(8,128)(2,1)S(1)} copy-done((bf16[4864,64]{0,1:T(8,128)(2,1)S(1)}, bf16[4864,64]{0,1:T(8,128)(2,1)}, u32[]{:S(2)}) %copy-start.6) | copy-done | bytes 622616
  1.8 3.0 %collective-permute-start = (bf16[64,1024]{1,0:T(8,128)(2,1)S(1)}, bf16[64,1024]{1,0:T(8,128)(2,1)S(1)}, u32[]{:S(2)}, u32[]{:S(2)}) collective-permute-start(bf16[64,1024]{1,0:T(8,128)(2,1)S(1)} %get-tuple-element.21.refs_4_), channel_id=1, source_target_pairs={{0,2},{1,3},{2,0},{3,1},{4,6},{5,7},{6,4},{7,5},{8,10},{9,11},{10,... | collective-permute-start | bytes 393224 | tf_op jit(solution)/shard_map/ppermute | solution.py:216
  5.4 2.5 %shard_map.69.refs_3_ = bf16[4864,512]{1,0:T(8,128)(2,1)S(1)} custom-call(bf16[4864,512]{1,0:T(8,128)(2,1)} %refs_0_.1), custom_call_target="tpu_custom_call" | custom-call | flops 10000000000 | bytes 4980736 | tf_op jit(solution)/shard_map/pallas_call | solution.py:76
  7.9 2.2 %copy-done = bf16[4864,512]{1,0:T(8,128)(2,1)} copy-done((bf16[4864,512]{1,0:T(8,128)(2,1)}, bf16[4864,512]{1,0:T(8,128)(2,1)S(1)}, u32[]{:S(2)}) %copy-start) | copy-done | bytes 4980760
  10.2 2.0 %collective-permute-start.3 = (bf16[128,512]{1,0:T(8,128)(2,1)S(1)}, bf16[128,512]{1,0:T(8,128)(2,1)S(1)}, u32[]{:S(2)}, u32[]{:S(2)}) collective-permute-start(bf16[128,512]{1,0:T(8,128)(2,1)S(1)} %get-tuple-element.41), channel_id=1, source_target_pairs={{0,4},{4,0},{8,12},{12,8},{16,20},{20,16},{24,28},{28,24},{1,5},{5... | collective-permute-start | bytes 393224 | tf_op jit(solution)/shard_map/ppermute | solution.py:222
  12.3 0.7 %collective-permute-start.4 = (bf16[128,512]{1,0:T(8,128)(2,1)S(1)}, bf16[128,512]{1,0:T(8,128)(2,1)S(1)}, u32[]{:S(2)}, u32[]{:S(2)}) collective-permute-start(bf16[128,512]{1,0:T(8,128)(2,1)S(1)} %get-tuple-element.40), channel_id=1, source_target_pairs={{4,8},{12,16},{20,24},{8,4},{16,12},{24,20},{5,9},{13,17},{21,25},... | collective-permute-start | bytes 393224 | tf_op jit(solution)/shard_map/ppermute | solution.py:226
  12.9 2.4 %copy-done.1 = bf16[4864,512]{1,0:T(8,128)(2,1)S(1)} copy-done((bf16[4864,512]{1,0:T(8,128)(2,1)S(1)}, bf16[4864,512]{1,0:T(8,128)(2,1)}, u32[]{:S(2)}) %copy-start.1) | copy-done | bytes 4980760
  15.4 2.1 %copy-done.2 = bf16[38,3,128,128]{3,2,1,0:T(8,128)(2,1)S(1)} copy-done((bf16[38,3,128,128]{3,2,1,0:T(8,128)(2,1)S(1)}, bf16[38,3,128,128]{3,2,1,0:T(8,128)(2,1)}, u32[]{:S(2)}) %copy-start.2) | copy-done | bytes 3735576
  17.4 2.1 %copy-done.4 = bf16[38,3,128,128]{3,2,1,0:T(8,128)(2,1)S(1)} copy-done((bf16[38,3,128,128]{3,2,1,0:T(8,128)(2,1)S(1)}, bf16[38,3,128,128]{3,2,1,0:T(8,128)(2,1)}, u32[]{:S(2)}) %copy-start.4) | copy-done | bytes 3735576
  19.5 3.5 %shard_map.70.refs_10_ = f32[512,256]{1,0:T(8,128)S(1)} custom-call(s32[3,38]{1,0:T(4,128)S(1)} %clamp_bitcast_fusion.refs_0_, bf16[38,3,128,128]{3,2,1,0:T(8,128)(2,1)S(1)} %copy-done.2, bf16[38,3,128,128]{3,2,1,0:T(8,128)(2,1)S(1)} %copy-done.4, bf16[4864,512]{1,0:T(8,128)(2,1)S(1)} %copy-done.1, bf16[64,1024]{1,0:T(8,128)(2,1)S(1)} %get-tuple-element.21.refs_4_, ...), custom_call_target="tpu_custom_call" | custom-call | flops 30 | bytes 30 | tf_op jit(solution)/shard_map/pallas_call | solution.py:149
  23.7 1.5 %collective-permute-done.5.refs_9_.refs_5_ = bf16[128,1024]{1,0:T(8,128)(2,1)S(1)} collective-permute-done((bf16[128,1024]{1,0:T(8,128)(2,1)S(1)}, bf16[128,1024]{1,0:T(8,128)(2,1)S(1)}, u32[]{:S(2)}, u32[]{:S(2)}) %collective-permute-start.5) | collective-permute-done | bytes 262176 | tf_op jit(solution)/shard_map/ppermute | solution.py:219
  25.2 1.6 %shard_map.71 = (bf16[4,64,256]{2,1,0:T(8,128)(2,1)S(1)}, f32[4,64,256]{2,1,0:T(8,128)S(1)}) custom-call(s32[3,38]{1,0:T(4,128)S(1)} %clamp_bitcast_fusion.refs_0_, bf16[38,3,128,128]{3,2,1,0:T(8,128)(2,1)S(1)} %copy-done.2, bf16[38,3,128,128]{3,2,1,0:T(8,128)(2,1)S(1)} %copy-done.4, bf16[4864,512]{1,0:T(8,128)(2,1)S(1)} %copy-done.1, ...), custom_call_target="tpu_custom_call" | custom-call | flops 8 | bytes 8 | tf_op jit(solution)/shard_map/pallas_call | solution.py:149
  26.9 4.3 %collective-permute-start.7 = (bf16[4,64,256]{2,1,0:T(8,128)(2,1)S(1)}, bf16[4,64,256]{2,1,0:T(8,128)(2,1)S(1)}, u32[]{:S(2)}, u32[]{:S(2)}) collective-permute-start(bf16[4,64,256]{2,1,0:T(8,128)(2,1)S(1)} %get-tuple-element.28), channel_id=1, source_target_pairs={{0,4},{4,0},{8,12},{12,8},{16,20},{20,16},{24,28},{28,24},{1,5},{5... | collective-permute-start | bytes 393224 | tf_op jit(solution)/shard_map/ppermute | solution.py:222
  31.2 4.2 %shard_map.73 = (bf16[4,64,256]{2,1,0:T(8,128)(2,1)S(1)}, f32[4,64,256]{2,1,0:T(8,128)S(1)}) custom-call(s32[3,38]{1,0:T(4,128)S(1)} %clamp_bitcast_fusion.refs_0_, bf16[38,3,128,128]{3,2,1,0:T(8,128)(2,1)S(1)} %copy-done.3, bf16[38,3,128,128]{3,2,1,0:T(8,128)(2,1)S(1)} %copy-done.5, bf16[4864,512]{1,0:T(8,128)(2,1)S(1)} %copy-done.1, ...), custom_call_target="tpu_custom_call" | custom-call | flops 38 | bytes 38 | tf_op jit(solution)/shard_map/pallas_call | solution.py:149
  35.5 1.6 %collective-permute-start.8 = (bf16[64,256]{1,0:T(8,128)(2,1)S(1)}, bf16[64,256]{1,0:T(8,128)(2,1)S(1)}, u32[]{:S(2)}, u32[]{:S(2)}) collective-permute-start(bf16[64,256]{1,0:T(8,128)(2,1)S(1)} %get-tuple-element.30), channel_id=1, source_target_pairs={{0,8},{4,12},{8,0},{12,4},{16,24},{20,28},{24,16},{28,20},{1,9},{5... | collective-permute-start | bytes 98312 | tf_op jit(solution)/shard_map/ppermute | solution.py:222
  37.2 1.9 %collective-permute-start.9 = (bf16[64,256]{1,0:T(8,128)(2,1)S(1)}, bf16[64,256]{1,0:T(8,128)(2,1)S(1)}, u32[]{:S(2)}, u32[]{:S(2)}) collective-permute-start(bf16[64,256]{1,0:T(8,128)(2,1)S(1)} %get-tuple-element.31), channel_id=1, source_target_pairs={{0,16},{4,20},{8,24},{12,28},{16,0},{20,4},{24,8},{28,12},{1,17},{... | collective-permute-start | bytes 98312 | tf_op jit(solution)/shard_map/ppermute | solution.py:222
  39.1 0.9 %collective-permute-start.10 = (bf16[64,256]{1,0:T(8,128)(2,1)S(1)}, bf16[64,256]{1,0:T(8,128)(2,1)S(1)}, u32[]{:S(2)}, u32[]{:S(2)}) collective-permute-start(bf16[64,256]{1,0:T(8,128)(2,1)S(1)} %get-tuple-element.32), channel_id=1, source_target_pairs={{0,24},{4,28},{8,16},{12,20},{16,8},{20,12},{24,0},{28,4},{1,25},{... | collective-permute-start | bytes 98312 | tf_op jit(solution)/shard_map/ppermute | solution.py:222
  40.0 0.7 %collective-permute-done.13.got = bf16[4,64,256]{2,1,0:T(8,128)(2,1)S(1)} collective-permute-done((bf16[4,64,256]{2,1,0:T(8,128)(2,1)S(1)}, bf16[4,64,256]{2,1,0:T(8,128)(2,1)S(1)}, u32[]{:S(2)}, u32[]{:S(2)}) %collective-permute-start.13) | collective-permute-done | bytes 131104 | tf_op jit(solution)/shard_map/ppermute | solution.py:222
  40.8 1.6 %collective-permute-start.14 = (bf16[64,256]{1,0:T(8,128)(2,1)S(1)}, bf16[64,256]{1,0:T(8,128)(2,1)S(1)}, u32[]{:S(2)}, u32[]{:S(2)}) collective-permute-start(bf16[64,256]{1,0:T(8,128)(2,1)S(1)} %get-tuple-element.37), channel_id=1, source_target_pairs={{0,8},{4,12},{8,0},{12,4},{16,24},{20,28},{24,16},{28,20},{1,9},{5... | collective-permute-start | bytes 98312 | tf_op jit(solution)/shard_map/ppermute | solution.py:222
  42.4 1.2 %collective-permute-start.15 = (bf16[64,256]{1,0:T(8,128)(2,1)S(1)}, bf16[64,256]{1,0:T(8,128)(2,1)S(1)}, u32[]{:S(2)}, u32[]{:S(2)}) collective-permute-start(bf16[64,256]{1,0:T(8,128)(2,1)S(1)} %get-tuple-element.38), channel_id=1, source_target_pairs={{0,16},{4,20},{8,24},{12,28},{16,0},{20,4},{24,8},{28,12},{1,17},{... | collective-permute-start | bytes 98312 | tf_op jit(solution)/shard_map/ppermute | solution.py:222
  43.6 1.6 %collective-permute-start.16 = (bf16[64,256]{1,0:T(8,128)(2,1)S(1)}, bf16[64,256]{1,0:T(8,128)(2,1)S(1)}, u32[]{:S(2)}, u32[]{:S(2)}) collective-permute-start(bf16[64,256]{1,0:T(8,128)(2,1)S(1)} %get-tuple-element.39), channel_id=1, source_target_pairs={{0,24},{4,28},{8,16},{12,20},{16,8},{20,12},{24,0},{28,4},{1,25},{... | collective-permute-start | bytes 98312 | tf_op jit(solution)/shard_map/ppermute | solution.py:222
  45.4 2.3 %collective-permute-done.15.refs_6_ = bf16[64,256]{1,0:T(8,128)(2,1)S(1)} collective-permute-done((bf16[64,256]{1,0:T(8,128)(2,1)S(1)}, bf16[64,256]{1,0:T(8,128)(2,1)S(1)}, u32[]{:S(2)}, u32[]{:S(2)}) %collective-permute-start.15) | collective-permute-done | bytes 32800 | tf_op jit(solution)/shard_map/ppermute | solution.py:222
  47.8 1.5 %collective-permute-done.16.refs_7_ = bf16[64,256]{1,0:T(8,128)(2,1)S(1)} collective-permute-done((bf16[64,256]{1,0:T(8,128)(2,1)S(1)}, bf16[64,256]{1,0:T(8,128)(2,1)S(1)}, u32[]{:S(2)}, u32[]{:S(2)}) %collective-permute-start.16) | collective-permute-done | bytes 32800 | tf_op jit(solution)/shard_map/ppermute | solution.py:222
  49.3 0.7 %shard_map.75 = (f32[64,256]{1,0:T(8,128)}, f32[64,256]{1,0:T(8,128)}) custom-call(f32[64,256]{1,0:T(8,128)S(1)} %get-tuple-element.29.refs_0_, bf16[64,256]{1,0:T(8,128)(2,1)S(1)} %collective-permute-done.8.refs_1_, bf16[64,256]{1,0:T(8,128)(2,1)S(1)} %collective-permute-done.9.refs_2_, bf16[64,256]{1,0:T(8,128)(2,1)S(1)} %collective-permute-done.10.refs_3_, ...), custom_call_target="tpu_custom_call" | custom-call | tf_op jit(solution)/shard_map/pallas_call | solution.py:199
  (40 shorter events, 1.9 us)
Async XLA Ops:
  1.8 8.3 %collective-permute-start = (bf16[64,1024]{1,0:T(8,128)(2,1)S(1)}, bf16[64,1024]{1,0:T(8,128)(2,1)S(1)}, u32[]{:S(2)}, u32[]{:S(2)}) collective-permute-start(bf16[64,1024]{1,0:T(8,128)(2,1)S(1)} %get-tuple-element.21.refs_4_), channel_id=1, source_target_pairs={{0,2},{1,3},{2,0},{3,1},{4,6},{5,7},{6,4},{7,5},{8,10},{9,11},{10,... | collective-permute-start | bytes 393224 | tf_op jit(solution)/shard_map/ppermute | solution.py:216
  4.8 8.1 %collective-permute-start.1 = (bf16[64,1024]{1,0:T(8,128)(2,1)S(1)}, bf16[64,1024]{1,0:T(8,128)(2,1)S(1)}, u32[]{:S(2)}, u32[]{:S(2)}) collective-permute-start(bf16[64,1024]{1,0:T(8,128)(2,1)S(1)} %get-tuple-element.21.refs_4_), channel_id=1, source_target_pairs={{0,1},{1,0},{2,3},{3,2},{4,5},{5,4},{6,7},{7,6},{8,9},{9,8},{10,11... | collective-permute-start | bytes 393224 | tf_op jit(solution)/shard_map/ppermute | solution.py:219
  4.8 8.1 %collective-permute-start.2 = (bf16[64,3840]{1,0:T(8,128)(2,1)S(1)}, bf16[64,3840]{1,0:T(8,128)(2,1)S(1)}, u32[]{:S(2)}, u32[]{:S(2)}) collective-permute-start(bf16[64,3840]{1,0:T(8,128)(2,1)S(1)} %get-tuple-element.24.refs_6_), channel_id=1, source_target_pairs={{0,1},{1,0},{2,3},{3,2},{4,5},{5,4},{6,7},{7,6},{8,9},{9,8},{10,11... | collective-permute-start | bytes 1474568 | tf_op jit(solution)/shard_map/ppermute | solution.py:219
  5.3 17.6 %collective-permute-start.6 = (bf16[64,3840]{1,0:T(8,128)(2,1)S(1)}, bf16[64,3840]{1,0:T(8,128)(2,1)S(1)}, u32[]{:S(2)}, u32[]{:S(2)}) collective-permute-start(bf16[64,3840]{1,0:T(8,128)(2,1)S(1)} %get-tuple-element.24.refs_6_), channel_id=1, source_target_pairs={{0,2},{1,3},{2,0},{3,1},{4,6},{5,7},{6,4},{7,5},{8,10},{9,11},{10,... | collective-permute-start | bytes 1474568 | tf_op jit(solution)/shard_map/ppermute | solution.py:216
  5.4 4.7 %copy-start.7 = (s32[38,3]{0,1:T(4,128)S(1)}, s32[38,3]{0,1:T(4,128)}, u32[]{:S(2)}) copy-start(s32[38,3]{0,1:T(4,128)} %param.9) | copy-start | bytes 1372
  7.9 2.2 %copy-start = (bf16[4864,512]{1,0:T(8,128)(2,1)}, bf16[4864,512]{1,0:T(8,128)(2,1)S(1)}, u32[]{:S(2)}) copy-start(bf16[4864,512]{1,0:T(8,128)(2,1)S(1)} %shard_map.69.refs_3_) | copy-start | bytes 14942212
  10.2 12.8 %collective-permute-start.3 = (bf16[128,512]{1,0:T(8,128)(2,1)S(1)}, bf16[128,512]{1,0:T(8,128)(2,1)S(1)}, u32[]{:S(2)}, u32[]{:S(2)}) collective-permute-start(bf16[128,512]{1,0:T(8,128)(2,1)S(1)} %get-tuple-element.41), channel_id=1, source_target_pairs={{0,4},{4,0},{8,12},{12,8},{16,20},{20,16},{24,28},{28,24},{1,5},{5... | collective-permute-start | bytes 393224 | tf_op jit(solution)/shard_map/ppermute | solution.py:222
  12.3 10.8 %collective-permute-start.4 = (bf16[128,512]{1,0:T(8,128)(2,1)S(1)}, bf16[128,512]{1,0:T(8,128)(2,1)S(1)}, u32[]{:S(2)}, u32[]{:S(2)}) collective-permute-start(bf16[128,512]{1,0:T(8,128)(2,1)S(1)} %get-tuple-element.40), channel_id=1, source_target_pairs={{4,8},{12,16},{20,24},{8,4},{16,12},{24,20},{5,9},{13,17},{21,25},... | collective-permute-start | bytes 393224 | tf_op jit(solution)/shard_map/ppermute | solution.py:226
  12.9 2.4 %copy-start.1 = (bf16[4864,512]{1,0:T(8,128)(2,1)S(1)}, bf16[4864,512]{1,0:T(8,128)(2,1)}, u32[]{:S(2)}) copy-start(bf16[4864,512]{1,0:T(8,128)(2,1)} %copy-done) | copy-start | bytes 14942212
  15.3 2.1 %copy-start.2 = (bf16[38,3,128,128]{3,2,1,0:T(8,128)(2,1)S(1)}, bf16[38,3,128,128]{3,2,1,0:T(8,128)(2,1)}, u32[]{:S(2)}) copy-start(bf16[38,3,128,128]{3,2,1,0:T(8,128)(2,1)} %refs_1_.5) | copy-start | bytes 11206660
  17.4 2.1 %copy-start.4 = (bf16[38,3,128,128]{3,2,1,0:T(8,128)(2,1)S(1)}, bf16[38,3,128,128]{3,2,1,0:T(8,128)(2,1)}, u32[]{:S(2)}) copy-start(bf16[38,3,128,128]{3,2,1,0:T(8,128)(2,1)} %refs_2_.5) | copy-start | bytes 11206660
  22.9 8.3 %collective-permute-start.12 = (bf16[64,3840]{1,0:T(8,128)(2,1)S(1)}, bf16[64,3840]{1,0:T(8,128)(2,1)S(1)}, u32[]{:S(2)}, u32[]{:S(2)}) collective-permute-start(bf16[64,3840]{1,0:T(8,128)(2,1)S(1)} %collective-permute-done.6.refs_8_), channel_id=1, source_target_pairs={{0,1},{1,0},{2,3},{3,2},{4,5},{5,4},{6,7},{7,6},{8,9},{9,8},{10,11... | collective-permute-start | bytes 1474568 | tf_op jit(solution)/shard_map/ppermute | solution.py:219
  23.1 8.1 %copy-start.3 = (bf16[38,3,128,128]{3,2,1,0:T(8,128)(2,1)S(1)}, bf16[38,3,128,128]{3,2,1,0:T(8,128)(2,1)}, u32[]{:S(2)}) copy-start(bf16[38,3,128,128]{3,2,1,0:T(8,128)(2,1)} %refs_1_.5) | copy-start | bytes 11206660
  23.1 8.1 %copy-start.5 = (bf16[38,3,128,128]{3,2,1,0:T(8,128)(2,1)S(1)}, bf16[38,3,128,128]{3,2,1,0:T(8,128)(2,1)}, u32[]{:S(2)}) copy-start(bf16[38,3,128,128]{3,2,1,0:T(8,128)(2,1)} %refs_2_.5) | copy-start | bytes 11206660
  23.1 2.1 %collective-permute-start.5 = (bf16[128,1024]{1,0:T(8,128)(2,1)S(1)}, bf16[128,1024]{1,0:T(8,128)(2,1)S(1)}, u32[]{:S(2)}, u32[]{:S(2)}) collective-permute-start(bf16[128,1024]{1,0:T(8,128)(2,1)S(1)} %constant_dynamic-update-slice_fusion.2.refs_8_.refs_4_), channel_id=1, source_target_pairs={{0,1},{1,0},{2,3},{3,2},{4,5},{5,4},{6,7},{7,6},{8,9},{9,8},{10,11... | collective-permute-start | bytes 786440 | tf_op jit(solution)/shard_map/ppermute | solution.py:219
  23.7 7.5 %collective-permute-start.11 = (bf16[64,1024]{1,0:T(8,128)(2,1)S(1)}, bf16[64,1024]{1,0:T(8,128)(2,1)S(1)}, u32[]{:S(2)}, u32[]{:S(2)}) collective-permute-start(bf16[64,1024]{1,0:T(8,128)(2,1)S(1)} %collective-permute-done.refs_6_), channel_id=1, source_target_pairs={{0,1},{1,0},{2,3},{3,2},{4,5},{5,4},{6,7},{7,6},{8,9},{9,8},{10,11... | collective-permute-start | bytes 393224 | tf_op jit(solution)/shard_map/ppermute | solution.py:219
  26.9 8.6 %collective-permute-start.7 = (bf16[4,64,256]{2,1,0:T(8,128)(2,1)S(1)}, bf16[4,64,256]{2,1,0:T(8,128)(2,1)S(1)}, u32[]{:S(2)}, u32[]{:S(2)}) collective-permute-start(bf16[4,64,256]{2,1,0:T(8,128)(2,1)S(1)} %get-tuple-element.28), channel_id=1, source_target_pairs={{0,4},{4,0},{8,12},{12,8},{16,20},{20,16},{24,28},{28,24},{1,5},{5... | collective-permute-start | bytes 393224 | tf_op jit(solution)/shard_map/ppermute | solution.py:222
  35.4 5.3 %collective-permute-start.13 = (bf16[4,64,256]{2,1,0:T(8,128)(2,1)S(1)}, bf16[4,64,256]{2,1,0:T(8,128)(2,1)S(1)}, u32[]{:S(2)}, u32[]{:S(2)}) collective-permute-start(bf16[4,64,256]{2,1,0:T(8,128)(2,1)S(1)} %get-tuple-element.35), channel_id=1, source_target_pairs={{0,4},{4,0},{8,12},{12,8},{16,20},{20,16},{24,28},{28,24},{1,5},{5... | collective-permute-start | bytes 393224 | tf_op jit(solution)/shard_map/ppermute | solution.py:222
  35.5 8.1 %collective-permute-start.8 = (bf16[64,256]{1,0:T(8,128)(2,1)S(1)}, bf16[64,256]{1,0:T(8,128)(2,1)S(1)}, u32[]{:S(2)}, u32[]{:S(2)}) collective-permute-start(bf16[64,256]{1,0:T(8,128)(2,1)S(1)} %get-tuple-element.30), channel_id=1, source_target_pairs={{0,8},{4,12},{8,0},{12,4},{16,24},{20,28},{24,16},{28,20},{1,9},{5... | collective-permute-start | bytes 98312 | tf_op jit(solution)/shard_map/ppermute | solution.py:222
  37.2 8.0 %collective-permute-start.9 = (bf16[64,256]{1,0:T(8,128)(2,1)S(1)}, bf16[64,256]{1,0:T(8,128)(2,1)S(1)}, u32[]{:S(2)}, u32[]{:S(2)}) collective-permute-start(bf16[64,256]{1,0:T(8,128)(2,1)S(1)} %get-tuple-element.31), channel_id=1, source_target_pairs={{0,16},{4,20},{8,24},{12,28},{16,0},{20,4},{24,8},{28,12},{1,17},{... | collective-permute-start | bytes 98312 | tf_op jit(solution)/shard_map/ppermute | solution.py:222
  39.1 6.2 %collective-permute-start.10 = (bf16[64,256]{1,0:T(8,128)(2,1)S(1)}, bf16[64,256]{1,0:T(8,128)(2,1)S(1)}, u32[]{:S(2)}, u32[]{:S(2)}) collective-permute-start(bf16[64,256]{1,0:T(8,128)(2,1)S(1)} %get-tuple-element.32), channel_id=1, source_target_pairs={{0,24},{4,28},{8,16},{12,20},{16,8},{20,12},{24,0},{28,4},{1,25},{... | collective-permute-start | bytes 98312 | tf_op jit(solution)/shard_map/ppermute | solution.py:222
  40.8 4.7 %collective-permute-start.14 = (bf16[64,256]{1,0:T(8,128)(2,1)S(1)}, bf16[64,256]{1,0:T(8,128)(2,1)S(1)}, u32[]{:S(2)}, u32[]{:S(2)}) collective-permute-start(bf16[64,256]{1,0:T(8,128)(2,1)S(1)} %get-tuple-element.37), channel_id=1, source_target_pairs={{0,8},{4,12},{8,0},{12,4},{16,24},{20,28},{24,16},{28,20},{1,9},{5... | collective-permute-start | bytes 98312 | tf_op jit(solution)/shard_map/ppermute | solution.py:222
  42.4 5.4 %collective-permute-start.15 = (bf16[64,256]{1,0:T(8,128)(2,1)S(1)}, bf16[64,256]{1,0:T(8,128)(2,1)S(1)}, u32[]{:S(2)}, u32[]{:S(2)}) collective-permute-start(bf16[64,256]{1,0:T(8,128)(2,1)S(1)} %get-tuple-element.38), channel_id=1, source_target_pairs={{0,16},{4,20},{8,24},{12,28},{16,0},{20,4},{24,8},{28,12},{1,17},{... | collective-permute-start | bytes 98312 | tf_op jit(solution)/shard_map/ppermute | solution.py:222
  43.6 5.7 %collective-permute-start.16 = (bf16[64,256]{1,0:T(8,128)(2,1)S(1)}, bf16[64,256]{1,0:T(8,128)(2,1)S(1)}, u32[]{:S(2)}, u32[]{:S(2)}) collective-permute-start(bf16[64,256]{1,0:T(8,128)(2,1)S(1)} %get-tuple-element.39), channel_id=1, source_target_pairs={{0,24},{4,28},{8,16},{12,20},{16,8},{20,12},{24,0},{28,4},{1,25},{... | collective-permute-start | bytes 98312 | tf_op jit(solution)/shard_map/ppermute | solution.py:222
  (1 other events, 1.1 us)

commit v9 on v8

--- a/solution.py
+++ b/solution.py
@@ -80,7 +80,7 @@
         out_specs=[VMEM] * len(arrays),
         scratch_shapes=[pltpu.SemaphoreType.DMA((len(arrays), 2))],
         compiler_params=params(45),
-        cost_estimate=pl.CostEstimate(flops=1 * 10**10, bytes_accessed=size, transcendentals=0),
+        cost_estimate=pl.CostEstimate(flops=0, bytes_accessed=size * 1, transcendentals=0),
     )(*arrays)
 
 
@@ -95,8 +95,8 @@
     core = lax.axis_index("col") % 2
     odd = lax.axis_index("node") % 2
 
-    for which, (base, parts) in enumerate(places):
-        for owner, ref in ((core, pieces[2 * which]), (1 - core, pieces[2 * which + 1])):
+    for which, (bases, parts) in enumerate(places):
+        for owner, base, ref in zip((core, 1 - core), bases, pieces[2 * which:2 * which + 2]):
             at = pl.ds(pl.multiple_of(owner * width, width), width)
             for source, even_target, odd_target, count in parts:
                 target = even_target
@@ -156,7 +156,7 @@
             pltpu.VMEM((count * BS, 4 * width), BF16),
         ],
         compiler_params=params(14),
-        cost_estimate=pl.CostEstimate(flops=count, bytes_accessed=count, transcendentals=0),
+        cost_estimate=pl.CostEstimate(flops=int(2.3e+09) if more else (count if last else int(1)), bytes_accessed=count, transcendentals=0),
     )(ids, g_blocks, c_blocks, basis, *arrays, *more)
 
 
@@ -227,28 +227,29 @@
 
     ends, middle = cut(panel.T)
     far_ends, far_middle = across(ends), across(middle)
+    ends_other = cores(ends)
     own = [
-        (ends, cores(ends), 0, [(0, inner, halo, halo), (halo, halo, inner, halo)]),
-        (middle, cores(middle), 0, [(0, 2 * halo, 2 * halo, inner - 2 * halo)]),
+        (ends, ends_other, (0, 0), [(0, inner, halo, halo), (halo, halo, inner, halo)]),
+        (middle, cores(middle), (0, 0), [(0, 2 * halo, 2 * halo, inner - 2 * halo)]),
     ]
     (basis,) = load(basis)
     ids = jnp.clip(block_cols.T - (lax.axis_index("node") * rows - HB), 0, rows + 2 * HB - 1)
     far_ends, basis, ids = lax.optimization_barrier((far_ends, basis, ids))
-    all_ends = jnp.concatenate([ends, far_ends], axis=0)
+    all_ends = jnp.concatenate([ends, ends_other, far_ends], axis=0)
     rim = jnp.concatenate([swap(all_ends[:, :halo], 1), swap_next(all_ends[:, halo:])], axis=1)
     fixed = (ids, g_blocks, c_blocks, basis)
     (part,) = project(fixed, own, [(HB, rows - HB)], groups, last=False)
     part, far_middle = lax.optimization_barrier((part, far_middle))
-    rim_other = cores(rim)
+    far_rim = 2 * ROWS_OF_CORE
     rim_parts = [(0, halo + inner, 0, halo), (halo, 0, halo + inner, halo)]
     send_a, keep_a = project(
-        fixed, own + [(rim, rim_other, 0, rim_parts)], [(0, HB), (rows - HB, rows)], groups, before=part
+        fixed, own + [(rim, rim, (0, ROWS_OF_CORE), rim_parts)], [(0, HB), (rows - HB, rows)], groups, before=part
     )
     got_a = swap(send_a, 1)
     far = [
-        (rim, rim_other, ROWS_OF_CORE, rim_parts),
-        (far_ends, cores(far_ends), 0, [(0, inner, halo, halo), (halo, halo, inner, halo)]),
-        (far_middle, cores(far_middle), 0, [(0, 2 * halo, 2 * halo, inner - 2 * halo)]),
+        (rim, cores(rim[far_rim:]), (far_rim, 0), rim_parts),
+        (far_ends, cores(far_ends), (0, 0), [(0, inner, halo, halo), (halo, halo, inner, halo)]),
+        (far_middle, cores(far_middle), (0, 0), [(0, 2 * halo, 2 * halo, inner - 2 * halo)]),
     ]
     send_b, keep_b = project(fixed, far, [(0, rows)], groups)
     got_b = swap(send_b, 1)

time: 50.3 us -> 43.6 us (0.87)
  local copies, waits for them, and re-layouts: 9.89 us -> 1.18 us
  waiting for transfers between devices: 6.37 us -> 9.7 us
  starting transfers between devices: 20.3 us -> 18.5 us
  other arithmetic: 0.01 us -> 0.69 us
    unnamed x18 -> x9, local copies, waits for them, and re-layouts: 9.85 us -> 1.11 us
    ppermute x2, waiting for transfers between devices: 0.01 us -> 3.84 us  [across(): return lax.ppermute(array, 'col', [(i, i ^ 2) for i in range(cols)])]
    ppermute x9, starting transfers between devices: 15.4 us -> 13.6 us  [swap(): return lax.ppermute(array, 'node', [(i, i ^ step) for i in range(nodes)])]
    ppermute x5, waiting for transfers between devices: 1.52 us -> 0.01 us  [cores(): return lax.ppermute(array, 'col', [(i, i ^ 1) for i in range(cols)])]
    ppermute x9, waiting for transfers between devices: 4.83 us -> 5.85 us  [swap(): return lax.ppermute(array, 'node', [(i, i ^ step) for i in range(nodes)])]
    min x1, other arithmetic: 0.01 us -> 0.69 us  [body(): jnp.clip(block_cols.T - (lax.axis_index('node') * rows - HB), 0, rows + 2...]
  transfers between devices with their start and end apart: 17 -> 17, of which waited for: 6 -> 5; matrix products, arithmetic and copies ran while one was open for 0% -> 2% of each run, Pallas kernels for 24% -> 27%
where the time goes in v9:
time: 43.6 us; the launch traced here: 43.5 us
  starting transfers between devices  18.5 us (42%)
  Pallas kernels  12.6 us (29%)
  waiting for transfers between devices  9.7 us (22%)
  local copies, waits for them, and re-layouts  1.18 us (3%)
  between operations  0.82 us (2%)
  other arithmetic  0.69 us (2%)
    ppermute x9, starting transfers between devices, swap(): return lax.ppermute(array, 'node', [(i, i ^ step) for i in range(nodes)])  13.6 us
    pallas_call x3, Pallas kernels, project(): pl.pallas_call(functools.partial(project_kernel, spans, places, groups, b...  9.17 us
    ppermute x9, waiting for transfers between devices, swap(): return lax.ppermute(array, 'node', [(i, i ^ step) for i in range(nodes)])  5.85 us
    ppermute x2, waiting for transfers between devices, across(): return lax.ppermute(array, 'col', [(i, i ^ 2) for i in range(cols)])  3.84 us
    ppermute x2, starting transfers between devices, across(): return lax.ppermute(array, 'col', [(i, i ^ 2) for i in range(cols)])  3.08 us
    pallas_call x1, Pallas kernels, load(): pl.pallas_call(load_kernel, out_shape=[shape(array.shape, array.dtype) fo...  2.62 us
    unnamed x9, local copies, waits for them, and re-layouts  1.11 us
    ppermute x5, starting transfers between devices, cores(): return lax.ppermute(array, 'col', [(i, i ^ 1) for i in range(cols)])  1.09 us
  transfers between devices with their start and end apart: 17, of which 5 were waited for; matrix products, arithmetic and copies ran while one was open for 2% of the time, Pallas kernels for 27%

profile of v9, /device:TPU:0, one launch (start us, length us, event | category | flops | bytes accessed | tf_op | source)
XLA Modules:
  0.0 43.5 jit_solution(7196726481578325724)
XLA Ops:
  0.6 1.1 %copy-done.2 = bf16[4864,64]{0,1:T(8,128)(2,1)S(1)} copy-done((bf16[4864,64]{0,1:T(8,128)(2,1)S(1)}, bf16[4864,64]{0,1:T(8,128)(2,1)}, u32[]{:S(2)}) %copy-start.2) | copy-done | bytes 622616
  1.8 3.0 %collective-permute-start = (bf16[64,1024]{1,0:T(8,128)(2,1)S(1)}, bf16[64,1024]{1,0:T(8,128)(2,1)S(1)}, u32[]{:S(2)}, u32[]{:S(2)}) collective-permute-start(bf16[64,1024]{1,0:T(8,128)(2,1)S(1)} %get-tuple-element.21.refs_4_), channel_id=1, source_target_pairs={{0,2},{1,3},{2,0},{3,1},{4,6},{5,7},{6,4},{7,5},{8,10},{9,11},{10,... | collective-permute-start | bytes 393224 | tf_op jit(solution)/shard_map/ppermute | solution.py:216
  4.8 0.5 %collective-permute-start.2 = (bf16[64,3840]{1,0:T(8,128)(2,1)S(1)}, bf16[64,3840]{1,0:T(8,128)(2,1)S(1)}, u32[]{:S(2)}, u32[]{:S(2)}) collective-permute-start(bf16[64,3840]{1,0:T(8,128)(2,1)S(1)} %get-tuple-element.24.refs_6_), channel_id=1, source_target_pairs={{0,1},{1,0},{2,3},{3,2},{4,5},{5,4},{6,7},{7,6},{8,9},{9,8},{10,11... | collective-permute-start | bytes 1474568 | tf_op jit(solution)/shard_map/ppermute | solution.py:219
  5.4 0.7 %clamp_bitcast_fusion.refs_0_ = s32[3,38]{1,0:T(4,128)S(1)} fusion(s32[38,3]{0,1:T(4,128)} %param.9, s32[]{:T(128)S(6)} %sub.10), kind=kLoop, calls=%fused_computation.5 | loop fusion | flops 228 | bytes 916 | tf_op jit(solution)/shard_map/jit(clip)/min | solution.py:236
  6.1 2.6 %shard_map.69.refs_3_ = bf16[4864,512]{1,0:T(8,128)(2,1)S(1)} custom-call(bf16[4864,512]{1,0:T(8,128)(2,1)} %refs_0_.1), custom_call_target="tpu_custom_call" | custom-call | bytes 4980736 | tf_op jit(solution)/shard_map/pallas_call | solution.py:76
  8.8 2.0 %collective-permute-start.3 = (bf16[192,512]{1,0:T(8,128)(2,1)S(1)}, bf16[192,512]{1,0:T(8,128)(2,1)S(1)}, u32[]{:S(2)}, u32[]{:S(2)}) collective-permute-start(bf16[192,512]{1,0:T(8,128)(2,1)S(1)} %get-tuple-element.41), channel_id=1, source_target_pairs={{0,4},{4,0},{8,12},{12,8},{16,20},{20,16},{24,28},{28,24},{1,5},{5... | collective-permute-start | bytes 589832 | tf_op jit(solution)/shard_map/ppermute | solution.py:222
  10.9 0.7 %collective-permute-start.4 = (bf16[192,512]{1,0:T(8,128)(2,1)S(1)}, bf16[192,512]{1,0:T(8,128)(2,1)S(1)}, u32[]{:S(2)}, u32[]{:S(2)}) collective-permute-start(bf16[192,512]{1,0:T(8,128)(2,1)S(1)} %get-tuple-element.40), channel_id=1, source_target_pairs={{4,8},{12,16},{20,24},{8,4},{16,12},{24,20},{5,9},{13,17},{21,25},... | collective-permute-start | bytes 589832 | tf_op jit(solution)/shard_map/ppermute | solution.py:226
  11.6 3.4 %shard_map.70.refs_10_ = f32[512,256]{1,0:T(8,128)S(1)} custom-call(s32[3,38]{1,0:T(4,128)S(1)} %clamp_bitcast_fusion.refs_0_, bf16[38,3,128,128]{3,2,1,0:T(8,128)(2,1)S(1)} %copy-done, bf16[38,3,128,128]{3,2,1,0:T(8,128)(2,1)S(1)} %copy-done.1, bf16[4864,512]{1,0:T(8,128)(2,1)S(1)} %shard_map.69.refs_3_, bf16[64,1024]{1,0:T(8,128)(2,1)S(1)} %get-tuple-element.21.refs_4_, ...), custom_call_target="tpu_custom_call" | custom-call | flops 1 | bytes 30 | tf_op jit(solution)/shard_map/pallas_call | solution.py:149
  15.0 3.8 %collective-permute-done.5.refs_8_ = bf16[64,3840]{1,0:T(8,128)(2,1)S(1)} collective-permute-done((bf16[64,3840]{1,0:T(8,128)(2,1)S(1)}, bf16[64,3840]{1,0:T(8,128)(2,1)S(1)}, u32[]{:S(2)}, u32[]{:S(2)}) %collective-permute-start.5) | collective-permute-done | bytes 491552 | tf_op jit(solution)/shard_map/ppermute | solution.py:216
  18.8 0.5 %collective-permute-start.11 = (bf16[64,1024]{1,0:T(8,128)(2,1)S(1)}, bf16[64,1024]{1,0:T(8,128)(2,1)S(1)}, u32[]{:S(2)}, u32[]{:S(2)}) collective-permute-start(bf16[64,1024]{1,0:T(8,128)(2,1)S(1)} %collective-permute-done.refs_6_), channel_id=1, source_target_pairs={{0,1},{1,0},{2,3},{3,2},{4,5},{5,4},{6,7},{7,6},{8,9},{9,8},{10,11... | collective-permute-start | bytes 393224 | tf_op jit(solution)/shard_map/ppermute | solution.py:219
  19.5 1.6 %shard_map.71 = (bf16[4,64,256]{2,1,0:T(8,128)(2,1)S(1)}, f32[4,64,256]{2,1,0:T(8,128)S(1)}) custom-call(s32[3,38]{1,0:T(4,128)S(1)} %clamp_bitcast_fusion.refs_0_, bf16[38,3,128,128]{3,2,1,0:T(8,128)(2,1)S(1)} %copy-done, bf16[38,3,128,128]{3,2,1,0:T(8,128)(2,1)S(1)} %copy-done.1, bf16[4864,512]{1,0:T(8,128)(2,1)S(1)} %shard_map.69.refs_3_, ...), custom_call_target="tpu_custom_call" | custom-call | flops 2300000000 | bytes 8 | tf_op jit(solution)/shard_map/pallas_call | solution.py:149
  21.1 2.3 %collective-permute-start.6 = (bf16[4,64,256]{2,1,0:T(8,128)(2,1)S(1)}, bf16[4,64,256]{2,1,0:T(8,128)(2,1)S(1)}, u32[]{:S(2)}, u32[]{:S(2)}) collective-permute-start(bf16[4,64,256]{2,1,0:T(8,128)(2,1)S(1)} %get-tuple-element.28), channel_id=1, source_target_pairs={{0,4},{4,0},{8,12},{12,8},{16,20},{20,16},{24,28},{28,24},{1,5},{5... | collective-permute-start | bytes 393224 | tf_op jit(solution)/shard_map/ppermute | solution.py:222
  23.5 4.1 %shard_map.73 = (bf16[4,64,256]{2,1,0:T(8,128)(2,1)S(1)}, f32[4,64,256]{2,1,0:T(8,128)S(1)}) custom-call(s32[3,38]{1,0:T(4,128)S(1)} %clamp_bitcast_fusion.refs_0_, bf16[38,3,128,128]{3,2,1,0:T(8,128)(2,1)S(1)} %copy-done, bf16[38,3,128,128]{3,2,1,0:T(8,128)(2,1)S(1)} %copy-done.1, bf16[4864,512]{1,0:T(8,128)(2,1)S(1)} %shard_map.69.refs_3_, ...), custom_call_target="tpu_custom_call" | custom-call | flops 38 | bytes 38 | tf_op jit(solution)/shard_map/pallas_call | solution.py:149
  27.6 0.1 collective-permute-start.13
  27.7 2.1 %collective-permute-start.7 = (bf16[64,256]{1,0:T(8,128)(2,1)S(1)}, bf16[64,256]{1,0:T(8,128)(2,1)S(1)}, u32[]{:S(2)}, u32[]{:S(2)}) collective-permute-start(bf16[64,256]{1,0:T(8,128)(2,1)S(1)} %get-tuple-element.30), channel_id=1, source_target_pairs={{0,8},{4,12},{8,0},{12,4},{16,24},{20,28},{24,16},{28,20},{1,9},{5... | collective-permute-start | bytes 98312 | tf_op jit(solution)/shard_map/ppermute | solution.py:222
  29.8 2.6 %collective-permute-start.8 = (bf16[64,256]{1,0:T(8,128)(2,1)S(1)}, bf16[64,256]{1,0:T(8,128)(2,1)S(1)}, u32[]{:S(2)}, u32[]{:S(2)}) collective-permute-start(bf16[64,256]{1,0:T(8,128)(2,1)S(1)} %get-tuple-element.31), channel_id=1, source_target_pairs={{0,16},{4,20},{8,24},{12,28},{16,0},{20,4},{24,8},{28,12},{1,17},{... | collective-permute-start | bytes 98312 | tf_op jit(solution)/shard_map/ppermute | solution.py:222
  32.4 0.8 %collective-permute-done.13.got = bf16[4,64,256]{2,1,0:T(8,128)(2,1)S(1)} collective-permute-done((bf16[4,64,256]{2,1,0:T(8,128)(2,1)S(1)}, bf16[4,64,256]{2,1,0:T(8,128)(2,1)S(1)}, u32[]{:S(2)}, u32[]{:S(2)}) %collective-permute-start.13) | collective-permute-done | bytes 131104 | tf_op jit(solution)/shard_map/ppermute | solution.py:222
  33.3 1.6 %collective-permute-start.14 = (bf16[64,256]{1,0:T(8,128)(2,1)S(1)}, bf16[64,256]{1,0:T(8,128)(2,1)S(1)}, u32[]{:S(2)}, u32[]{:S(2)}) collective-permute-start(bf16[64,256]{1,0:T(8,128)(2,1)S(1)} %get-tuple-element.37), channel_id=1, source_target_pairs={{0,8},{4,12},{8,0},{12,4},{16,24},{20,28},{24,16},{28,20},{1,9},{5... | collective-permute-start | bytes 98312 | tf_op jit(solution)/shard_map/ppermute | solution.py:222
  34.9 2.1 %collective-permute-start.15 = (bf16[64,256]{1,0:T(8,128)(2,1)S(1)}, bf16[64,256]{1,0:T(8,128)(2,1)S(1)}, u32[]{:S(2)}, u32[]{:S(2)}) collective-permute-start(bf16[64,256]{1,0:T(8,128)(2,1)S(1)} %get-tuple-element.38), channel_id=1, source_target_pairs={{0,16},{4,20},{8,24},{12,28},{16,0},{20,4},{24,8},{28,12},{1,17},{... | collective-permute-start | bytes 98312 | tf_op jit(solution)/shard_map/ppermute | solution.py:222
  37.1 0.7 %collective-permute-start.16 = (bf16[64,256]{1,0:T(8,128)(2,1)S(1)}, bf16[64,256]{1,0:T(8,128)(2,1)S(1)}, u32[]{:S(2)}, u32[]{:S(2)}) collective-permute-start(bf16[64,256]{1,0:T(8,128)(2,1)S(1)} %get-tuple-element.39), channel_id=1, source_target_pairs={{0,24},{4,28},{8,16},{12,20},{16,8},{20,12},{24,0},{28,4},{1,25},{... | collective-permute-start | bytes 98312 | tf_op jit(solution)/shard_map/ppermute | solution.py:222
  37.8 0.7 %collective-permute-done.9.refs_3_ = bf16[64,256]{1,0:T(8,128)(2,1)S(1)} collective-permute-done((bf16[64,256]{1,0:T(8,128)(2,1)S(1)}, bf16[64,256]{1,0:T(8,128)(2,1)S(1)}, u32[]{:S(2)}, u32[]{:S(2)}) %collective-permute-start.9) | collective-permute-done | bytes 32800 | tf_op jit(solution)/shard_map/ppermute | solution.py:222
  38.5 1.5 %collective-permute-done.15.refs_6_ = bf16[64,256]{1,0:T(8,128)(2,1)S(1)} collective-permute-done((bf16[64,256]{1,0:T(8,128)(2,1)S(1)}, bf16[64,256]{1,0:T(8,128)(2,1)S(1)}, u32[]{:S(2)}, u32[]{:S(2)}) %collective-permute-start.15) | collective-permute-done | bytes 32800 | tf_op jit(solution)/shard_map/ppermute | solution.py:222
  40.0 2.8 %collective-permute-done.16.refs_7_ = bf16[64,256]{1,0:T(8,128)(2,1)S(1)} collective-permute-done((bf16[64,256]{1,0:T(8,128)(2,1)S(1)}, bf16[64,256]{1,0:T(8,128)(2,1)S(1)}, u32[]{:S(2)}, u32[]{:S(2)}) %collective-permute-start.16) | collective-permute-done | bytes 32800 | tf_op jit(solution)/shard_map/ppermute | solution.py:222
  42.8 0.7 %shard_map.75 = (f32[64,256]{1,0:T(8,128)}, f32[64,256]{1,0:T(8,128)}) custom-call(f32[64,256]{1,0:T(8,128)S(1)} %get-tuple-element.29.refs_0_, bf16[64,256]{1,0:T(8,128)(2,1)S(1)} %collective-permute-done.7.refs_1_, bf16[64,256]{1,0:T(8,128)(2,1)S(1)} %collective-permute-done.8.refs_2_, bf16[64,256]{1,0:T(8,128)(2,1)S(1)} %collective-permute-done.9.refs_3_, ...), custom_call_target="tpu_custom_call" | custom-call | tf_op jit(solution)/shard_map/pallas_call | solution.py:199
  (32 shorter events, 0.5 us)
Async XLA Ops:
  0.6 1.1 %copy-start.2 = (bf16[4864,64]{0,1:T(8,128)(2,1)S(1)}, bf16[4864,64]{0,1:T(8,128)(2,1)}, u32[]{:S(2)}) copy-start(bf16[4864,64]{0,1:T(8,128)(2,1)} %param.5) | copy-start | bytes 1867780
  1.8 6.9 %collective-permute-start = (bf16[64,1024]{1,0:T(8,128)(2,1)S(1)}, bf16[64,1024]{1,0:T(8,128)(2,1)S(1)}, u32[]{:S(2)}, u32[]{:S(2)}) collective-permute-start(bf16[64,1024]{1,0:T(8,128)(2,1)S(1)} %get-tuple-element.21.refs_4_), channel_id=1, source_target_pairs={{0,2},{1,3},{2,0},{3,1},{4,6},{5,7},{6,4},{7,5},{8,10},{9,11},{10,... | collective-permute-start | bytes 393224 | tf_op jit(solution)/shard_map/ppermute | solution.py:216
  4.8 3.9 %collective-permute-start.1 = (bf16[64,1024]{1,0:T(8,128)(2,1)S(1)}, bf16[64,1024]{1,0:T(8,128)(2,1)S(1)}, u32[]{:S(2)}, u32[]{:S(2)}) collective-permute-start(bf16[64,1024]{1,0:T(8,128)(2,1)S(1)} %get-tuple-element.21.refs_4_), channel_id=1, source_target_pairs={{0,1},{1,0},{2,3},{3,2},{4,5},{5,4},{6,7},{7,6},{8,9},{9,8},{10,11... | collective-permute-start | bytes 393224 | tf_op jit(solution)/shard_map/ppermute | solution.py:219
  4.8 6.7 %collective-permute-start.2 = (bf16[64,3840]{1,0:T(8,128)(2,1)S(1)}, bf16[64,3840]{1,0:T(8,128)(2,1)S(1)}, u32[]{:S(2)}, u32[]{:S(2)}) collective-permute-start(bf16[64,3840]{1,0:T(8,128)(2,1)S(1)} %get-tuple-element.24.refs_6_), channel_id=1, source_target_pairs={{0,1},{1,0},{2,3},{3,2},{4,5},{5,4},{6,7},{7,6},{8,9},{9,8},{10,11... | collective-permute-start | bytes 1474568 | tf_op jit(solution)/shard_map/ppermute | solution.py:219
  5.3 13.5 %collective-permute-start.5 = (bf16[64,3840]{1,0:T(8,128)(2,1)S(1)}, bf16[64,3840]{1,0:T(8,128)(2,1)S(1)}, u32[]{:S(2)}, u32[]{:S(2)}) collective-permute-start(bf16[64,3840]{1,0:T(8,128)(2,1)S(1)} %get-tuple-element.24.refs_6_), channel_id=1, source_target_pairs={{0,2},{1,3},{2,0},{3,1},{4,6},{5,7},{6,4},{7,5},{8,10},{9,11},{10,... | collective-permute-start | bytes 1474568 | tf_op jit(solution)/shard_map/ppermute | solution.py:216
  6.1 5.5 %copy-start = (bf16[38,3,128,128]{3,2,1,0:T(8,128)(2,1)S(1)}, bf16[38,3,128,128]{3,2,1,0:T(8,128)(2,1)}, u32[]{:S(2)}) copy-start(bf16[38,3,128,128]{3,2,1,0:T(8,128)(2,1)} %refs_1_.5) | copy-start | bytes 11206660
  6.1 5.5 %copy-start.1 = (bf16[38,3,128,128]{3,2,1,0:T(8,128)(2,1)S(1)}, bf16[38,3,128,128]{3,2,1,0:T(8,128)(2,1)}, u32[]{:S(2)}) copy-start(bf16[38,3,128,128]{3,2,1,0:T(8,128)(2,1)} %refs_2_.5) | copy-start | bytes 11206660
  8.8 10.5 %collective-permute-start.3 = (bf16[192,512]{1,0:T(8,128)(2,1)S(1)}, bf16[192,512]{1,0:T(8,128)(2,1)S(1)}, u32[]{:S(2)}, u32[]{:S(2)}) collective-permute-start(bf16[192,512]{1,0:T(8,128)(2,1)S(1)} %get-tuple-element.41), channel_id=1, source_target_pairs={{0,4},{4,0},{8,12},{12,8},{16,20},{20,16},{24,28},{28,24},{1,5},{5... | collective-permute-start | bytes 589832 | tf_op jit(solution)/shard_map/ppermute | solution.py:222
  10.9 8.5 %collective-permute-start.4 = (bf16[192,512]{1,0:T(8,128)(2,1)S(1)}, bf16[192,512]{1,0:T(8,128)(2,1)S(1)}, u32[]{:S(2)}, u32[]{:S(2)}) collective-permute-start(bf16[192,512]{1,0:T(8,128)(2,1)S(1)} %get-tuple-element.40), channel_id=1, source_target_pairs={{4,8},{12,16},{20,24},{8,4},{16,12},{24,20},{5,9},{13,17},{21,25},... | collective-permute-start | bytes 589832 | tf_op jit(solution)/shard_map/ppermute | solution.py:226
  18.8 4.6 %collective-permute-start.12 = (bf16[64,3840]{1,0:T(8,128)(2,1)S(1)}, bf16[64,3840]{1,0:T(8,128)(2,1)S(1)}, u32[]{:S(2)}, u32[]{:S(2)}) collective-permute-start(bf16[64,3840]{1,0:T(8,128)(2,1)S(1)} %collective-permute-done.5.refs_8_), channel_id=1, source_target_pairs={{0,1},{1,0},{2,3},{3,2},{4,5},{5,4},{6,7},{7,6},{8,9},{9,8},{10,11... | collective-permute-start | bytes 1474568 | tf_op jit(solution)/shard_map/ppermute | solution.py:219
  18.8 4.6 %collective-permute-start.11 = (bf16[64,1024]{1,0:T(8,128)(2,1)S(1)}, bf16[64,1024]{1,0:T(8,128)(2,1)S(1)}, u32[]{:S(2)}, u32[]{:S(2)}) collective-permute-start(bf16[64,1024]{1,0:T(8,128)(2,1)S(1)} %collective-permute-done.refs_6_), channel_id=1, source_target_pairs={{0,1},{1,0},{2,3},{3,2},{4,5},{5,4},{6,7},{7,6},{8,9},{9,8},{10,11... | collective-permute-start | bytes 393224 | tf_op jit(solution)/shard_map/ppermute | solution.py:219
  19.4 4.0 %collective-permute-start.10 = (bf16[64,1024]{1,0:T(8,128)(2,1)S(1)}, bf16[64,1024]{1,0:T(8,128)(2,1)S(1)}, u32[]{:S(2)}, u32[]{:S(2)}) collective-permute-start(bf16[64,1024]{1,0:T(8,128)(2,1)S(1)} %slice.14), channel_id=1, source_target_pairs={{0,1},{1,0},{2,3},{3,2},{4,5},{5,4},{6,7},{7,6},{8,9},{9,8},{10,11... | collective-permute-start | bytes 393224 | tf_op jit(solution)/shard_map/ppermute | solution.py:219
  21.1 6.6 %collective-permute-start.6 = (bf16[4,64,256]{2,1,0:T(8,128)(2,1)S(1)}, bf16[4,64,256]{2,1,0:T(8,128)(2,1)S(1)}, u32[]{:S(2)}, u32[]{:S(2)}) collective-permute-start(bf16[4,64,256]{2,1,0:T(8,128)(2,1)S(1)} %get-tuple-element.28), channel_id=1, source_target_pairs={{0,4},{4,0},{8,12},{12,8},{16,20},{20,16},{24,28},{28,24},{1,5},{5... | collective-permute-start | bytes 393224 | tf_op jit(solution)/shard_map/ppermute | solution.py:222
  27.6 5.7 %collective-permute-start.13 = (bf16[4,64,256]{2,1,0:T(8,128)(2,1)S(1)}, bf16[4,64,256]{2,1,0:T(8,128)(2,1)S(1)}, u32[]{:S(2)}, u32[]{:S(2)}) collective-permute-start(bf16[4,64,256]{2,1,0:T(8,128)(2,1)S(1)} %get-tuple-element.35), channel_id=1, source_target_pairs={{0,4},{4,0},{8,12},{12,8},{16,20},{20,16},{24,28},{28,24},{1,5},{5... | collective-permute-start | bytes 393224 | tf_op jit(solution)/shard_map/ppermute | solution.py:222
  27.7 9.3 %collective-permute-start.7 = (bf16[64,256]{1,0:T(8,128)(2,1)S(1)}, bf16[64,256]{1,0:T(8,128)(2,1)S(1)}, u32[]{:S(2)}, u32[]{:S(2)}) collective-permute-start(bf16[64,256]{1,0:T(8,128)(2,1)S(1)} %get-tuple-element.30), channel_id=1, source_target_pairs={{0,8},{4,12},{8,0},{12,4},{16,24},{20,28},{24,16},{28,20},{1,9},{5... | collective-permute-start | bytes 98312 | tf_op jit(solution)/shard_map/ppermute | solution.py:222
  29.8 7.9 %collective-permute-start.8 = (bf16[64,256]{1,0:T(8,128)(2,1)S(1)}, bf16[64,256]{1,0:T(8,128)(2,1)S(1)}, u32[]{:S(2)}, u32[]{:S(2)}) collective-permute-start(bf16[64,256]{1,0:T(8,128)(2,1)S(1)} %get-tuple-element.31), channel_id=1, source_target_pairs={{0,16},{4,20},{8,24},{12,28},{16,0},{20,4},{24,8},{28,12},{1,17},{... | collective-permute-start | bytes 98312 | tf_op jit(solution)/shard_map/ppermute | solution.py:222
  32.4 6.1 %collective-permute-start.9 = (bf16[64,256]{1,0:T(8,128)(2,1)S(1)}, bf16[64,256]{1,0:T(8,128)(2,1)S(1)}, u32[]{:S(2)}, u32[]{:S(2)}) collective-permute-start(bf16[64,256]{1,0:T(8,128)(2,1)S(1)} %get-tuple-element.32), channel_id=1, source_target_pairs={{0,24},{4,28},{8,16},{12,20},{16,8},{20,12},{24,0},{28,4},{1,25},{... | collective-permute-start | bytes 98312 | tf_op jit(solution)/shard_map/ppermute | solution.py:222
  33.3 5.2 %collective-permute-start.14 = (bf16[64,256]{1,0:T(8,128)(2,1)S(1)}, bf16[64,256]{1,0:T(8,128)(2,1)S(1)}, u32[]{:S(2)}, u32[]{:S(2)}) collective-permute-start(bf16[64,256]{1,0:T(8,128)(2,1)S(1)} %get-tuple-element.37), channel_id=1, source_target_pairs={{0,8},{4,12},{8,0},{12,4},{16,24},{20,28},{24,16},{28,20},{1,9},{5... | collective-permute-start | bytes 98312 | tf_op jit(solution)/shard_map/ppermute | solution.py:222
  34.9 5.1 %collective-permute-start.15 = (bf16[64,256]{1,0:T(8,128)(2,1)S(1)}, bf16[64,256]{1,0:T(8,128)(2,1)S(1)}, u32[]{:S(2)}, u32[]{:S(2)}) collective-permute-start(bf16[64,256]{1,0:T(8,128)(2,1)S(1)} %get-tuple-element.38), channel_id=1, source_target_pairs={{0,16},{4,20},{8,24},{12,28},{16,0},{20,4},{24,8},{28,12},{1,17},{... | collective-permute-start | bytes 98312 | tf_op jit(solution)/shard_map/ppermute | solution.py:222
  37.1 5.7 %collective-permute-start.16 = (bf16[64,256]{1,0:T(8,128)(2,1)S(1)}, bf16[64,256]{1,0:T(8,128)(2,1)S(1)}, u32[]{:S(2)}, u32[]{:S(2)}) collective-permute-start(bf16[64,256]{1,0:T(8,128)(2,1)S(1)} %get-tuple-element.39), channel_id=1, source_target_pairs={{0,24},{4,28},{8,16},{12,20},{16,8},{20,12},{24,0},{28,4},{1,25},{... | collective-permute-start | bytes 98312 | tf_op jit(solution)/shard_map/ppermute | solution.py:222

commit v10 on v9

--- a/solution.py
+++ b/solution.py
@@ -256,7 +256,8 @@
     halves = []
     for keep, got in ((keep_a, got_a), (keep_b, got_b)):
         keep, *sends = spread(groups, keep, got)
-        halves.append([keep] + [swap(send, 2 * step) for step, send in enumerate(sends, 1)])
+        steps = sorted(range(1, groups), key=lambda step: -step)
+        halves.append([keep] + [swap(sends[step - 1], 2 * step) for step in steps])
     return finish(*halves)
 
 

time: 43.6 us -> 42.2 us (0.968)
  waiting for transfers between devices: 9.7 us -> 8.19 us
    ppermute x9, waiting for transfers between devices: 5.85 us -> 4.34 us  [swap(): return lax.ppermute(array, 'node', [(i, i ^ step) for i in range(nodes)])]
  transfers between devices with their start and end apart: 17 -> 17, of which waited for: 5 -> 4; matrix products, arithmetic and copies ran while one was open for 2% -> 2% of each run, Pallas kernels for 27% -> 28%
where the time goes in v10:
time: 42.2 us; the launch traced here: 42 us
  starting transfers between devices  18.5 us (44%)
  Pallas kernels  12.6 us (30%)
  waiting for transfers between devices  8.19 us (19%)
  local copies, waits for them, and re-layouts  1.18 us (3%)
  between operations  0.82 us (2%)
  other arithmetic  0.69 us (2%)
    ppermute x9, starting transfers between devices, swap(): return lax.ppermute(array, 'node', [(i, i ^ step) for i in range(nodes)])  13.7 us
    pallas_call x3, Pallas kernels, project(): pl.pallas_call(functools.partial(project_kernel, spans, places, groups, b...  9.18 us
    ppermute x9, waiting for transfers between devices, swap(): return lax.ppermute(array, 'node', [(i, i ^ step) for i in range(nodes)])  4.34 us
    ppermute x2, waiting for transfers between devices, across(): return lax.ppermute(array, 'col', [(i, i ^ 2) for i in range(cols)])  3.83 us
    ppermute x2, starting transfers between devices, across(): return lax.ppermute(array, 'col', [(i, i ^ 2) for i in range(cols)])  3.08 us
    pallas_call x1, Pallas kernels, load(): pl.pallas_call(load_kernel, out_shape=[shape(array.shape, array.dtype) fo...  2.62 us
    unnamed x9, local copies, waits for them, and re-layouts  1.11 us
    ppermute x5, starting transfers between devices, cores(): return lax.ppermute(array, 'col', [(i, i ^ 1) for i in range(cols)])  1.09 us
  transfers between devices with their start and end apart: 17, of which 4 were waited for; matrix products, arithmetic and copies ran while one was open for 2% of the time, Pallas kernels for 28%

profile of v10, /device:TPU:0, one launch (start us, length us, event | category | flops | bytes accessed | tf_op | source)
XLA Modules:
  0.0 42.0 jit_solution(6917478563275176759)
XLA Ops:
  0.6 1.1 %copy-done.2 = bf16[4864,64]{0,1:T(8,128)(2,1)S(1)} copy-done((bf16[4864,64]{0,1:T(8,128)(2,1)S(1)}, bf16[4864,64]{0,1:T(8,128)(2,1)}, u32[]{:S(2)}) %copy-start.2) | copy-done | bytes 622616
  1.7 0.1 shard_map.68
  1.8 3.0 %collective-permute-start = (bf16[64,1024]{1,0:T(8,128)(2,1)S(1)}, bf16[64,1024]{1,0:T(8,128)(2,1)S(1)}, u32[]{:S(2)}, u32[]{:S(2)}) collective-permute-start(bf16[64,1024]{1,0:T(8,128)(2,1)S(1)} %get-tuple-element.21.refs_4_), channel_id=1, source_target_pairs={{0,2},{1,3},{2,0},{3,1},{4,6},{5,7},{6,4},{7,5},{8,10},{9,11},{10,... | collective-permute-start | bytes 393224 | tf_op jit(solution)/shard_map/ppermute | solution.py:216
  4.8 0.5 %collective-permute-start.2 = (bf16[64,3840]{1,0:T(8,128)(2,1)S(1)}, bf16[64,3840]{1,0:T(8,128)(2,1)S(1)}, u32[]{:S(2)}, u32[]{:S(2)}) collective-permute-start(bf16[64,3840]{1,0:T(8,128)(2,1)S(1)} %get-tuple-element.24.refs_6_), channel_id=1, source_target_pairs={{0,1},{1,0},{2,3},{3,2},{4,5},{5,4},{6,7},{7,6},{8,9},{9,8},{10,11... | collective-permute-start | bytes 1474568 | tf_op jit(solution)/shard_map/ppermute | solution.py:219
  5.3 0.1 collective-permute-start.5
  5.4 0.7 %clamp_bitcast_fusion.refs_0_ = s32[3,38]{1,0:T(4,128)S(1)} fusion(s32[38,3]{0,1:T(4,128)} %param.9, s32[]{:T(128)S(6)} %sub.10), kind=kLoop, calls=%fused_computation.5 | loop fusion | flops 228 | bytes 916 | tf_op jit(solution)/shard_map/jit(clip)/min | solution.py:236
  6.1 2.6 %shard_map.69.refs_3_ = bf16[4864,512]{1,0:T(8,128)(2,1)S(1)} custom-call(bf16[4864,512]{1,0:T(8,128)(2,1)} %refs_0_.1), custom_call_target="tpu_custom_call" | custom-call | bytes 4980736 | tf_op jit(solution)/shard_map/pallas_call | solution.py:76
  8.8 2.0 %collective-permute-start.3 = (bf16[192,512]{1,0:T(8,128)(2,1)S(1)}, bf16[192,512]{1,0:T(8,128)(2,1)S(1)}, u32[]{:S(2)}, u32[]{:S(2)}) collective-permute-start(bf16[192,512]{1,0:T(8,128)(2,1)S(1)} %get-tuple-element.41), channel_id=1, source_target_pairs={{0,4},{4,0},{8,12},{12,8},{16,20},{20,16},{24,28},{28,24},{1,5},{5... | collective-permute-start | bytes 589832 | tf_op jit(solution)/shard_map/ppermute | solution.py:222
  10.9 0.7 %collective-permute-start.4 = (bf16[192,512]{1,0:T(8,128)(2,1)S(1)}, bf16[192,512]{1,0:T(8,128)(2,1)S(1)}, u32[]{:S(2)}, u32[]{:S(2)}) collective-permute-start(bf16[192,512]{1,0:T(8,128)(2,1)S(1)} %get-tuple-element.40), channel_id=1, source_target_pairs={{4,8},{12,16},{20,24},{8,4},{16,12},{24,20},{5,9},{13,17},{21,25},... | collective-permute-start | bytes 589832 | tf_op jit(solution)/shard_map/ppermute | solution.py:226
  11.6 3.4 %shard_map.70.refs_10_ = f32[512,256]{1,0:T(8,128)S(1)} custom-call(s32[3,38]{1,0:T(4,128)S(1)} %clamp_bitcast_fusion.refs_0_, bf16[38,3,128,128]{3,2,1,0:T(8,128)(2,1)S(1)} %copy-done, bf16[38,3,128,128]{3,2,1,0:T(8,128)(2,1)S(1)} %copy-done.1, bf16[4864,512]{1,0:T(8,128)(2,1)S(1)} %shard_map.69.refs_3_, bf16[64,1024]{1,0:T(8,128)(2,1)S(1)} %get-tuple-element.21.refs_4_, ...), custom_call_target="tpu_custom_call" | custom-call | flops 1 | bytes 30 | tf_op jit(solution)/shard_map/pallas_call | solution.py:149
  15.0 3.8 %collective-permute-done.5.refs_8_ = bf16[64,3840]{1,0:T(8,128)(2,1)S(1)} collective-permute-done((bf16[64,3840]{1,0:T(8,128)(2,1)S(1)}, bf16[64,3840]{1,0:T(8,128)(2,1)S(1)}, u32[]{:S(2)}, u32[]{:S(2)}) %collective-permute-start.5) | collective-permute-done | bytes 491552 | tf_op jit(solution)/shard_map/ppermute | solution.py:216
  18.8 0.5 %collective-permute-start.11 = (bf16[64,1024]{1,0:T(8,128)(2,1)S(1)}, bf16[64,1024]{1,0:T(8,128)(2,1)S(1)}, u32[]{:S(2)}, u32[]{:S(2)}) collective-permute-start(bf16[64,1024]{1,0:T(8,128)(2,1)S(1)} %collective-permute-done.refs_6_), channel_id=1, source_target_pairs={{0,1},{1,0},{2,3},{3,2},{4,5},{5,4},{6,7},{7,6},{8,9},{9,8},{10,11... | collective-permute-start | bytes 393224 | tf_op jit(solution)/shard_map/ppermute | solution.py:219
  19.5 1.6 %shard_map.71 = (bf16[4,64,256]{2,1,0:T(8,128)(2,1)S(1)}, f32[4,64,256]{2,1,0:T(8,128)S(1)}) custom-call(s32[3,38]{1,0:T(4,128)S(1)} %clamp_bitcast_fusion.refs_0_, bf16[38,3,128,128]{3,2,1,0:T(8,128)(2,1)S(1)} %copy-done, bf16[38,3,128,128]{3,2,1,0:T(8,128)(2,1)S(1)} %copy-done.1, bf16[4864,512]{1,0:T(8,128)(2,1)S(1)} %shard_map.69.refs_3_, ...), custom_call_target="tpu_custom_call" | custom-call | flops 2300000000 | bytes 8 | tf_op jit(solution)/shard_map/pallas_call | solution.py:149
  21.1 2.3 %collective-permute-start.6 = (bf16[4,64,256]{2,1,0:T(8,128)(2,1)S(1)}, bf16[4,64,256]{2,1,0:T(8,128)(2,1)S(1)}, u32[]{:S(2)}, u32[]{:S(2)}) collective-permute-start(bf16[4,64,256]{2,1,0:T(8,128)(2,1)S(1)} %get-tuple-element.28), channel_id=1, source_target_pairs={{0,4},{4,0},{8,12},{12,8},{16,20},{20,16},{24,28},{28,24},{1,5},{5... | collective-permute-start | bytes 393224 | tf_op jit(solution)/shard_map/ppermute | solution.py:222
  23.5 4.1 %shard_map.73 = (bf16[4,64,256]{2,1,0:T(8,128)(2,1)S(1)}, f32[4,64,256]{2,1,0:T(8,128)S(1)}) custom-call(s32[3,38]{1,0:T(4,128)S(1)} %clamp_bitcast_fusion.refs_0_, bf16[38,3,128,128]{3,2,1,0:T(8,128)(2,1)S(1)} %copy-done, bf16[38,3,128,128]{3,2,1,0:T(8,128)(2,1)S(1)} %copy-done.1, bf16[4864,512]{1,0:T(8,128)(2,1)S(1)} %shard_map.69.refs_3_, ...), custom_call_target="tpu_custom_call" | custom-call | flops 38 | bytes 38 | tf_op jit(solution)/shard_map/pallas_call | solution.py:149
  27.6 0.1 collective-permute-start.13
  27.7 4.1 %collective-permute-start.7 = (bf16[64,256]{1,0:T(8,128)(2,1)S(1)}, bf16[64,256]{1,0:T(8,128)(2,1)S(1)}, u32[]{:S(2)}, u32[]{:S(2)}) collective-permute-start(bf16[64,256]{1,0:T(8,128)(2,1)S(1)} %get-tuple-element.30), channel_id=1, source_target_pairs={{0,24},{4,28},{8,16},{12,20},{16,8},{20,12},{24,0},{28,4},{1,25},{... | collective-permute-start | bytes 98312 | tf_op jit(solution)/shard_map/ppermute | solution.py:222
  31.9 0.6 %collective-permute-start.9 = (bf16[64,256]{1,0:T(8,128)(2,1)S(1)}, bf16[64,256]{1,0:T(8,128)(2,1)S(1)}, u32[]{:S(2)}, u32[]{:S(2)}) collective-permute-start(bf16[64,256]{1,0:T(8,128)(2,1)S(1)} %get-tuple-element.32), channel_id=1, source_target_pairs={{0,8},{4,12},{8,0},{12,4},{16,24},{20,28},{24,16},{28,20},{1,9},{5... | collective-permute-start | bytes 98312 | tf_op jit(solution)/shard_map/ppermute | solution.py:222
  32.5 0.8 %collective-permute-done.13.got = bf16[4,64,256]{2,1,0:T(8,128)(2,1)S(1)} collective-permute-done((bf16[4,64,256]{2,1,0:T(8,128)(2,1)S(1)}, bf16[4,64,256]{2,1,0:T(8,128)(2,1)S(1)}, u32[]{:S(2)}, u32[]{:S(2)}) %collective-permute-start.13) | collective-permute-done | bytes 131104 | tf_op jit(solution)/shard_map/ppermute | solution.py:222
  33.3 3.2 %collective-permute-start.14 = (bf16[64,256]{1,0:T(8,128)(2,1)S(1)}, bf16[64,256]{1,0:T(8,128)(2,1)S(1)}, u32[]{:S(2)}, u32[]{:S(2)}) collective-permute-start(bf16[64,256]{1,0:T(8,128)(2,1)S(1)} %get-tuple-element.37), channel_id=1, source_target_pairs={{0,24},{4,28},{8,16},{12,20},{16,8},{20,12},{24,0},{28,4},{1,25},{... | collective-permute-start | bytes 98312 | tf_op jit(solution)/shard_map/ppermute | solution.py:222
  36.5 1.3 %collective-permute-start.16 = (bf16[64,256]{1,0:T(8,128)(2,1)S(1)}, bf16[64,256]{1,0:T(8,128)(2,1)S(1)}, u32[]{:S(2)}, u32[]{:S(2)}) collective-permute-start(bf16[64,256]{1,0:T(8,128)(2,1)S(1)} %get-tuple-element.39), channel_id=1, source_target_pairs={{0,8},{4,12},{8,0},{12,4},{16,24},{20,28},{24,16},{28,20},{1,9},{5... | collective-permute-start | bytes 98312 | tf_op jit(solution)/shard_map/ppermute | solution.py:222
  37.8 1.5 %collective-permute-done.14.refs_5_ = bf16[64,256]{1,0:T(8,128)(2,1)S(1)} collective-permute-done((bf16[64,256]{1,0:T(8,128)(2,1)S(1)}, bf16[64,256]{1,0:T(8,128)(2,1)S(1)}, u32[]{:S(2)}, u32[]{:S(2)}) %collective-permute-start.14) | collective-permute-done | bytes 32800 | tf_op jit(solution)/shard_map/ppermute | solution.py:222
  39.3 2.1 %collective-permute-done.15.refs_6_ = bf16[64,256]{1,0:T(8,128)(2,1)S(1)} collective-permute-done((bf16[64,256]{1,0:T(8,128)(2,1)S(1)}, bf16[64,256]{1,0:T(8,128)(2,1)S(1)}, u32[]{:S(2)}, u32[]{:S(2)}) %collective-permute-start.15) | collective-permute-done | bytes 32800 | tf_op jit(solution)/shard_map/ppermute | solution.py:222
  41.3 0.7 %shard_map.75 = (f32[64,256]{1,0:T(8,128)}, f32[64,256]{1,0:T(8,128)}) custom-call(f32[64,256]{1,0:T(8,128)S(1)} %get-tuple-element.29.refs_0_, bf16[64,256]{1,0:T(8,128)(2,1)S(1)} %collective-permute-done.7.refs_1_, bf16[64,256]{1,0:T(8,128)(2,1)S(1)} %collective-permute-done.8.refs_2_, bf16[64,256]{1,0:T(8,128)(2,1)S(1)} %collective-permute-done.9.refs_3_, ...), custom_call_target="tpu_custom_call" | custom-call | tf_op jit(solution)/shard_map/pallas_call | solution.py:199
  (32 shorter events, 0.3 us)
Async XLA Ops:
  0.6 1.1 %copy-start.2 = (bf16[4864,64]{0,1:T(8,128)(2,1)S(1)}, bf16[4864,64]{0,1:T(8,128)(2,1)}, u32[]{:S(2)}) copy-start(bf16[4864,64]{0,1:T(8,128)(2,1)} %param.5) | copy-start | bytes 1867780
  1.8 6.9 %collective-permute-start = (bf16[64,1024]{1,0:T(8,128)(2,1)S(1)}, bf16[64,1024]{1,0:T(8,128)(2,1)S(1)}, u32[]{:S(2)}, u32[]{:S(2)}) collective-permute-start(bf16[64,1024]{1,0:T(8,128)(2,1)S(1)} %get-tuple-element.21.refs_4_), channel_id=1, source_target_pairs={{0,2},{1,3},{2,0},{3,1},{4,6},{5,7},{6,4},{7,5},{8,10},{9,11},{10,... | collective-permute-start | bytes 393224 | tf_op jit(solution)/shard_map/ppermute | solution.py:216
  4.8 3.9 %collective-permute-start.1 = (bf16[64,1024]{1,0:T(8,128)(2,1)S(1)}, bf16[64,1024]{1,0:T(8,128)(2,1)S(1)}, u32[]{:S(2)}, u32[]{:S(2)}) collective-permute-start(bf16[64,1024]{1,0:T(8,128)(2,1)S(1)} %get-tuple-element.21.refs_4_), channel_id=1, source_target_pairs={{0,1},{1,0},{2,3},{3,2},{4,5},{5,4},{6,7},{7,6},{8,9},{9,8},{10,11... | collective-permute-start | bytes 393224 | tf_op jit(solution)/shard_map/ppermute | solution.py:219
  4.8 6.7 %collective-permute-start.2 = (bf16[64,3840]{1,0:T(8,128)(2,1)S(1)}, bf16[64,3840]{1,0:T(8,128)(2,1)S(1)}, u32[]{:S(2)}, u32[]{:S(2)}) collective-permute-start(bf16[64,3840]{1,0:T(8,128)(2,1)S(1)} %get-tuple-element.24.refs_6_), channel_id=1, source_target_pairs={{0,1},{1,0},{2,3},{3,2},{4,5},{5,4},{6,7},{7,6},{8,9},{9,8},{10,11... | collective-permute-start | bytes 1474568 | tf_op jit(solution)/shard_map/ppermute | solution.py:219
  5.3 13.5 %collective-permute-start.5 = (bf16[64,3840]{1,0:T(8,128)(2,1)S(1)}, bf16[64,3840]{1,0:T(8,128)(2,1)S(1)}, u32[]{:S(2)}, u32[]{:S(2)}) collective-permute-start(bf16[64,3840]{1,0:T(8,128)(2,1)S(1)} %get-tuple-element.24.refs_6_), channel_id=1, source_target_pairs={{0,2},{1,3},{2,0},{3,1},{4,6},{5,7},{6,4},{7,5},{8,10},{9,11},{10,... | collective-permute-start | bytes 1474568 | tf_op jit(solution)/shard_map/ppermute | solution.py:216
  6.1 5.5 %copy-start = (bf16[38,3,128,128]{3,2,1,0:T(8,128)(2,1)S(1)}, bf16[38,3,128,128]{3,2,1,0:T(8,128)(2,1)}, u32[]{:S(2)}) copy-start(bf16[38,3,128,128]{3,2,1,0:T(8,128)(2,1)} %refs_1_.5) | copy-start | bytes 11206660
  6.1 5.5 %copy-start.1 = (bf16[38,3,128,128]{3,2,1,0:T(8,128)(2,1)S(1)}, bf16[38,3,128,128]{3,2,1,0:T(8,128)(2,1)}, u32[]{:S(2)}) copy-start(bf16[38,3,128,128]{3,2,1,0:T(8,128)(2,1)} %refs_2_.5) | copy-start | bytes 11206660
  8.8 10.5 %collective-permute-start.3 = (bf16[192,512]{1,0:T(8,128)(2,1)S(1)}, bf16[192,512]{1,0:T(8,128)(2,1)S(1)}, u32[]{:S(2)}, u32[]{:S(2)}) collective-permute-start(bf16[192,512]{1,0:T(8,128)(2,1)S(1)} %get-tuple-element.41), channel_id=1, source_target_pairs={{0,4},{4,0},{8,12},{12,8},{16,20},{20,16},{24,28},{28,24},{1,5},{5... | collective-permute-start | bytes 589832 | tf_op jit(solution)/shard_map/ppermute | solution.py:222
  10.9 8.5 %collective-permute-start.4 = (bf16[192,512]{1,0:T(8,128)(2,1)S(1)}, bf16[192,512]{1,0:T(8,128)(2,1)S(1)}, u32[]{:S(2)}, u32[]{:S(2)}) collective-permute-start(bf16[192,512]{1,0:T(8,128)(2,1)S(1)} %get-tuple-element.40), channel_id=1, source_target_pairs={{4,8},{12,16},{20,24},{8,4},{16,12},{24,20},{5,9},{13,17},{21,25},... | collective-permute-start | bytes 589832 | tf_op jit(solution)/shard_map/ppermute | solution.py:226
  18.8 4.6 %collective-permute-start.12 = (bf16[64,3840]{1,0:T(8,128)(2,1)S(1)}, bf16[64,3840]{1,0:T(8,128)(2,1)S(1)}, u32[]{:S(2)}, u32[]{:S(2)}) collective-permute-start(bf16[64,3840]{1,0:T(8,128)(2,1)S(1)} %collective-permute-done.5.refs_8_), channel_id=1, source_target_pairs={{0,1},{1,0},{2,3},{3,2},{4,5},{5,4},{6,7},{7,6},{8,9},{9,8},{10,11... | collective-permute-start | bytes 1474568 | tf_op jit(solution)/shard_map/ppermute | solution.py:219
  18.8 4.6 %collective-permute-start.11 = (bf16[64,1024]{1,0:T(8,128)(2,1)S(1)}, bf16[64,1024]{1,0:T(8,128)(2,1)S(1)}, u32[]{:S(2)}, u32[]{:S(2)}) collective-permute-start(bf16[64,1024]{1,0:T(8,128)(2,1)S(1)} %collective-permute-done.refs_6_), channel_id=1, source_target_pairs={{0,1},{1,0},{2,3},{3,2},{4,5},{5,4},{6,7},{7,6},{8,9},{9,8},{10,11... | collective-permute-start | bytes 393224 | tf_op jit(solution)/shard_map/ppermute | solution.py:219
  19.4 4.0 %collective-permute-start.10 = (bf16[64,1024]{1,0:T(8,128)(2,1)S(1)}, bf16[64,1024]{1,0:T(8,128)(2,1)S(1)}, u32[]{:S(2)}, u32[]{:S(2)}) collective-permute-start(bf16[64,1024]{1,0:T(8,128)(2,1)S(1)} %slice.14), channel_id=1, source_target_pairs={{0,1},{1,0},{2,3},{3,2},{4,5},{5,4},{6,7},{7,6},{8,9},{9,8},{10,11... | collective-permute-start | bytes 393224 | tf_op jit(solution)/shard_map/ppermute | solution.py:219
  21.1 6.6 %collective-permute-start.6 = (bf16[4,64,256]{2,1,0:T(8,128)(2,1)S(1)}, bf16[4,64,256]{2,1,0:T(8,128)(2,1)S(1)}, u32[]{:S(2)}, u32[]{:S(2)}) collective-permute-start(bf16[4,64,256]{2,1,0:T(8,128)(2,1)S(1)} %get-tuple-element.28), channel_id=1, source_target_pairs={{0,4},{4,0},{8,12},{12,8},{16,20},{20,16},{24,28},{28,24},{1,5},{5... | collective-permute-start | bytes 393224 | tf_op jit(solution)/shard_map/ppermute | solution.py:222
  27.6 5.7 %collective-permute-start.13 = (bf16[4,64,256]{2,1,0:T(8,128)(2,1)S(1)}, bf16[4,64,256]{2,1,0:T(8,128)(2,1)S(1)}, u32[]{:S(2)}, u32[]{:S(2)}) collective-permute-start(bf16[4,64,256]{2,1,0:T(8,128)(2,1)S(1)} %get-tuple-element.35), channel_id=1, source_target_pairs={{0,4},{4,0},{8,12},{12,8},{16,20},{20,16},{24,28},{28,24},{1,5},{5... | collective-permute-start | bytes 393224 | tf_op jit(solution)/shard_map/ppermute | solution.py:222
  27.7 8.8 %collective-permute-start.7 = (bf16[64,256]{1,0:T(8,128)(2,1)S(1)}, bf16[64,256]{1,0:T(8,128)(2,1)S(1)}, u32[]{:S(2)}, u32[]{:S(2)}) collective-permute-start(bf16[64,256]{1,0:T(8,128)(2,1)S(1)} %get-tuple-element.30), channel_id=1, source_target_pairs={{0,24},{4,28},{8,16},{12,20},{16,8},{20,12},{24,0},{28,4},{1,25},{... | collective-permute-start | bytes 98312 | tf_op jit(solution)/shard_map/ppermute | solution.py:222
  31.9 5.9 %collective-permute-start.8 = (bf16[64,256]{1,0:T(8,128)(2,1)S(1)}, bf16[64,256]{1,0:T(8,128)(2,1)S(1)}, u32[]{:S(2)}, u32[]{:S(2)}) collective-permute-start(bf16[64,256]{1,0:T(8,128)(2,1)S(1)} %get-tuple-element.31), channel_id=1, source_target_pairs={{0,16},{4,20},{8,24},{12,28},{16,0},{20,4},{24,8},{28,12},{1,17},{... | collective-permute-start | bytes 98312 | tf_op jit(solution)/shard_map/ppermute | solution.py:222
  31.9 5.9 %collective-permute-start.9 = (bf16[64,256]{1,0:T(8,128)(2,1)S(1)}, bf16[64,256]{1,0:T(8,128)(2,1)S(1)}, u32[]{:S(2)}, u32[]{:S(2)}) collective-permute-start(bf16[64,256]{1,0:T(8,128)(2,1)S(1)} %get-tuple-element.32), channel_id=1, source_target_pairs={{0,8},{4,12},{8,0},{12,4},{16,24},{20,28},{24,16},{28,20},{1,9},{5... | collective-permute-start | bytes 98312 | tf_op jit(solution)/shard_map/ppermute | solution.py:222
  33.3 6.0 %collective-permute-start.14 = (bf16[64,256]{1,0:T(8,128)(2,1)S(1)}, bf16[64,256]{1,0:T(8,128)(2,1)S(1)}, u32[]{:S(2)}, u32[]{:S(2)}) collective-permute-start(bf16[64,256]{1,0:T(8,128)(2,1)S(1)} %get-tuple-element.37), channel_id=1, source_target_pairs={{0,24},{4,28},{8,16},{12,20},{16,8},{20,12},{24,0},{28,4},{1,25},{... | collective-permute-start | bytes 98312 | tf_op jit(solution)/shard_map/ppermute | solution.py:222
  36.5 4.8 %collective-permute-start.15 = (bf16[64,256]{1,0:T(8,128)(2,1)S(1)}, bf16[64,256]{1,0:T(8,128)(2,1)S(1)}, u32[]{:S(2)}, u32[]{:S(2)}) collective-permute-start(bf16[64,256]{1,0:T(8,128)(2,1)S(1)} %get-tuple-element.38), channel_id=1, source_target_pairs={{0,16},{4,20},{8,24},{12,28},{16,0},{20,4},{24,8},{28,12},{1,17},{... | collective-permute-start | bytes 98312 | tf_op jit(solution)/shard_map/ppermute | solution.py:222
  36.5 4.8 %collective-permute-start.16 = (bf16[64,256]{1,0:T(8,128)(2,1)S(1)}, bf16[64,256]{1,0:T(8,128)(2,1)S(1)}, u32[]{:S(2)}, u32[]{:S(2)}) collective-permute-start(bf16[64,256]{1,0:T(8,128)(2,1)S(1)} %get-tuple-element.39), channel_id=1, source_target_pairs={{0,8},{4,12},{8,0},{12,4},{16,24},{20,28},{24,16},{28,20},{1,9},{5... | collective-permute-start | bytes 98312 | tf_op jit(solution)/shard_map/ppermute | solution.py:222

commit v11 on v10

--- a/solution.py
+++ b/solution.py
@@ -156,7 +156,7 @@
             pltpu.VMEM((count * BS, 4 * width), BF16),
         ],
         compiler_params=params(14),
-        cost_estimate=pl.CostEstimate(flops=int(2.3e+09) if more else (count if last else int(1)), bytes_accessed=count, transcendentals=0),
+        cost_estimate=pl.CostEstimate(flops=int(3.45e+09) if more else (count if last else int(1)), bytes_accessed=count, transcendentals=0),
     )(ids, g_blocks, c_blocks, basis, *arrays, *more)
 
 
@@ -241,9 +241,11 @@
     (part,) = project(fixed, own, [(HB, rows - HB)], groups, last=False)
     part, far_middle = lax.optimization_barrier((part, far_middle))
     far_rim = 2 * ROWS_OF_CORE
+    near_parts = [(0, 2 * halo, 2 * halo, halo), (inner - 3 * halo, inner - halo, inner - halo, halo)]
+    near_rim = [own[0], own[1][:3] + (near_parts,)]
     rim_parts = [(0, halo + inner, 0, halo), (halo, 0, halo + inner, halo)]
     send_a, keep_a = project(
-        fixed, own + [(rim, rim, (0, ROWS_OF_CORE), rim_parts)], [(0, HB), (rows - HB, rows)], groups, before=part
+        fixed, near_rim + [(rim, rim, (0, ROWS_OF_CORE), rim_parts)], [(0, HB), (rows - HB, rows)], groups, before=part
     )
     got_a = swap(send_a, 1)
     far = [

time: 42.2 us -> 42 us (level)
  transfers between devices with their start and end apart: 17 -> 17, of which waited for: 4 -> 5; matrix products, arithmetic and copies ran while one was open for 2% -> 2% of each run, Pallas kernels for 28% -> 28%
where the time goes in v11:
time: 42 us; the launch traced here: 41.8 us
  starting transfers between devices  18.3 us (44%)
  Pallas kernels  12.6 us (30%)
  waiting for transfers between devices  8.24 us (20%)
  local copies, waits for them, and re-layouts  1.18 us (3%)
  between operations  0.82 us (2%)
  other arithmetic  0.69 us (2%)
    ppermute x9, starting transfers between devices, swap(): return lax.ppermute(array, 'node', [(i, i ^ step) for i in range(nodes)])  13.7 us
    pallas_call x3, Pallas kernels, project(): pl.pallas_call(functools.partial(project_kernel, spans, places, groups, b...  9.11 us
    ppermute x9, waiting for transfers between devices, swap(): return lax.ppermute(array, 'node', [(i, i ^ step) for i in range(nodes)])  4.46 us
    ppermute x2, waiting for transfers between devices, across(): return lax.ppermute(array, 'col', [(i, i ^ 2) for i in range(cols)])  3.76 us
    ppermute x2, starting transfers between devices, across(): return lax.ppermute(array, 'col', [(i, i ^ 2) for i in range(cols)])  3.08 us
    pallas_call x1, Pallas kernels, load(): pl.pallas_call(load_kernel, out_shape=[shape(array.shape, array.dtype) fo...  2.62 us
    unnamed x9, local copies, waits for them, and re-layouts  1.11 us
    ppermute x5, starting transfers between devices, cores(): return lax.ppermute(array, 'col', [(i, i ^ 1) for i in range(cols)])  0.87 us
  transfers between devices with their start and end apart: 17, of which 5 were waited for; matrix products, arithmetic and copies ran while one was open for 2% of the time, Pallas kernels for 28%

profile of v11, /device:TPU:0, one launch (start us, length us, event | category | flops | bytes accessed | tf_op | source)
XLA Modules:
  0.0 41.8 jit_solution(9142607492529388205)
XLA Ops:
  0.6 1.1 %copy-done.2 = bf16[4864,64]{0,1:T(8,128)(2,1)S(1)} copy-done((bf16[4864,64]{0,1:T(8,128)(2,1)S(1)}, bf16[4864,64]{0,1:T(8,128)(2,1)}, u32[]{:S(2)}) %copy-start.2) | copy-done | bytes 622616
  1.7 0.1 shard_map.68
  1.8 3.0 %collective-permute-start = (bf16[64,1024]{1,0:T(8,128)(2,1)S(1)}, bf16[64,1024]{1,0:T(8,128)(2,1)S(1)}, u32[]{:S(2)}, u32[]{:S(2)}) collective-permute-start(bf16[64,1024]{1,0:T(8,128)(2,1)S(1)} %get-tuple-element.21.refs_4_), channel_id=1, source_target_pairs={{0,2},{1,3},{2,0},{3,1},{4,6},{5,7},{6,4},{7,5},{8,10},{9,11},{10,... | collective-permute-start | bytes 393224 | tf_op jit(solution)/shard_map/ppermute | solution.py:216
  4.8 0.5 %collective-permute-start.2 = (bf16[64,3840]{1,0:T(8,128)(2,1)S(1)}, bf16[64,3840]{1,0:T(8,128)(2,1)S(1)}, u32[]{:S(2)}, u32[]{:S(2)}) collective-permute-start(bf16[64,3840]{1,0:T(8,128)(2,1)S(1)} %get-tuple-element.24.refs_6_), channel_id=1, source_target_pairs={{0,1},{1,0},{2,3},{3,2},{4,5},{5,4},{6,7},{7,6},{8,9},{9,8},{10,11... | collective-permute-start | bytes 1474568 | tf_op jit(solution)/shard_map/ppermute | solution.py:219
  5.4 0.7 %clamp_bitcast_fusion.refs_0_ = s32[3,38]{1,0:T(4,128)S(1)} fusion(s32[38,3]{0,1:T(4,128)} %param.9, s32[]{:T(128)S(6)} %sub.10), kind=kLoop, calls=%fused_computation.5 | loop fusion | flops 228 | bytes 916 | tf_op jit(solution)/shard_map/jit(clip)/min | solution.py:236
  6.1 2.6 %shard_map.69.refs_3_ = bf16[4864,512]{1,0:T(8,128)(2,1)S(1)} custom-call(bf16[4864,512]{1,0:T(8,128)(2,1)} %refs_0_.1), custom_call_target="tpu_custom_call" | custom-call | bytes 4980736 | tf_op jit(solution)/shard_map/pallas_call | solution.py:76
  8.8 2.0 %collective-permute-start.3 = (bf16[192,512]{1,0:T(8,128)(2,1)S(1)}, bf16[192,512]{1,0:T(8,128)(2,1)S(1)}, u32[]{:S(2)}, u32[]{:S(2)}) collective-permute-start(bf16[192,512]{1,0:T(8,128)(2,1)S(1)} %get-tuple-element.41), channel_id=1, source_target_pairs={{0,4},{4,0},{8,12},{12,8},{16,20},{20,16},{24,28},{28,24},{1,5},{5... | collective-permute-start | bytes 589832 | tf_op jit(solution)/shard_map/ppermute | solution.py:222
  10.9 0.7 %collective-permute-start.4 = (bf16[192,512]{1,0:T(8,128)(2,1)S(1)}, bf16[192,512]{1,0:T(8,128)(2,1)S(1)}, u32[]{:S(2)}, u32[]{:S(2)}) collective-permute-start(bf16[192,512]{1,0:T(8,128)(2,1)S(1)} %get-tuple-element.40), channel_id=1, source_target_pairs={{4,8},{12,16},{20,24},{8,4},{16,12},{24,20},{5,9},{13,17},{21,25},... | collective-permute-start | bytes 589832 | tf_op jit(solution)/shard_map/ppermute | solution.py:226
  11.7 3.4 %shard_map.70.refs_10_ = f32[512,256]{1,0:T(8,128)S(1)} custom-call(s32[3,38]{1,0:T(4,128)S(1)} %clamp_bitcast_fusion.refs_0_, bf16[38,3,128,128]{3,2,1,0:T(8,128)(2,1)S(1)} %copy-done, bf16[38,3,128,128]{3,2,1,0:T(8,128)(2,1)S(1)} %copy-done.1, bf16[4864,512]{1,0:T(8,128)(2,1)S(1)} %shard_map.69.refs_3_, bf16[64,1024]{1,0:T(8,128)(2,1)S(1)} %get-tuple-element.21.refs_4_, ...), custom_call_target="tpu_custom_call" | custom-call | flops 1 | bytes 30 | tf_op jit(solution)/shard_map/pallas_call | solution.py:149
  15.1 3.8 %collective-permute-done.5.refs_8_ = bf16[64,3840]{1,0:T(8,128)(2,1)S(1)} collective-permute-done((bf16[64,3840]{1,0:T(8,128)(2,1)S(1)}, bf16[64,3840]{1,0:T(8,128)(2,1)S(1)}, u32[]{:S(2)}, u32[]{:S(2)}) %collective-permute-start.5) | collective-permute-done | bytes 491552 | tf_op jit(solution)/shard_map/ppermute | solution.py:216
  18.8 0.3 collective-permute-done.3
  19.2 0.3 collective-permute-start.10
  19.5 1.6 %shard_map.71 = (bf16[4,64,256]{2,1,0:T(8,128)(2,1)S(1)}, f32[4,64,256]{2,1,0:T(8,128)S(1)}) custom-call(s32[3,38]{1,0:T(4,128)S(1)} %clamp_bitcast_fusion.refs_0_, bf16[38,3,128,128]{3,2,1,0:T(8,128)(2,1)S(1)} %copy-done, bf16[38,3,128,128]{3,2,1,0:T(8,128)(2,1)S(1)} %copy-done.1, bf16[4864,512]{1,0:T(8,128)(2,1)S(1)} %shard_map.69.refs_3_, ...), custom_call_target="tpu_custom_call" | custom-call | flops 3449999872 | bytes 8 | tf_op jit(solution)/shard_map/pallas_call | solution.py:149
  21.1 2.3 %collective-permute-start.6 = (bf16[4,64,256]{2,1,0:T(8,128)(2,1)S(1)}, bf16[4,64,256]{2,1,0:T(8,128)(2,1)S(1)}, u32[]{:S(2)}, u32[]{:S(2)}) collective-permute-start(bf16[4,64,256]{2,1,0:T(8,128)(2,1)S(1)} %get-tuple-element.28), channel_id=1, source_target_pairs={{0,4},{4,0},{8,12},{12,8},{16,20},{20,16},{24,28},{28,24},{1,5},{5... | collective-permute-start | bytes 393224 | tf_op jit(solution)/shard_map/ppermute | solution.py:222
  23.4 4.1 %shard_map.73 = (bf16[4,64,256]{2,1,0:T(8,128)(2,1)S(1)}, f32[4,64,256]{2,1,0:T(8,128)S(1)}) custom-call(s32[3,38]{1,0:T(4,128)S(1)} %clamp_bitcast_fusion.refs_0_, bf16[38,3,128,128]{3,2,1,0:T(8,128)(2,1)S(1)} %copy-done, bf16[38,3,128,128]{3,2,1,0:T(8,128)(2,1)S(1)} %copy-done.1, bf16[4864,512]{1,0:T(8,128)(2,1)S(1)} %shard_map.69.refs_3_, ...), custom_call_target="tpu_custom_call" | custom-call | flops 38 | bytes 38 | tf_op jit(solution)/shard_map/pallas_call | solution.py:149
  27.5 0.1 collective-permute-start.13
  27.7 4.1 %collective-permute-start.7 = (bf16[64,256]{1,0:T(8,128)(2,1)S(1)}, bf16[64,256]{1,0:T(8,128)(2,1)S(1)}, u32[]{:S(2)}, u32[]{:S(2)}) collective-permute-start(bf16[64,256]{1,0:T(8,128)(2,1)S(1)} %get-tuple-element.30), channel_id=1, source_target_pairs={{0,24},{4,28},{8,16},{12,20},{16,8},{20,12},{24,0},{28,4},{1,25},{... | collective-permute-start | bytes 98312 | tf_op jit(solution)/shard_map/ppermute | solution.py:222
  31.8 0.6 %collective-permute-start.9 = (bf16[64,256]{1,0:T(8,128)(2,1)S(1)}, bf16[64,256]{1,0:T(8,128)(2,1)S(1)}, u32[]{:S(2)}, u32[]{:S(2)}) collective-permute-start(bf16[64,256]{1,0:T(8,128)(2,1)S(1)} %get-tuple-element.32), channel_id=1, source_target_pairs={{0,8},{4,12},{8,0},{12,4},{16,24},{20,28},{24,16},{28,20},{1,9},{5... | collective-permute-start | bytes 98312 | tf_op jit(solution)/shard_map/ppermute | solution.py:222
  32.5 0.8 %collective-permute-done.13.got = bf16[4,64,256]{2,1,0:T(8,128)(2,1)S(1)} collective-permute-done((bf16[4,64,256]{2,1,0:T(8,128)(2,1)S(1)}, bf16[4,64,256]{2,1,0:T(8,128)(2,1)S(1)}, u32[]{:S(2)}, u32[]{:S(2)}) %collective-permute-start.13) | collective-permute-done | bytes 131104 | tf_op jit(solution)/shard_map/ppermute | solution.py:222
  33.3 3.0 %collective-permute-start.14 = (bf16[64,256]{1,0:T(8,128)(2,1)S(1)}, bf16[64,256]{1,0:T(8,128)(2,1)S(1)}, u32[]{:S(2)}, u32[]{:S(2)}) collective-permute-start(bf16[64,256]{1,0:T(8,128)(2,1)S(1)} %get-tuple-element.37), channel_id=1, source_target_pairs={{0,24},{4,28},{8,16},{12,20},{16,8},{20,12},{24,0},{28,4},{1,25},{... | collective-permute-start | bytes 98312 | tf_op jit(solution)/shard_map/ppermute | solution.py:222
  36.4 1.4 %collective-permute-start.16 = (bf16[64,256]{1,0:T(8,128)(2,1)S(1)}, bf16[64,256]{1,0:T(8,128)(2,1)S(1)}, u32[]{:S(2)}, u32[]{:S(2)}) collective-permute-start(bf16[64,256]{1,0:T(8,128)(2,1)S(1)} %get-tuple-element.39), channel_id=1, source_target_pairs={{0,8},{4,12},{8,0},{12,4},{16,24},{20,28},{24,16},{28,20},{1,9},{5... | collective-permute-start | bytes 98312 | tf_op jit(solution)/shard_map/ppermute | solution.py:222
  37.7 1.5 %collective-permute-done.14.refs_5_ = bf16[64,256]{1,0:T(8,128)(2,1)S(1)} collective-permute-done((bf16[64,256]{1,0:T(8,128)(2,1)S(1)}, bf16[64,256]{1,0:T(8,128)(2,1)S(1)}, u32[]{:S(2)}, u32[]{:S(2)}) %collective-permute-start.14) | collective-permute-done | bytes 32800 | tf_op jit(solution)/shard_map/ppermute | solution.py:222
  39.3 1.9 %collective-permute-done.15.refs_6_ = bf16[64,256]{1,0:T(8,128)(2,1)S(1)} collective-permute-done((bf16[64,256]{1,0:T(8,128)(2,1)S(1)}, bf16[64,256]{1,0:T(8,128)(2,1)S(1)}, u32[]{:S(2)}, u32[]{:S(2)}) %collective-permute-start.15) | collective-permute-done | bytes 32800 | tf_op jit(solution)/shard_map/ppermute | solution.py:222
  41.1 0.7 %shard_map.75 = (f32[64,256]{1,0:T(8,128)}, f32[64,256]{1,0:T(8,128)}) custom-call(f32[64,256]{1,0:T(8,128)S(1)} %get-tuple-element.29.refs_0_, bf16[64,256]{1,0:T(8,128)(2,1)S(1)} %collective-permute-done.7.refs_1_, bf16[64,256]{1,0:T(8,128)(2,1)S(1)} %collective-permute-done.8.refs_2_, bf16[64,256]{1,0:T(8,128)(2,1)S(1)} %collective-permute-done.9.refs_3_, ...), custom_call_target="tpu_custom_call" | custom-call | tf_op jit(solution)/shard_map/pallas_call | solution.py:199
  (32 shorter events, 0.4 us)
Async XLA Ops:
  0.6 1.1 %copy-start.2 = (bf16[4864,64]{0,1:T(8,128)(2,1)S(1)}, bf16[4864,64]{0,1:T(8,128)(2,1)}, u32[]{:S(2)}) copy-start(bf16[4864,64]{0,1:T(8,128)(2,1)} %param.5) | copy-start | bytes 1867780
  1.8 6.9 %collective-permute-start = (bf16[64,1024]{1,0:T(8,128)(2,1)S(1)}, bf16[64,1024]{1,0:T(8,128)(2,1)S(1)}, u32[]{:S(2)}, u32[]{:S(2)}) collective-permute-start(bf16[64,1024]{1,0:T(8,128)(2,1)S(1)} %get-tuple-element.21.refs_4_), channel_id=1, source_target_pairs={{0,2},{1,3},{2,0},{3,1},{4,6},{5,7},{6,4},{7,5},{8,10},{9,11},{10,... | collective-permute-start | bytes 393224 | tf_op jit(solution)/shard_map/ppermute | solution.py:216
  4.8 3.9 %collective-permute-start.1 = (bf16[64,1024]{1,0:T(8,128)(2,1)S(1)}, bf16[64,1024]{1,0:T(8,128)(2,1)S(1)}, u32[]{:S(2)}, u32[]{:S(2)}) collective-permute-start(bf16[64,1024]{1,0:T(8,128)(2,1)S(1)} %get-tuple-element.21.refs_4_), channel_id=1, source_target_pairs={{0,1},{1,0},{2,3},{3,2},{4,5},{5,4},{6,7},{7,6},{8,9},{9,8},{10,11... | collective-permute-start | bytes 393224 | tf_op jit(solution)/shard_map/ppermute | solution.py:219
  4.8 6.8 %collective-permute-start.2 = (bf16[64,3840]{1,0:T(8,128)(2,1)S(1)}, bf16[64,3840]{1,0:T(8,128)(2,1)S(1)}, u32[]{:S(2)}, u32[]{:S(2)}) collective-permute-start(bf16[64,3840]{1,0:T(8,128)(2,1)S(1)} %get-tuple-element.24.refs_6_), channel_id=1, source_target_pairs={{0,1},{1,0},{2,3},{3,2},{4,5},{5,4},{6,7},{7,6},{8,9},{9,8},{10,11... | collective-permute-start | bytes 1474568 | tf_op jit(solution)/shard_map/ppermute | solution.py:219
  5.3 13.5 %collective-permute-start.5 = (bf16[64,3840]{1,0:T(8,128)(2,1)S(1)}, bf16[64,3840]{1,0:T(8,128)(2,1)S(1)}, u32[]{:S(2)}, u32[]{:S(2)}) collective-permute-start(bf16[64,3840]{1,0:T(8,128)(2,1)S(1)} %get-tuple-element.24.refs_6_), channel_id=1, source_target_pairs={{0,2},{1,3},{2,0},{3,1},{4,6},{5,7},{6,4},{7,5},{8,10},{9,11},{10,... | collective-permute-start | bytes 1474568 | tf_op jit(solution)/shard_map/ppermute | solution.py:216
  6.1 5.5 %copy-start = (bf16[38,3,128,128]{3,2,1,0:T(8,128)(2,1)S(1)}, bf16[38,3,128,128]{3,2,1,0:T(8,128)(2,1)}, u32[]{:S(2)}) copy-start(bf16[38,3,128,128]{3,2,1,0:T(8,128)(2,1)} %refs_1_.5) | copy-start | bytes 11206660
  6.1 5.6 %copy-start.1 = (bf16[38,3,128,128]{3,2,1,0:T(8,128)(2,1)S(1)}, bf16[38,3,128,128]{3,2,1,0:T(8,128)(2,1)}, u32[]{:S(2)}) copy-start(bf16[38,3,128,128]{3,2,1,0:T(8,128)(2,1)} %refs_2_.5) | copy-start | bytes 11206660
  8.8 10.3 %collective-permute-start.3 = (bf16[192,512]{1,0:T(8,128)(2,1)S(1)}, bf16[192,512]{1,0:T(8,128)(2,1)S(1)}, u32[]{:S(2)}, u32[]{:S(2)}) collective-permute-start(bf16[192,512]{1,0:T(8,128)(2,1)S(1)} %get-tuple-element.41), channel_id=1, source_target_pairs={{0,4},{4,0},{8,12},{12,8},{16,20},{20,16},{24,28},{28,24},{1,5},{5... | collective-permute-start | bytes 589832 | tf_op jit(solution)/shard_map/ppermute | solution.py:222
  10.9 8.3 %collective-permute-start.4 = (bf16[192,512]{1,0:T(8,128)(2,1)S(1)}, bf16[192,512]{1,0:T(8,128)(2,1)S(1)}, u32[]{:S(2)}, u32[]{:S(2)}) collective-permute-start(bf16[192,512]{1,0:T(8,128)(2,1)S(1)} %get-tuple-element.40), channel_id=1, source_target_pairs={{4,8},{12,16},{20,24},{8,4},{16,12},{24,20},{5,9},{13,17},{21,25},... | collective-permute-start | bytes 589832 | tf_op jit(solution)/shard_map/ppermute | solution.py:226
  11.5 11.9 %collective-permute-start.11 = (bf16[64,1024]{1,0:T(8,128)(2,1)S(1)}, bf16[64,1024]{1,0:T(8,128)(2,1)S(1)}, u32[]{:S(2)}, u32[]{:S(2)}) collective-permute-start(bf16[64,1024]{1,0:T(8,128)(2,1)S(1)} %collective-permute-done.refs_6_), channel_id=1, source_target_pairs={{0,1},{1,0},{2,3},{3,2},{4,5},{5,4},{6,7},{7,6},{8,9},{9,8},{10,11... | collective-permute-start | bytes 393224 | tf_op jit(solution)/shard_map/ppermute | solution.py:219
  18.8 4.6 %collective-permute-start.12 = (bf16[64,3840]{1,0:T(8,128)(2,1)S(1)}, bf16[64,3840]{1,0:T(8,128)(2,1)S(1)}, u32[]{:S(2)}, u32[]{:S(2)}) collective-permute-start(bf16[64,3840]{1,0:T(8,128)(2,1)S(1)} %collective-permute-done.5.refs_8_), channel_id=1, source_target_pairs={{0,1},{1,0},{2,3},{3,2},{4,5},{5,4},{6,7},{7,6},{8,9},{9,8},{10,11... | collective-permute-start | bytes 1474568 | tf_op jit(solution)/shard_map/ppermute | solution.py:219
  19.2 4.2 %collective-permute-start.10 = (bf16[64,1024]{1,0:T(8,128)(2,1)S(1)}, bf16[64,1024]{1,0:T(8,128)(2,1)S(1)}, u32[]{:S(2)}, u32[]{:S(2)}) collective-permute-start(bf16[64,1024]{1,0:T(8,128)(2,1)S(1)} %slice.14), channel_id=1, source_target_pairs={{0,1},{1,0},{2,3},{3,2},{4,5},{5,4},{6,7},{7,6},{8,9},{9,8},{10,11... | collective-permute-start | bytes 393224 | tf_op jit(solution)/shard_map/ppermute | solution.py:219
  21.1 6.6 %collective-permute-start.6 = (bf16[4,64,256]{2,1,0:T(8,128)(2,1)S(1)}, bf16[4,64,256]{2,1,0:T(8,128)(2,1)S(1)}, u32[]{:S(2)}, u32[]{:S(2)}) collective-permute-start(bf16[4,64,256]{2,1,0:T(8,128)(2,1)S(1)} %get-tuple-element.28), channel_id=1, source_target_pairs={{0,4},{4,0},{8,12},{12,8},{16,20},{20,16},{24,28},{28,24},{1,5},{5... | collective-permute-start | bytes 393224 | tf_op jit(solution)/shard_map/ppermute | solution.py:222
  27.5 5.7 %collective-permute-start.13 = (bf16[4,64,256]{2,1,0:T(8,128)(2,1)S(1)}, bf16[4,64,256]{2,1,0:T(8,128)(2,1)S(1)}, u32[]{:S(2)}, u32[]{:S(2)}) collective-permute-start(bf16[4,64,256]{2,1,0:T(8,128)(2,1)S(1)} %get-tuple-element.35), channel_id=1, source_target_pairs={{0,4},{4,0},{8,12},{12,8},{16,20},{20,16},{24,28},{28,24},{1,5},{5... | collective-permute-start | bytes 393224 | tf_op jit(solution)/shard_map/ppermute | solution.py:222
  27.7 8.7 %collective-permute-start.7 = (bf16[64,256]{1,0:T(8,128)(2,1)S(1)}, bf16[64,256]{1,0:T(8,128)(2,1)S(1)}, u32[]{:S(2)}, u32[]{:S(2)}) collective-permute-start(bf16[64,256]{1,0:T(8,128)(2,1)S(1)} %get-tuple-element.30), channel_id=1, source_target_pairs={{0,24},{4,28},{8,16},{12,20},{16,8},{20,12},{24,0},{28,4},{1,25},{... | collective-permute-start | bytes 98312 | tf_op jit(solution)/shard_map/ppermute | solution.py:222
  31.8 5.9 %collective-permute-start.8 = (bf16[64,256]{1,0:T(8,128)(2,1)S(1)}, bf16[64,256]{1,0:T(8,128)(2,1)S(1)}, u32[]{:S(2)}, u32[]{:S(2)}) collective-permute-start(bf16[64,256]{1,0:T(8,128)(2,1)S(1)} %get-tuple-element.31), channel_id=1, source_target_pairs={{0,16},{4,20},{8,24},{12,28},{16,0},{20,4},{24,8},{28,12},{1,17},{... | collective-permute-start | bytes 98312 | tf_op jit(solution)/shard_map/ppermute | solution.py:222
  31.8 5.9 %collective-permute-start.9 = (bf16[64,256]{1,0:T(8,128)(2,1)S(1)}, bf16[64,256]{1,0:T(8,128)(2,1)S(1)}, u32[]{:S(2)}, u32[]{:S(2)}) collective-permute-start(bf16[64,256]{1,0:T(8,128)(2,1)S(1)} %get-tuple-element.32), channel_id=1, source_target_pairs={{0,8},{4,12},{8,0},{12,4},{16,24},{20,28},{24,16},{28,20},{1,9},{5... | collective-permute-start | bytes 98312 | tf_op jit(solution)/shard_map/ppermute | solution.py:222
  33.3 6.0 %collective-permute-start.14 = (bf16[64,256]{1,0:T(8,128)(2,1)S(1)}, bf16[64,256]{1,0:T(8,128)(2,1)S(1)}, u32[]{:S(2)}, u32[]{:S(2)}) collective-permute-start(bf16[64,256]{1,0:T(8,128)(2,1)S(1)} %get-tuple-element.37), channel_id=1, source_target_pairs={{0,24},{4,28},{8,16},{12,20},{16,8},{20,12},{24,0},{28,4},{1,25},{... | collective-permute-start | bytes 98312 | tf_op jit(solution)/shard_map/ppermute | solution.py:222
  36.3 4.8 %collective-permute-start.15 = (bf16[64,256]{1,0:T(8,128)(2,1)S(1)}, bf16[64,256]{1,0:T(8,128)(2,1)S(1)}, u32[]{:S(2)}, u32[]{:S(2)}) collective-permute-start(bf16[64,256]{1,0:T(8,128)(2,1)S(1)} %get-tuple-element.38), channel_id=1, source_target_pairs={{0,16},{4,20},{8,24},{12,28},{16,0},{20,4},{24,8},{28,12},{1,17},{... | collective-permute-start | bytes 98312 | tf_op jit(solution)/shard_map/ppermute | solution.py:222
  36.4 4.8 %collective-permute-start.16 = (bf16[64,256]{1,0:T(8,128)(2,1)S(1)}, bf16[64,256]{1,0:T(8,128)(2,1)S(1)}, u32[]{:S(2)}, u32[]{:S(2)}) collective-permute-start(bf16[64,256]{1,0:T(8,128)(2,1)S(1)} %get-tuple-element.39), channel_id=1, source_target_pairs={{0,8},{4,12},{8,0},{12,4},{16,24},{20,28},{24,16},{28,20},{1,9},{5... | collective-permute-start | bytes 98312 | tf_op jit(solution)/shard_map/ppermute | solution.py:222

commit v12 on v11

--- a/solution.py
+++ b/solution.py
@@ -62,8 +62,9 @@
     sources, targets, sems = refs[:count], refs[count:2 * count], refs[-1]
     copies = []
     for which, (source, target) in enumerate(zip(sources, targets)):
-        middle = source.shape[0] // 2
-        for part, span in enumerate((pl.ds(0, middle), pl.ds(middle, source.shape[0] - middle))):
+        size = source.shape[0] // 4
+        for part in range(4):
+            span = pl.ds(part * size, size if part < 3 else source.shape[0] - 3 * size)
             copies.append(pltpu.make_async_copy(source.at[span], target.at[span], sems.at[which, part]))
     for copy in copies:
         copy.start()
@@ -78,7 +79,7 @@
         out_shape=[shape(array.shape, array.dtype) for array in arrays],
         in_specs=[HBM] * len(arrays),
         out_specs=[VMEM] * len(arrays),
-        scratch_shapes=[pltpu.SemaphoreType.DMA((len(arrays), 2))],
+        scratch_shapes=[pltpu.SemaphoreType.DMA((len(arrays), 4))],
         compiler_params=params(45),
         cost_estimate=pl.CostEstimate(flops=0, bytes_accessed=size * 1, transcendentals=0),
     )(*arrays)

time: 42 us -> 42 us (level)
  no operation moved by 1% of the time
where the time goes in v12:
time: 42 us; the launch traced here: 41.8 us
  starting transfers between devices  18.3 us (44%)
  Pallas kernels  12.5 us (30%)
  waiting for transfers between devices  8.23 us (20%)
  local copies, waits for them, and re-layouts  1.18 us (3%)
  between operations  0.82 us (2%)
  other arithmetic  0.69 us (2%)
    ppermute x9, starting transfers between devices, swap(): return lax.ppermute(array, 'node', [(i, i ^ step) for i in range(nodes)])  13.7 us
    pallas_call x3, Pallas kernels, project(): pl.pallas_call(functools.partial(project_kernel, spans, places, groups, b...  9.11 us
    ppermute x9, waiting for transfers between devices, swap(): return lax.ppermute(array, 'node', [(i, i ^ step) for i in range(nodes)])  4.45 us
    ppermute x2, waiting for transfers between devices, across(): return lax.ppermute(array, 'col', [(i, i ^ 2) for i in range(cols)])  3.77 us
    ppermute x2, starting transfers between devices, across(): return lax.ppermute(array, 'col', [(i, i ^ 2) for i in range(cols)])  3.08 us
    pallas_call x1, Pallas kernels, load(): pl.pallas_call(load_kernel, out_shape=[shape(array.shape, array.dtype) fo...  2.6 us
    unnamed x9, local copies, waits for them, and re-layouts  1.11 us
    ppermute x5, starting transfers between devices, cores(): return lax.ppermute(array, 'col', [(i, i ^ 1) for i in range(cols)])  0.89 us
  transfers between devices with their start and end apart: 17, of which 5 were waited for; matrix products, arithmetic and copies ran while one was open for 2% of the time, Pallas kernels for 28%

profile of v12, /device:TPU:0, one launch (start us, length us, event | category | flops | bytes accessed | tf_op | source)
XLA Modules:
  0.0 41.8 jit_solution(5524846212202474334)
XLA Ops:
  0.6 1.1 %copy-done.2 = bf16[4864,64]{0,1:T(8,128)(2,1)S(1)} copy-done((bf16[4864,64]{0,1:T(8,128)(2,1)S(1)}, bf16[4864,64]{0,1:T(8,128)(2,1)}, u32[]{:S(2)}) %copy-start.2) | copy-done | bytes 622616
  1.7 0.1 shard_map.68
  1.8 3.0 %collective-permute-start = (bf16[64,1024]{1,0:T(8,128)(2,1)S(1)}, bf16[64,1024]{1,0:T(8,128)(2,1)S(1)}, u32[]{:S(2)}, u32[]{:S(2)}) collective-permute-start(bf16[64,1024]{1,0:T(8,128)(2,1)S(1)} %get-tuple-element.21.refs_4_), channel_id=1, source_target_pairs={{0,2},{1,3},{2,0},{3,1},{4,6},{5,7},{6,4},{7,5},{8,10},{9,11},{10,... | collective-permute-start | bytes 393224 | tf_op jit(solution)/shard_map/ppermute | solution.py:217
  4.8 0.5 %collective-permute-start.2 = (bf16[64,3840]{1,0:T(8,128)(2,1)S(1)}, bf16[64,3840]{1,0:T(8,128)(2,1)S(1)}, u32[]{:S(2)}, u32[]{:S(2)}) collective-permute-start(bf16[64,3840]{1,0:T(8,128)(2,1)S(1)} %get-tuple-element.24.refs_6_), channel_id=1, source_target_pairs={{0,1},{1,0},{2,3},{3,2},{4,5},{5,4},{6,7},{7,6},{8,9},{9,8},{10,11... | collective-permute-start | bytes 1474568 | tf_op jit(solution)/shard_map/ppermute | solution.py:220
  5.4 0.7 %clamp_bitcast_fusion.refs_0_ = s32[3,38]{1,0:T(4,128)S(1)} fusion(s32[38,3]{0,1:T(4,128)} %param.9, s32[]{:T(128)S(6)} %sub.10), kind=kLoop, calls=%fused_computation.5 | loop fusion | flops 228 | bytes 916 | tf_op jit(solution)/shard_map/jit(clip)/min | solution.py:237
  6.1 2.6 %shard_map.69.refs_3_ = bf16[4864,512]{1,0:T(8,128)(2,1)S(1)} custom-call(bf16[4864,512]{1,0:T(8,128)(2,1)} %refs_0_.1), custom_call_target="tpu_custom_call" | custom-call | bytes 4980736 | tf_op jit(solution)/shard_map/pallas_call | solution.py:77
  8.8 2.0 %collective-permute-start.3 = (bf16[192,512]{1,0:T(8,128)(2,1)S(1)}, bf16[192,512]{1,0:T(8,128)(2,1)S(1)}, u32[]{:S(2)}, u32[]{:S(2)}) collective-permute-start(bf16[192,512]{1,0:T(8,128)(2,1)S(1)} %get-tuple-element.41), channel_id=1, source_target_pairs={{0,4},{4,0},{8,12},{12,8},{16,20},{20,16},{24,28},{28,24},{1,5},{5... | collective-permute-start | bytes 589832 | tf_op jit(solution)/shard_map/ppermute | solution.py:223
  10.9 0.7 %collective-permute-start.4 = (bf16[192,512]{1,0:T(8,128)(2,1)S(1)}, bf16[192,512]{1,0:T(8,128)(2,1)S(1)}, u32[]{:S(2)}, u32[]{:S(2)}) collective-permute-start(bf16[192,512]{1,0:T(8,128)(2,1)S(1)} %get-tuple-element.40), channel_id=1, source_target_pairs={{4,8},{12,16},{20,24},{8,4},{16,12},{24,20},{5,9},{13,17},{21,25},... | collective-permute-start | bytes 589832 | tf_op jit(solution)/shard_map/ppermute | solution.py:227
  11.6 3.4 %shard_map.70.refs_10_ = f32[512,256]{1,0:T(8,128)S(1)} custom-call(s32[3,38]{1,0:T(4,128)S(1)} %clamp_bitcast_fusion.refs_0_, bf16[38,3,128,128]{3,2,1,0:T(8,128)(2,1)S(1)} %copy-done, bf16[38,3,128,128]{3,2,1,0:T(8,128)(2,1)S(1)} %copy-done.1, bf16[4864,512]{1,0:T(8,128)(2,1)S(1)} %shard_map.69.refs_3_, bf16[64,1024]{1,0:T(8,128)(2,1)S(1)} %get-tuple-element.21.refs_4_, ...), custom_call_target="tpu_custom_call" | custom-call | flops 1 | bytes 30 | tf_op jit(solution)/shard_map/pallas_call | solution.py:150
  15.1 3.8 %collective-permute-done.5.refs_8_ = bf16[64,3840]{1,0:T(8,128)(2,1)S(1)} collective-permute-done((bf16[64,3840]{1,0:T(8,128)(2,1)S(1)}, bf16[64,3840]{1,0:T(8,128)(2,1)S(1)}, u32[]{:S(2)}, u32[]{:S(2)}) %collective-permute-start.5) | collective-permute-done | bytes 491552 | tf_op jit(solution)/shard_map/ppermute | solution.py:217
  18.8 0.3 collective-permute-done.3
  19.2 0.3 collective-permute-start.10
  19.5 1.6 %shard_map.71 = (bf16[4,64,256]{2,1,0:T(8,128)(2,1)S(1)}, f32[4,64,256]{2,1,0:T(8,128)S(1)}) custom-call(s32[3,38]{1,0:T(4,128)S(1)} %clamp_bitcast_fusion.refs_0_, bf16[38,3,128,128]{3,2,1,0:T(8,128)(2,1)S(1)} %copy-done, bf16[38,3,128,128]{3,2,1,0:T(8,128)(2,1)S(1)} %copy-done.1, bf16[4864,512]{1,0:T(8,128)(2,1)S(1)} %shard_map.69.refs_3_, ...), custom_call_target="tpu_custom_call" | custom-call | flops 3449999872 | bytes 8 | tf_op jit(solution)/shard_map/pallas_call | solution.py:150
  21.1 2.3 %collective-permute-start.6 = (bf16[4,64,256]{2,1,0:T(8,128)(2,1)S(1)}, bf16[4,64,256]{2,1,0:T(8,128)(2,1)S(1)}, u32[]{:S(2)}, u32[]{:S(2)}) collective-permute-start(bf16[4,64,256]{2,1,0:T(8,128)(2,1)S(1)} %get-tuple-element.28), channel_id=1, source_target_pairs={{0,4},{4,0},{8,12},{12,8},{16,20},{20,16},{24,28},{28,24},{1,5},{5... | collective-permute-start | bytes 393224 | tf_op jit(solution)/shard_map/ppermute | solution.py:223
  23.4 4.1 %shard_map.73 = (bf16[4,64,256]{2,1,0:T(8,128)(2,1)S(1)}, f32[4,64,256]{2,1,0:T(8,128)S(1)}) custom-call(s32[3,38]{1,0:T(4,128)S(1)} %clamp_bitcast_fusion.refs_0_, bf16[38,3,128,128]{3,2,1,0:T(8,128)(2,1)S(1)} %copy-done, bf16[38,3,128,128]{3,2,1,0:T(8,128)(2,1)S(1)} %copy-done.1, bf16[4864,512]{1,0:T(8,128)(2,1)S(1)} %shard_map.69.refs_3_, ...), custom_call_target="tpu_custom_call" | custom-call | flops 38 | bytes 38 | tf_op jit(solution)/shard_map/pallas_call | solution.py:150
  27.5 0.1 collective-permute-start.13
  27.7 4.1 %collective-permute-start.7 = (bf16[64,256]{1,0:T(8,128)(2,1)S(1)}, bf16[64,256]{1,0:T(8,128)(2,1)S(1)}, u32[]{:S(2)}, u32[]{:S(2)}) collective-permute-start(bf16[64,256]{1,0:T(8,128)(2,1)S(1)} %get-tuple-element.30), channel_id=1, source_target_pairs={{0,24},{4,28},{8,16},{12,20},{16,8},{20,12},{24,0},{28,4},{1,25},{... | collective-permute-start | bytes 98312 | tf_op jit(solution)/shard_map/ppermute | solution.py:223
  31.8 0.6 %collective-permute-start.9 = (bf16[64,256]{1,0:T(8,128)(2,1)S(1)}, bf16[64,256]{1,0:T(8,128)(2,1)S(1)}, u32[]{:S(2)}, u32[]{:S(2)}) collective-permute-start(bf16[64,256]{1,0:T(8,128)(2,1)S(1)} %get-tuple-element.32), channel_id=1, source_target_pairs={{0,8},{4,12},{8,0},{12,4},{16,24},{20,28},{24,16},{28,20},{1,9},{5... | collective-permute-start | bytes 98312 | tf_op jit(solution)/shard_map/ppermute | solution.py:223
  32.5 0.8 %collective-permute-done.13.got = bf16[4,64,256]{2,1,0:T(8,128)(2,1)S(1)} collective-permute-done((bf16[4,64,256]{2,1,0:T(8,128)(2,1)S(1)}, bf16[4,64,256]{2,1,0:T(8,128)(2,1)S(1)}, u32[]{:S(2)}, u32[]{:S(2)}) %collective-permute-start.13) | collective-permute-done | bytes 131104 | tf_op jit(solution)/shard_map/ppermute | solution.py:223
  33.2 3.1 %collective-permute-start.14 = (bf16[64,256]{1,0:T(8,128)(2,1)S(1)}, bf16[64,256]{1,0:T(8,128)(2,1)S(1)}, u32[]{:S(2)}, u32[]{:S(2)}) collective-permute-start(bf16[64,256]{1,0:T(8,128)(2,1)S(1)} %get-tuple-element.37), channel_id=1, source_target_pairs={{0,24},{4,28},{8,16},{12,20},{16,8},{20,12},{24,0},{28,4},{1,25},{... | collective-permute-start | bytes 98312 | tf_op jit(solution)/shard_map/ppermute | solution.py:223
  36.4 1.3 %collective-permute-start.16 = (bf16[64,256]{1,0:T(8,128)(2,1)S(1)}, bf16[64,256]{1,0:T(8,128)(2,1)S(1)}, u32[]{:S(2)}, u32[]{:S(2)}) collective-permute-start(bf16[64,256]{1,0:T(8,128)(2,1)S(1)} %get-tuple-element.39), channel_id=1, source_target_pairs={{0,8},{4,12},{8,0},{12,4},{16,24},{20,28},{24,16},{28,20},{1,9},{5... | collective-permute-start | bytes 98312 | tf_op jit(solution)/shard_map/ppermute | solution.py:223
  37.7 1.5 %collective-permute-done.14.refs_5_ = bf16[64,256]{1,0:T(8,128)(2,1)S(1)} collective-permute-done((bf16[64,256]{1,0:T(8,128)(2,1)S(1)}, bf16[64,256]{1,0:T(8,128)(2,1)S(1)}, u32[]{:S(2)}, u32[]{:S(2)}) %collective-permute-start.14) | collective-permute-done | bytes 32800 | tf_op jit(solution)/shard_map/ppermute | solution.py:223
  39.2 1.9 %collective-permute-done.15.refs_6_ = bf16[64,256]{1,0:T(8,128)(2,1)S(1)} collective-permute-done((bf16[64,256]{1,0:T(8,128)(2,1)S(1)}, bf16[64,256]{1,0:T(8,128)(2,1)S(1)}, u32[]{:S(2)}, u32[]{:S(2)}) %collective-permute-start.15) | collective-permute-done | bytes 32800 | tf_op jit(solution)/shard_map/ppermute | solution.py:223
  41.1 0.7 %shard_map.75 = (f32[64,256]{1,0:T(8,128)}, f32[64,256]{1,0:T(8,128)}) custom-call(f32[64,256]{1,0:T(8,128)S(1)} %get-tuple-element.29.refs_0_, bf16[64,256]{1,0:T(8,128)(2,1)S(1)} %collective-permute-done.7.refs_1_, bf16[64,256]{1,0:T(8,128)(2,1)S(1)} %collective-permute-done.8.refs_2_, bf16[64,256]{1,0:T(8,128)(2,1)S(1)} %collective-permute-done.9.refs_3_, ...), custom_call_target="tpu_custom_call" | custom-call | tf_op jit(solution)/shard_map/pallas_call | solution.py:200
  (32 shorter events, 0.4 us)
Async XLA Ops:
  0.6 1.1 %copy-start.2 = (bf16[4864,64]{0,1:T(8,128)(2,1)S(1)}, bf16[4864,64]{0,1:T(8,128)(2,1)}, u32[]{:S(2)}) copy-start(bf16[4864,64]{0,1:T(8,128)(2,1)} %param.5) | copy-start | bytes 1867780
  1.8 6.9 %collective-permute-start = (bf16[64,1024]{1,0:T(8,128)(2,1)S(1)}, bf16[64,1024]{1,0:T(8,128)(2,1)S(1)}, u32[]{:S(2)}, u32[]{:S(2)}) collective-permute-start(bf16[64,1024]{1,0:T(8,128)(2,1)S(1)} %get-tuple-element.21.refs_4_), channel_id=1, source_target_pairs={{0,2},{1,3},{2,0},{3,1},{4,6},{5,7},{6,4},{7,5},{8,10},{9,11},{10,... | collective-permute-start | bytes 393224 | tf_op jit(solution)/shard_map/ppermute | solution.py:217
  4.8 3.9 %collective-permute-start.1 = (bf16[64,1024]{1,0:T(8,128)(2,1)S(1)}, bf16[64,1024]{1,0:T(8,128)(2,1)S(1)}, u32[]{:S(2)}, u32[]{:S(2)}) collective-permute-start(bf16[64,1024]{1,0:T(8,128)(2,1)S(1)} %get-tuple-element.21.refs_4_), channel_id=1, source_target_pairs={{0,1},{1,0},{2,3},{3,2},{4,5},{5,4},{6,7},{7,6},{8,9},{9,8},{10,11... | collective-permute-start | bytes 393224 | tf_op jit(solution)/shard_map/ppermute | solution.py:220
  4.8 6.8 %collective-permute-start.2 = (bf16[64,3840]{1,0:T(8,128)(2,1)S(1)}, bf16[64,3840]{1,0:T(8,128)(2,1)S(1)}, u32[]{:S(2)}, u32[]{:S(2)}) collective-permute-start(bf16[64,3840]{1,0:T(8,128)(2,1)S(1)} %get-tuple-element.24.refs_6_), channel_id=1, source_target_pairs={{0,1},{1,0},{2,3},{3,2},{4,5},{5,4},{6,7},{7,6},{8,9},{9,8},{10,11... | collective-permute-start | bytes 1474568 | tf_op jit(solution)/shard_map/ppermute | solution.py:220
  5.3 13.5 %collective-permute-start.5 = (bf16[64,3840]{1,0:T(8,128)(2,1)S(1)}, bf16[64,3840]{1,0:T(8,128)(2,1)S(1)}, u32[]{:S(2)}, u32[]{:S(2)}) collective-permute-start(bf16[64,3840]{1,0:T(8,128)(2,1)S(1)} %get-tuple-element.24.refs_6_), channel_id=1, source_target_pairs={{0,2},{1,3},{2,0},{3,1},{4,6},{5,7},{6,4},{7,5},{8,10},{9,11},{10,... | collective-permute-start | bytes 1474568 | tf_op jit(solution)/shard_map/ppermute | solution.py:217
  6.1 5.5 %copy-start = (bf16[38,3,128,128]{3,2,1,0:T(8,128)(2,1)S(1)}, bf16[38,3,128,128]{3,2,1,0:T(8,128)(2,1)}, u32[]{:S(2)}) copy-start(bf16[38,3,128,128]{3,2,1,0:T(8,128)(2,1)} %refs_1_.5) | copy-start | bytes 11206660
  6.1 5.5 %copy-start.1 = (bf16[38,3,128,128]{3,2,1,0:T(8,128)(2,1)S(1)}, bf16[38,3,128,128]{3,2,1,0:T(8,128)(2,1)}, u32[]{:S(2)}) copy-start(bf16[38,3,128,128]{3,2,1,0:T(8,128)(2,1)} %refs_2_.5) | copy-start | bytes 11206660
  8.8 10.3 %collective-permute-start.3 = (bf16[192,512]{1,0:T(8,128)(2,1)S(1)}, bf16[192,512]{1,0:T(8,128)(2,1)S(1)}, u32[]{:S(2)}, u32[]{:S(2)}) collective-permute-start(bf16[192,512]{1,0:T(8,128)(2,1)S(1)} %get-tuple-element.41), channel_id=1, source_target_pairs={{0,4},{4,0},{8,12},{12,8},{16,20},{20,16},{24,28},{28,24},{1,5},{5... | collective-permute-start | bytes 589832 | tf_op jit(solution)/shard_map/ppermute | solution.py:223
  10.9 8.3 %collective-permute-start.4 = (bf16[192,512]{1,0:T(8,128)(2,1)S(1)}, bf16[192,512]{1,0:T(8,128)(2,1)S(1)}, u32[]{:S(2)}, u32[]{:S(2)}) collective-permute-start(bf16[192,512]{1,0:T(8,128)(2,1)S(1)} %get-tuple-element.40), channel_id=1, source_target_pairs={{4,8},{12,16},{20,24},{8,4},{16,12},{24,20},{5,9},{13,17},{21,25},... | collective-permute-start | bytes 589832 | tf_op jit(solution)/shard_map/ppermute | solution.py:227
  11.5 11.9 %collective-permute-start.11 = (bf16[64,1024]{1,0:T(8,128)(2,1)S(1)}, bf16[64,1024]{1,0:T(8,128)(2,1)S(1)}, u32[]{:S(2)}, u32[]{:S(2)}) collective-permute-start(bf16[64,1024]{1,0:T(8,128)(2,1)S(1)} %collective-permute-done.refs_6_), channel_id=1, source_target_pairs={{0,1},{1,0},{2,3},{3,2},{4,5},{5,4},{6,7},{7,6},{8,9},{9,8},{10,11... | collective-permute-start | bytes 393224 | tf_op jit(solution)/shard_map/ppermute | solution.py:220
  18.8 4.6 %collective-permute-start.12 = (bf16[64,3840]{1,0:T(8,128)(2,1)S(1)}, bf16[64,3840]{1,0:T(8,128)(2,1)S(1)}, u32[]{:S(2)}, u32[]{:S(2)}) collective-permute-start(bf16[64,3840]{1,0:T(8,128)(2,1)S(1)} %collective-permute-done.5.refs_8_), channel_id=1, source_target_pairs={{0,1},{1,0},{2,3},{3,2},{4,5},{5,4},{6,7},{7,6},{8,9},{9,8},{10,11... | collective-permute-start | bytes 1474568 | tf_op jit(solution)/shard_map/ppermute | solution.py:220
  19.2 4.2 %collective-permute-start.10 = (bf16[64,1024]{1,0:T(8,128)(2,1)S(1)}, bf16[64,1024]{1,0:T(8,128)(2,1)S(1)}, u32[]{:S(2)}, u32[]{:S(2)}) collective-permute-start(bf16[64,1024]{1,0:T(8,128)(2,1)S(1)} %slice.14), channel_id=1, source_target_pairs={{0,1},{1,0},{2,3},{3,2},{4,5},{5,4},{6,7},{7,6},{8,9},{9,8},{10,11... | collective-permute-start | bytes 393224 | tf_op jit(solution)/shard_map/ppermute | solution.py:220
  21.1 6.6 %collective-permute-start.6 = (bf16[4,64,256]{2,1,0:T(8,128)(2,1)S(1)}, bf16[4,64,256]{2,1,0:T(8,128)(2,1)S(1)}, u32[]{:S(2)}, u32[]{:S(2)}) collective-permute-start(bf16[4,64,256]{2,1,0:T(8,128)(2,1)S(1)} %get-tuple-element.28), channel_id=1, source_target_pairs={{0,4},{4,0},{8,12},{12,8},{16,20},{20,16},{24,28},{28,24},{1,5},{5... | collective-permute-start | bytes 393224 | tf_op jit(solution)/shard_map/ppermute | solution.py:223
  27.5 5.7 %collective-permute-start.13 = (bf16[4,64,256]{2,1,0:T(8,128)(2,1)S(1)}, bf16[4,64,256]{2,1,0:T(8,128)(2,1)S(1)}, u32[]{:S(2)}, u32[]{:S(2)}) collective-permute-start(bf16[4,64,256]{2,1,0:T(8,128)(2,1)S(1)} %get-tuple-element.35), channel_id=1, source_target_pairs={{0,4},{4,0},{8,12},{12,8},{16,20},{20,16},{24,28},{28,24},{1,5},{5... | collective-permute-start | bytes 393224 | tf_op jit(solution)/shard_map/ppermute | solution.py:223
  27.7 8.7 %collective-permute-start.7 = (bf16[64,256]{1,0:T(8,128)(2,1)S(1)}, bf16[64,256]{1,0:T(8,128)(2,1)S(1)}, u32[]{:S(2)}, u32[]{:S(2)}) collective-permute-start(bf16[64,256]{1,0:T(8,128)(2,1)S(1)} %get-tuple-element.30), channel_id=1, source_target_pairs={{0,24},{4,28},{8,16},{12,20},{16,8},{20,12},{24,0},{28,4},{1,25},{... | collective-permute-start | bytes 98312 | tf_op jit(solution)/shard_map/ppermute | solution.py:223
  31.8 5.9 %collective-permute-start.8 = (bf16[64,256]{1,0:T(8,128)(2,1)S(1)}, bf16[64,256]{1,0:T(8,128)(2,1)S(1)}, u32[]{:S(2)}, u32[]{:S(2)}) collective-permute-start(bf16[64,256]{1,0:T(8,128)(2,1)S(1)} %get-tuple-element.31), channel_id=1, source_target_pairs={{0,16},{4,20},{8,24},{12,28},{16,0},{20,4},{24,8},{28,12},{1,17},{... | collective-permute-start | bytes 98312 | tf_op jit(solution)/shard_map/ppermute | solution.py:223
  31.8 5.9 %collective-permute-start.9 = (bf16[64,256]{1,0:T(8,128)(2,1)S(1)}, bf16[64,256]{1,0:T(8,128)(2,1)S(1)}, u32[]{:S(2)}, u32[]{:S(2)}) collective-permute-start(bf16[64,256]{1,0:T(8,128)(2,1)S(1)} %get-tuple-element.32), channel_id=1, source_target_pairs={{0,8},{4,12},{8,0},{12,4},{16,24},{20,28},{24,16},{28,20},{1,9},{5... | collective-permute-start | bytes 98312 | tf_op jit(solution)/shard_map/ppermute | solution.py:223
  33.2 6.0 %collective-permute-start.14 = (bf16[64,256]{1,0:T(8,128)(2,1)S(1)}, bf16[64,256]{1,0:T(8,128)(2,1)S(1)}, u32[]{:S(2)}, u32[]{:S(2)}) collective-permute-start(bf16[64,256]{1,0:T(8,128)(2,1)S(1)} %get-tuple-element.37), channel_id=1, source_target_pairs={{0,24},{4,28},{8,16},{12,20},{16,8},{20,12},{24,0},{28,4},{1,25},{... | collective-permute-start | bytes 98312 | tf_op jit(solution)/shard_map/ppermute | solution.py:223
  36.3 4.8 %collective-permute-start.15 = (bf16[64,256]{1,0:T(8,128)(2,1)S(1)}, bf16[64,256]{1,0:T(8,128)(2,1)S(1)}, u32[]{:S(2)}, u32[]{:S(2)}) collective-permute-start(bf16[64,256]{1,0:T(8,128)(2,1)S(1)} %get-tuple-element.38), channel_id=1, source_target_pairs={{0,16},{4,20},{8,24},{12,28},{16,0},{20,4},{24,8},{28,12},{1,17},{... | collective-permute-start | bytes 98312 | tf_op jit(solution)/shard_map/ppermute | solution.py:223
  36.4 4.8 %collective-permute-start.16 = (bf16[64,256]{1,0:T(8,128)(2,1)S(1)}, bf16[64,256]{1,0:T(8,128)(2,1)S(1)}, u32[]{:S(2)}, u32[]{:S(2)}) collective-permute-start(bf16[64,256]{1,0:T(8,128)(2,1)S(1)} %get-tuple-element.39), channel_id=1, source_target_pairs={{0,8},{4,12},{8,0},{12,4},{16,24},{20,28},{24,16},{28,20},{1,9},{5... | collective-permute-start | bytes 98312 | tf_op jit(solution)/shard_map/ppermute | solution.py:223
